TPU v7x, 32 devices: a whole 2x2x4 slice. The times are simulated.
32 devices in a mesh: hrow: 4 (over z), hcol: 8 (over y, x, core).
Axes of the slice: x: 2, y: 2, z: 4, core: 2. Of those that a mesh axis runs over, the one named last changes fastest.
Arguments:
- expect: bfloat16 [2, 256, 25600], P(None, 'hrow', 'hcol'), may hold values from -6 to 6
- distrib: bfloat16 [2, 256, 25600], P(None, 'hrow', 'hcol'), may hold values from -0.0048828125 to 0.0048828125
- direct: float32 [2, 2, 256], P(None, None, 'hcol'), may hold values from -4 to 4
- pair_index: int32 [4, 2], replicated, may hold values from 0 to 1
Outputs:
- jacobian: float32 [4, 256, 256], P(None, 'hrow', 'hcol')
Inputs may be any that keep to these rules, and one draw needn't show every extreme that they name: `pair_index`: column 0 of each row names a shock and column 1 an output; pairs may repeat.
All inputs are finite; a program needn't handle non-finite values.
Results may differ from a plain program's by a relative error of at most 0.0003.
Values may be sent and summed in bfloat16 or wider, within the bound.
No kernel may reach another device: no remote copies, remote signals or barrier semaphores. Data moves between devices by JAX's collectives and lax.ppermute only.
A program may use at most 64 MiB of HBM per device.

v0:
```python
import jax
import jax.numpy as jnp
from jax import lax
from jax.sharding import PartitionSpec as P


def from_behind(block, axis, distance):
    devices = range(lax.axis_size(axis))
    route = [(i - distance, i) for i in devices if i - distance in devices]
    return lax.ppermute(block, axis, route)


def diagonal_sums(values):
    row_count = values.shape[1]
    col_count = values.shape[2]
    offset = 1
    while offset < min(row_count, col_count):
        padded = jnp.pad(values, ((0, 0), (offset, 0), (offset, 0)))
        values = values + padded[:, :row_count, :col_count]
        offset = offset * 2
    return values


def shift_down(values, amount):
    if amount == 0:
        return values
    width_rows = values.shape[1]
    filler = jnp.zeros((values.shape[0], amount), values.dtype)
    return jnp.concatenate([filler, values[:, : width_rows - amount]], axis=1)


def shards(expect, distrib, direct, pair_index):
    row_devices = lax.axis_size("hrow")
    col_devices = lax.axis_size("hcol")
    stride = col_devices // row_devices
    output_count, row_count, _ = expect.shape
    shock_count = distrib.shape[0]
    horizon_all = distrib.shape[1] * row_devices
    col_count = horizon_all // col_devices
    pair_count = pair_index.shape[0]
    partial_tiles = jnp.einsum(
        "orn,scn->osrc",
        expect,
        lax.all_gather(distrib, "hrow", axis=1, tiled=True),
        preferred_element_type=jnp.float32,
    )
    products = lax.psum_scatter(partial_tiles, "hcol", scatter_dimension=3, tiled=True)
    shock_pick = (pair_index[:, 0][:, None] == jnp.arange(shock_count)[None, :]).astype(jnp.float32)
    output_pick = (pair_index[:, 1][:, None] == jnp.arange(output_count)[None, :]).astype(
        jnp.float32
    )
    weights = output_pick[:, :, None] * shock_pick[:, None, :]
    fake_news = jnp.sum(weights[:, :, :, None, None] * products[None], axis=(1, 2))
    direct_pick = jnp.sum(
        shock_pick[:, :, None, None] * output_pick[:, None, :, None] * direct[None], axis=(1, 2)
    )
    top_first = jnp.where(lax.axis_index("hrow") == 0, direct_pick, jnp.zeros_like(direct_pick))
    fake_news = fake_news.at[:, 0, :].add(top_first)
    within = diagonal_sums(fake_news)
    last_col = within[:, :, col_count - 1]
    incoming = jnp.zeros((pair_count, row_count), jnp.float32)
    for offset in range(1, stride + 1):
        shifted = from_behind(last_col, "hcol", offset)
        incoming = incoming + shift_down(shifted, (offset - 1) * col_count)
    padded_in = jnp.concatenate([jnp.zeros((pair_count, 1), jnp.float32), incoming], axis=1)
    band_last = within[:, row_count - 1, :] + jnp.flip(
        padded_in[:, row_count - col_count : row_count], axis=1
    )

    def advance(counter, received):
        moved = from_behind(received, "hcol", stride)
        return from_behind(band_last + moved, "hrow", 1)

    prev_band = lax.fori_loop(0, row_devices - 1, advance, jnp.zeros_like(band_last))
    blocks = [prev_band]
    for offset in range(1, stride + 1):
        blocks.insert(0, from_behind(prev_band, "hcol", offset))
    window = jnp.concatenate(blocks, axis=1)
    top_rim = window[:, row_count - 1 : row_count + col_count - 1]
    left_rim = incoming[:, : row_count - 1] + jnp.flip(window[:, : row_count - 1], axis=1)
    injected = jnp.zeros((pair_count, row_count, col_count), jnp.float32)
    injected = injected.at[:, 0, :].set(top_rim)
    injected = injected.at[:, 1:, 0].set(left_rim)
    return within + diagonal_sums(injected)


def solution(mesh):
    placed = (P(None, "hrow", "hcol"), P(None, "hrow", "hcol"), P(None, None, "hcol"), P())
    return jax.shard_map(
        shards, mesh=mesh, in_specs=placed, out_specs=P(None, "hrow", "hcol"), check_vma=False
    )
```

profile of v0, /device:TPU:0, one launch (start us, length us, event | category | flops | bytes accessed | tf_op | source)
XLA Modules:
  0.0 192.8 jit_solution(18018738455701783061)
XLA Ops:
  6.5 0.7 all-gather.2.cloned.1.call-update
  7.3 1.3 dynamic-slice.24
  9.2 0.8 slice_bitcast_fusion.2
  10.2 0.8 multiply_reduce_fusion.1
  11.0 66.3 %all-gather.2.cloned.1.call-done = bf16[2,256,3200]{2,1,0:T(8,128)(2,1)} async-done(((bf16[2,64,3200]{2,1,0:T(8,128)(2,1)}), bf16[2,256,3200]{2,1,0:T(8,128)(2,1)}) %all-gather.2.cloned.1.call-update) | async-done | bytes 3276816 | tf_op jit(solution)/shard_map/all_gather | solution.py:44
  77.3 3.1 %fusion.2 = f32[2,2,64,256]{3,2,0,1:T(8,128)S(1)} fusion(bf16[2,256,3200]{2,1,0:T(8,128)(2,1)} %all-gather.2.cloned.1.call-done, bf16[2,64,3200]{2,1,0:T(8,128)(2,1)S(1)} %copy-done), kind=kOutput, calls=%fused_computation.2 | convolution fusion | flops 419430400 | bytes 4358144 | tf_op jit(solution)/shard_map/orn,scn->osrc/dot_general | solution.py:41
  80.4 1.0 copy.42
  81.5 53.3 %all-reduce.15.cloned.1.call-done = f32[2,2,64,256]{2,1,0,3:T(2,128)} async-done(((f32[2,2,64,256]{2,1,0,3:T(2,128)}), f32[2,2,64,256]{2,1,0,3:T(2,128)}) %all-reduce.15.cloned.1.call-update) | async-done | bytes 262160
  134.8 0.8 constant_dynamic-slice_fusion
  135.8 0.1 scatter-add.4
  136.3 2.7 %collective-permute-start.3 = (f32[4,64]{1,0:T(4,128)S(1)}, f32[4,64]{1,0:T(4,128)S(1)}, u32[]{:S(2)}, u32[]{:S(2)}) collective-permute-start(f32[4,64]{1,0:T(4,128)S(1)} %bitcast.30), channel_id=1, source_target_pairs={{0,2},{1,3},{2,4},{3,5},{4,6},{5,7},{8,10},{9,11},{10,12},{11,13},... | collective-permute-start | bytes 3080 | tf_op jit(solution)/shard_map/ppermute | solution.py:10
  139.0 1.3 collective-permute-start.2
  140.3 0.2 slice_reduce_fusion
  140.5 0.6 collective-permute-done.2
  141.4 34.1 %while.13 = (s32[]{:T(128)}, f32[4,32]{1,0:T(4,128)S(1)}, f32[4,32]{1,0:T(4,128)S(1)}, s32[]{:T(128)}) while((s32[]{:T(128)}, f32[4,32]{1,0:T(4,128)S(1)}, f32[4,32]{1,0:T(4,128)S(1)}, s32[]{:T(128)}) %tuple.35), condition=%wide.region_4.5_spmd, body=%wide.region_3.4_spmd.sunk | while | flops 130 | bytes 5765 | solution.py:74
  141.4 6.1 %collective-permute-start = (f32[4,32]{1,0:T(4,128)S(1)}, f32[4,32]{1,0:T(4,128)S(1)}, u32[]{:S(2)}, u32[]{:S(2)}) collective-permute-start(f32[4,32]{1,0:T(4,128)S(1)} %get-tuple-element.101), channel_id=1, source_target_pairs={{0,2},{1,3},{2,4},{3,5},{4,6},{5,7},{8,10},{9,11},{10,12},{11,13},... | collective-permute-start | bytes 1544 | tf_op jit(solution)/shard_map/while/body/eval_jaxpr/ppermute | solution.py:10
  147.5 1.3 collective-permute-done
  148.8 3.4 %collective-permute-start.1 = (f32[4,32]{1,0:T(4,128)S(1)}, f32[4,32]{1,0:T(4,128)S(1)}, u32[]{:S(2)}, u32[]{:S(2)}) collective-permute-start(f32[4,32]{1,0:T(4,128)S(1)} %add.124), channel_id=1, source_target_pairs={{0,8},{8,16},{16,24},{1,9},{9,17},{17,25},{2,10},{10,18},{18,26},{... | collective-permute-start | bytes 1544 | tf_op jit(solution)/shard_map/while/body/eval_jaxpr/ppermute | solution.py:10
  152.2 1.3 collective-permute-done.1
  153.5 4.2 %collective-permute-start = (f32[4,32]{1,0:T(4,128)S(1)}, f32[4,32]{1,0:T(4,128)S(1)}, u32[]{:S(2)}, u32[]{:S(2)}) collective-permute-start(f32[4,32]{1,0:T(4,128)S(1)} %get-tuple-element.101), channel_id=1, source_target_pairs={{0,2},{1,3},{2,4},{3,5},{4,6},{5,7},{8,10},{9,11},{10,12},{11,13},... | collective-permute-start | bytes 1544 | tf_op jit(solution)/shard_map/while/body/eval_jaxpr/ppermute | solution.py:10
  157.7 1.3 collective-permute-done
  159.0 4.2 %collective-permute-start.1 = (f32[4,32]{1,0:T(4,128)S(1)}, f32[4,32]{1,0:T(4,128)S(1)}, u32[]{:S(2)}, u32[]{:S(2)}) collective-permute-start(f32[4,32]{1,0:T(4,128)S(1)} %add.124), channel_id=1, source_target_pairs={{0,8},{8,16},{16,24},{1,9},{9,17},{17,25},{2,10},{10,18},{18,26},{... | collective-permute-start | bytes 1544 | tf_op jit(solution)/shard_map/while/body/eval_jaxpr/ppermute | solution.py:10
  163.1 1.3 collective-permute-done.1
  164.4 4.3 %collective-permute-start = (f32[4,32]{1,0:T(4,128)S(1)}, f32[4,32]{1,0:T(4,128)S(1)}, u32[]{:S(2)}, u32[]{:S(2)}) collective-permute-start(f32[4,32]{1,0:T(4,128)S(1)} %get-tuple-element.101), channel_id=1, source_target_pairs={{0,2},{1,3},{2,4},{3,5},{4,6},{5,7},{8,10},{9,11},{10,12},{11,13},... | collective-permute-start | bytes 1544 | tf_op jit(solution)/shard_map/while/body/eval_jaxpr/ppermute | solution.py:10
  168.7 1.3 collective-permute-done
  170.0 4.2 %collective-permute-start.1 = (f32[4,32]{1,0:T(4,128)S(1)}, f32[4,32]{1,0:T(4,128)S(1)}, u32[]{:S(2)}, u32[]{:S(2)}) collective-permute-start(f32[4,32]{1,0:T(4,128)S(1)} %add.124), channel_id=1, source_target_pairs={{0,8},{8,16},{16,24},{1,9},{9,17},{17,25},{2,10},{10,18},{18,26},{... | collective-permute-start | bytes 1544 | tf_op jit(solution)/shard_map/while/body/eval_jaxpr/ppermute | solution.py:10
  174.2 1.3 collective-permute-done.1
  175.5 1.3 collective-permute-start.4
  176.7 5.7 %collective-permute-start.5 = (f32[4,32]{1,0:T(4,128)S(1)}, f32[4,32]{1,0:T(4,128)S(1)}, u32[]{:S(2)}, u32[]{:S(2)}) collective-permute-start(f32[4,32]{1,0:T(4,128)S(1)} %get-tuple-element.58), channel_id=1, source_target_pairs={{0,2},{1,3},{2,4},{3,5},{4,6},{5,7},{8,10},{9,11},{10,12},{11,13},... | collective-permute-start | bytes 1544 | tf_op jit(solution)/shard_map/ppermute | solution.py:10
  182.5 1.3 collective-permute-done.5
  184.1 0.8 scatter.9
  185.2 0.7 fusion.16
  (41 shorter events, 1.9 us)
Async XLA Ops:
  6.5 70.8 %copy-start = (bf16[2,64,3200]{2,1,0:T(8,128)(2,1)S(1)}, bf16[2,64,3200]{2,1,0:T(8,128)(2,1)}, u32[]{:S(2)}) copy-start(bf16[2,64,3200]{2,1,0:T(8,128)(2,1)} %param.12) | copy-start | bytes 2457604
  6.5 70.8 %all-gather.2.cloned.1.call-start = ((), (), s32[]{:S(2)}) async-start(), calls=%async_computation | async-start | bytes 4096000 | tf_op jit(solution)/shard_map/all_gather | solution.py:44
  7.3 127.5 %all-reduce.15.cloned.1.call-start = ((), (), s32[]{:S(2)}) async-start(), calls=%async_computation.1 | async-start | bytes 1048576
  136.3 4.2 %collective-permute-start.3 = (f32[4,64]{1,0:T(4,128)S(1)}, f32[4,64]{1,0:T(4,128)S(1)}, u32[]{:S(2)}, u32[]{:S(2)}) collective-permute-start(f32[4,64]{1,0:T(4,128)S(1)} %bitcast.30), channel_id=1, source_target_pairs={{0,2},{1,3},{2,4},{3,5},{4,6},{5,7},{8,10},{9,11},{10,12},{11,13},... | collective-permute-start | bytes 3080 | tf_op jit(solution)/shard_map/ppermute | solution.py:10
  139.0 2.1 %collective-permute-start.2 = (f32[4,64]{1,0:T(4,128)S(1)}, f32[4,64]{1,0:T(4,128)S(1)}, u32[]{:S(2)}, u32[]{:S(2)}) collective-permute-start(f32[4,64]{1,0:T(4,128)S(1)} %bitcast.31), channel_id=1, source_target_pairs={{0,1},{1,2},{2,3},{3,4},{4,5},{5,6},{6,7},{8,9},{9,10},{10,11},{11... | collective-permute-start | bytes 3080 | tf_op jit(solution)/shard_map/ppermute | solution.py:10
  141.4 7.4 %collective-permute-start = (f32[4,32]{1,0:T(4,128)S(1)}, f32[4,32]{1,0:T(4,128)S(1)}, u32[]{:S(2)}, u32[]{:S(2)}) collective-permute-start(f32[4,32]{1,0:T(4,128)S(1)} %get-tuple-element.101), channel_id=1, source_target_pairs={{0,2},{1,3},{2,4},{3,5},{4,6},{5,7},{8,10},{9,11},{10,12},{11,13},... | collective-permute-start | bytes 1544 | tf_op jit(solution)/shard_map/while/body/eval_jaxpr/ppermute | solution.py:10
  148.8 4.7 %collective-permute-start.1 = (f32[4,32]{1,0:T(4,128)S(1)}, f32[4,32]{1,0:T(4,128)S(1)}, u32[]{:S(2)}, u32[]{:S(2)}) collective-permute-start(f32[4,32]{1,0:T(4,128)S(1)} %add.124), channel_id=1, source_target_pairs={{0,8},{8,16},{16,24},{1,9},{9,17},{17,25},{2,10},{10,18},{18,26},{... | collective-permute-start | bytes 1544 | tf_op jit(solution)/shard_map/while/body/eval_jaxpr/ppermute | solution.py:10
  153.5 5.5 %collective-permute-start = (f32[4,32]{1,0:T(4,128)S(1)}, f32[4,32]{1,0:T(4,128)S(1)}, u32[]{:S(2)}, u32[]{:S(2)}) collective-permute-start(f32[4,32]{1,0:T(4,128)S(1)} %get-tuple-element.101), channel_id=1, source_target_pairs={{0,2},{1,3},{2,4},{3,5},{4,6},{5,7},{8,10},{9,11},{10,12},{11,13},... | collective-permute-start | bytes 1544 | tf_op jit(solution)/shard_map/while/body/eval_jaxpr/ppermute | solution.py:10
  159.0 5.5 %collective-permute-start.1 = (f32[4,32]{1,0:T(4,128)S(1)}, f32[4,32]{1,0:T(4,128)S(1)}, u32[]{:S(2)}, u32[]{:S(2)}) collective-permute-start(f32[4,32]{1,0:T(4,128)S(1)} %add.124), channel_id=1, source_target_pairs={{0,8},{8,16},{16,24},{1,9},{9,17},{17,25},{2,10},{10,18},{18,26},{... | collective-permute-start | bytes 1544 | tf_op jit(solution)/shard_map/while/body/eval_jaxpr/ppermute | solution.py:10
  164.4 5.6 %collective-permute-start = (f32[4,32]{1,0:T(4,128)S(1)}, f32[4,32]{1,0:T(4,128)S(1)}, u32[]{:S(2)}, u32[]{:S(2)}) collective-permute-start(f32[4,32]{1,0:T(4,128)S(1)} %get-tuple-element.101), channel_id=1, source_target_pairs={{0,2},{1,3},{2,4},{3,5},{4,6},{5,7},{8,10},{9,11},{10,12},{11,13},... | collective-permute-start | bytes 1544 | tf_op jit(solution)/shard_map/while/body/eval_jaxpr/ppermute | solution.py:10
  170.0 5.5 %collective-permute-start.1 = (f32[4,32]{1,0:T(4,128)S(1)}, f32[4,32]{1,0:T(4,128)S(1)}, u32[]{:S(2)}, u32[]{:S(2)}) collective-permute-start(f32[4,32]{1,0:T(4,128)S(1)} %add.124), channel_id=1, source_target_pairs={{0,8},{8,16},{16,24},{1,9},{9,17},{17,25},{2,10},{10,18},{18,26},{... | collective-permute-start | bytes 1544 | tf_op jit(solution)/shard_map/while/body/eval_jaxpr/ppermute | solution.py:10
  175.5 7.0 %collective-permute-start.4 = (f32[4,32]{1,0:T(4,128)S(1)}, f32[4,32]{1,0:T(4,128)S(1)}, u32[]{:S(2)}, u32[]{:S(2)}) collective-permute-start(f32[4,32]{1,0:T(4,128)S(1)} %get-tuple-element.58), channel_id=1, source_target_pairs={{0,1},{1,2},{2,3},{3,4},{4,5},{5,6},{6,7},{8,9},{9,10},{10,11},{11... | collective-permute-start | bytes 1544 | tf_op jit(solution)/shard_map/ppermute | solution.py:10
  176.7 7.0 %collective-permute-start.5 = (f32[4,32]{1,0:T(4,128)S(1)}, f32[4,32]{1,0:T(4,128)S(1)}, u32[]{:S(2)}, u32[]{:S(2)}) collective-permute-start(f32[4,32]{1,0:T(4,128)S(1)} %get-tuple-element.58), channel_id=1, source_target_pairs={{0,2},{1,3},{2,4},{3,5},{4,6},{5,7},{8,10},{9,11},{10,12},{11,13},... | collective-permute-start | bytes 1544 | tf_op jit(solution)/shard_map/ppermute | solution.py:10
Sparse Core Ops, SparseCore 0:
  8.9 68.3 all-gather.1
  81.6 53.1 all-reduce.14
where the time goes:
time: 196 us; the launch traced here: 193 us
  waiting for transfers between devices  130 us (66%)
  starting transfers between devices  37.3 us (19%)
  between operations  14.2 us (7%)
  local copies, waits for them, and re-layouts  5.68 us (3%)
  matrix products  3.11 us (2%)
  other arithmetic  2.6 us (1%)
    all_gather x1, waiting for transfers between devices, shards(): lax.all_gather(distrib, 'hrow', axis=1, tiled=True)  66.3 us
    unnamed x3, waiting for transfers between devices  54 us
    ppermute x10, starting transfers between devices, from_behind(): return lax.ppermute(block, axis, route)  37.2 us
    ppermute x10, waiting for transfers between devices, from_behind(): return lax.ppermute(block, axis, route)  9.65 us
  transfers between devices with their start and end apart: 12, of which 10 were waited for; matrix products, arithmetic and copies ran while one was open for 2% of the time, Pallas kernels for 0%

commit v1 on v0

v1 whole, which is shorter than its diff:
```python
import functools

import jax
import jax.numpy as jnp
from jax import lax
from jax.experimental import pallas as pl
from jax.experimental.pallas import tpu as pltpu
from jax.sharding import PartitionSpec as P

LANES = 128
VMEM_BYTES = 56 * 1024 * 1024


def swap(block, axis, mask):
    return lax.ppermute(block, axis, [(i, i ^ mask) for i in range(lax.axis_size(axis))])


def gather_rows_kernel(width, spot_ref, own_ref, *refs):
    *received, out_ref = refs
    rows = own_ref.shape[1]
    z = spot_ref[0]
    out_ref[:, :, width:] = jnp.zeros(out_ref.shape[:2] + (out_ref.shape[2] - width,), out_ref.dtype)
    out_ref[:, pl.ds(pl.multiple_of(z * rows, rows), rows), :] = own_ref[...]
    for mask, ref in enumerate(received, 1):
        out_ref[:, pl.ds(pl.multiple_of((z ^ mask) * rows, rows), rows), :width] = ref[...]


def partial_kernel(shock, spot_ref, expect_ref, direct_ref, *refs):
    *pieces, keep_ref, give_ref, responses, products = refs
    rows = pieces[0].shape[0]
    half = rows // 2
    horizon = products.shape[0]
    z = spot_ref[0]
    core = spot_ref[1]
    for mask, ref in enumerate(pieces):
        responses[pl.ds(pl.multiple_of((z ^ mask) * rows, rows), rows), :] = ref[...]
    step = 256
    row_id = lax.broadcasted_iota(jnp.int32, (rows, horizon), 0)
    date_id = lax.broadcasted_iota(jnp.int32, (rows, horizon), 1)
    for output in range(expect_ref.shape[0]):
        for start in range(0, horizon, step):
            products[start : start + step, :] = lax.dot_general(
                responses[start : start + step, :],
                expect_ref[output],
                (((1,), (1,)), ((), ())),
                preferred_element_type=jnp.float32,
            )

        def one_block(index, carry):
            block = products[pl.ds(pl.multiple_of(index * rows, rows), rows), :]
            added = direct_ref[shock, output, pl.ds(pl.multiple_of(index * rows, rows), rows), :]
            block = block + jnp.where(date_id == 0, added, 0.0)
            offset = 1
            while offset < rows:
                moved = pltpu.roll(pltpu.roll(block, offset, 1), offset, 0)
                inside = (row_id >= offset) & (date_id >= offset)
                block = block + jnp.where(inside, moved, 0.0)
                offset = offset * 2
            spread = jnp.broadcast_to(carry, (rows, horizon))
            moved = pltpu.roll(spread, 1, 1, stride=1, stride_axis=0)
            block = block + jnp.where(date_id > row_id, moved, 0.0)
            low = block[:half]
            high = block[half:]
            keep_ref[index, output] = jnp.where(core == 0, low, high)
            give_ref[index, output] = jnp.where(core == 0, high, low)
            return block[rows - 1 :]

        lax.fori_loop(0, horizon // rows, one_block, jnp.zeros((1, horizon), jnp.float32))


def pack_kernel(spot_ref, *refs):
    planes = (len(refs) - 1) // 2
    parts = refs[: len(refs) - 1 - planes]
    outs = refs[len(parts) : -1]
    cut = refs[-1]
    z = spot_ref[0]
    total = parts[0][...]
    for ref in parts[1:]:
        total = total + ref[...]
    width = total.shape[2] // len(outs)
    for plane in range(len(outs)):
        piece = total[:, :, plane * width : (plane + 1) * width]
        cut[plane] = jnp.concatenate([piece[o] for o in range(piece.shape[0])], axis=1)
    for mask, ref in enumerate(outs):
        ref[...] = cut[z ^ mask]


def finish_kernel(planes, pair_ref, *refs):
    *parts, out_ref, picked = refs
    rows = out_ref.shape[1]
    for shock in range(len(parts) // planes):
        total = parts[shock * planes][...]
        for ref in parts[shock * planes + 1 : (shock + 1) * planes]:
            total = total + ref[...]
        turned = total.T
        for output in range(turned.shape[0] // rows):
            picked[shock, output] = turned[output * rows : (output + 1) * rows]
    for pair in range(out_ref.shape[0]):
        out_ref[pair] = picked[pair_ref[pair, 0], pair_ref[pair, 1]]


def call(kernel, name, out_shape, scalars, arrays, scratch=()):
    specs = [pl.BlockSpec(memory_space=pltpu.SMEM)]
    specs += [pl.BlockSpec(memory_space=pltpu.VMEM)] * len(arrays)
    return pl.pallas_call(
        kernel,
        name=name,
        out_shape=out_shape,
        in_specs=specs,
        out_specs=jax.tree.map(lambda _: pl.BlockSpec(memory_space=pltpu.VMEM), out_shape),
        scratch_shapes=list(scratch),
        compiler_params=pltpu.CompilerParams(vmem_limit_bytes=VMEM_BYTES),
    )(scalars, *arrays)


def shards(expect, distrib, direct, pair_index):
    planes = lax.axis_size("hrow")
    col_devices = lax.axis_size("hcol")
    chips = col_devices // 2
    outputs, rows, grid = expect.shape
    shocks = distrib.shape[0]
    horizon = rows * planes
    cols = horizon // col_devices
    pairs = pair_index.shape[0]
    z = lax.axis_index("hrow")
    c = lax.axis_index("hcol")
    chip = c // 2
    spot = jnp.stack([z, c % 2]).astype(jnp.int32)

    width = grid // LANES // planes * LANES
    rest = grid - width * planes

    def cut(values, plane):
        return lax.dynamic_slice_in_dim(values, plane * width, width, axis=-1)

    def with_rest(values, plane):
        return jnp.concatenate([cut(values, plane), values[..., grid - rest :]], axis=-1)

    masks = range(1, planes)
    expect_in = [swap(cut(expect, z ^ m), "hrow", m) for m in masks]
    expect_all = call(
        functools.partial(gather_rows_kernel, width),
        "gather_rows",
        jax.ShapeDtypeStruct((outputs, horizon, width + rest), expect.dtype),
        spot,
        [with_rest(expect, z)] + expect_in,
    )

    top = jnp.where(z == 0, direct, jnp.zeros_like(direct))
    top = lax.dynamic_update_slice_in_dim(
        jnp.zeros((shocks, outputs, horizon), jnp.float32), top, c * cols, axis=2
    )[..., None]

    done = []
    for shock in range(shocks):
        own = with_rest(distrib[shock], z)
        received = [swap(with_rest(distrib[shock], z ^ m), "hrow", m) for m in masks]
        part = jax.ShapeDtypeStruct((chips, outputs, cols, horizon), jnp.float32)
        keep, give = call(
            functools.partial(partial_kernel, shock),
            f"partial_{shock}",
            (part, part),
            spot,
            [expect_all, top, own] + received,
            [
                pltpu.VMEM((horizon, width + rest), distrib.dtype),
                pltpu.VMEM((horizon, horizon), jnp.float32),
            ],
        )
        chip_sums = keep + swap(give, "hcol", 1)

        def of_chip(index):
            return lax.dynamic_index_in_dim(chip_sums, index, 0, False)

        parts = [of_chip(chip)] + [swap(of_chip(chip ^ m), "hcol", 2 * m) for m in range(1, chips)]
        packed = jax.ShapeDtypeStruct((cols, outputs * rows), jnp.float32)
        pieces = call(
            pack_kernel,
            f"pack_{shock}",
            (packed,) * planes,
            spot,
            parts,
            [pltpu.VMEM((planes, cols, outputs * rows), jnp.float32)],
        )
        done += [pieces[0]] + [swap(pieces[m], "hrow", m) for m in masks]

    return call(
        functools.partial(finish_kernel, planes),
        "finish",
        jax.ShapeDtypeStruct((pairs, rows, cols), jnp.float32),
        pair_index,
        done,
        [pltpu.VMEM((shocks, outputs, rows, cols), jnp.float32)],
    )


def solution(mesh):
    placed = (P(None, "hrow", "hcol"), P(None, "hrow", "hcol"), P(None, None, "hcol"), P())
    return jax.shard_map(
        shards, mesh=mesh, in_specs=placed, out_specs=P(None, "hrow", "hcol"), check_vma=False
    )
```

time: 196 us -> 98.8 us (0.50); the launches traced: 193 us -> 98.4 us
  waiting for transfers between devices: 130 us -> 28.1 us
  Pallas kernels: 0 us -> 21.7 us
  between operations: 14.2 us -> 0.27 us
  local copies, waits for them, and re-layouts: 5.68 us -> 10.5 us
  matrix products: 3.11 us -> 0 us
  starting transfers between devices: 37.3 us -> 35 us
    all_gather x1 -> x0, waiting for transfers between devices: 66.3 us -> none  [shards(): lax.all_gather(distrib, 'hrow', axis=1, tiled=True)]
    unnamed x3 -> x0, waiting for transfers between devices: 54 us -> none
    pallas_call x0 -> x6, Pallas kernels: none -> 21.7 us  [call(): pl.pallas_call(kernel, name=name, out_shape=out_shape, in_specs=specs, ou...]
    ppermute x10 -> x23, waiting for transfers between devices: 9.65 us -> 28.1 us  [swap(): lax.ppermute(block, axis, [(i, i ^ mask) for i in range(lax.axis_size(axi...]
    unnamed x4 -> x55, local copies, waits for them, and re-layouts: 2.11 us -> 5.31 us
    dot_general x1 -> x0, matrix products: 3.11 us -> none  [shards(): jnp.einsum('orn,scn->osrc', expect, lax.all_gather(distrib, 'hrow', axis=...]
    ppermute x10 -> x23, starting transfers between devices: 37.2 us -> 35 us  [swap(): lax.ppermute(block, axis, [(i, i ^ mask) for i in range(lax.axis_size(axi...]
    concatenate x1 -> x3, other arithmetic: 0.07 us -> 2.07 us  [with_rest(): jnp.concatenate([cut(values, plane), values[..., grid - rest:]], axis=-1)]
  transfers between devices with their start and end apart: 12 -> 23, of which waited for: 10 -> 7; matrix products, arithmetic and copies ran while one was open for 2% -> 4% of each run, Pallas kernels for 0% -> 13%
where the time goes in v1:
time: 98.8 us; the launch traced here: 98.4 us
  starting transfers between devices  35 us (35%)
  waiting for transfers between devices  28.1 us (28%)
  Pallas kernels  21.7 us (22%)
  local copies, waits for them, and re-layouts  10.5 us (11%)
  other arithmetic  2.77 us (3%)
    ppermute x23, starting transfers between devices, swap(): lax.ppermute(block, axis, [(i, i ^ mask) for i in range(lax.axis_size(axi...  35 us
    ppermute x23, waiting for transfers between devices, swap(): lax.ppermute(block, axis, [(i, i ^ mask) for i in range(lax.axis_size(axi...  28.1 us
    pallas_call x6, Pallas kernels, call(): pl.pallas_call(kernel, name=name, out_shape=out_shape, in_specs=specs, ou...  21.7 us
    unnamed x55, local copies, waits for them, and re-layouts  5.31 us
    concatenate x3, other arithmetic, with_rest(): jnp.concatenate([cut(values, plane), values[..., grid - rest:]], axis=-1)  2.07 us
  transfers between devices with their start and end apart: 23, of which 7 were waited for; matrix products, arithmetic and copies ran while one was open for 4% of the time, Pallas kernels for 13%

profile of v1, /device:TPU:0, one launch (start us, length us, event | category | flops | bytes accessed | tf_op | source)
XLA Modules:
  0.0 98.4 jit_solution(1078386659484898520)
XLA Ops:
  0.0 1.2 %fusion = (bf16[1,64,3200]{2,1,0:T(8,128)(2,1)S(1)}, bf16[64,3200]{1,0:T(8,128)(2,1)S(1)}, bf16[64,3200]{1,0:T(8,128)(2,1)S(1)}, bf16[1,64,3200]{2,1,0:T(8,128)(2,1)S(1)}) fusion(bf16[2,64,3200]{2,1,0:T(8,128)(2,1)} %param.5), kind=kLoop, calls=%fused_computation.34 | loop fusion | bytes 2457600 | tf_op jit(solution)/shard_map/slice | solution.py:156
  2.1 3.0 %collective-permute-start.13 = (bf16[64,896]{1,0:T(8,128)(2,1)S(1)}, bf16[64,896]{1,0:T(8,128)(2,1)S(1)}, u32[]{:S(2)}, u32[]{:S(2)}) collective-permute-start(bf16[64,896]{1,0:T(8,128)(2,1)S(1)} %get-tuple-element.54), channel_id=1, source_target_pairs={{0,8},{8,0},{16,24},{24,16},{1,9},{9,1},{17,25},{25,17},{2,10},{10... | collective-permute-start | bytes 344072 | tf_op jit(solution)/shard_map/ppermute | solution.py:15
  5.1 2.6 %collective-permute-start.14 = (bf16[64,896]{1,0:T(8,128)(2,1)S(1)}, bf16[64,896]{1,0:T(8,128)(2,1)S(1)}, u32[]{:S(2)}, u32[]{:S(2)}) collective-permute-start(bf16[64,896]{1,0:T(8,128)(2,1)S(1)} %get-tuple-element.55), channel_id=1, source_target_pairs={{0,16},{8,24},{16,0},{24,8},{1,17},{9,25},{17,1},{25,9},{2,18},{10... | collective-permute-start | bytes 344072 | tf_op jit(solution)/shard_map/ppermute | solution.py:15
  7.7 1.0 collective-permute-start
  8.7 3.5 %collective-permute-start.1 = (bf16[2,64,768]{2,1,0:T(8,128)(2,1)S(1)}, bf16[2,64,768]{2,1,0:T(8,128)(2,1)S(1)}, u32[]{:S(2)}, u32[]{:S(2)}) collective-permute-start(bf16[2,64,768]{2,1,0:T(8,128)(2,1)S(1)} %get-tuple-element.36), channel_id=1, source_target_pairs={{0,16},{8,24},{16,0},{24,8},{1,17},{9,25},{17,1},{25,9},{2,18},{10... | collective-permute-start | bytes 589832 | tf_op jit(solution)/shard_map/ppermute | solution.py:15
  13.7 4.8 %collective-permute-done.refs_0_ = bf16[2,64,768]{2,1,0:T(8,128)(2,1)S(1)} collective-permute-done((bf16[2,64,768]{2,1,0:T(8,128)(2,1)S(1)}, bf16[2,64,768]{2,1,0:T(8,128)(2,1)S(1)}, u32[]{:S(2)}, u32[]{:S(2)}) %collective-permute-start) | collective-permute-done | bytes 196640 | tf_op jit(solution)/shard_map/ppermute | solution.py:15
  18.4 3.5 %collective-permute-start.2 = (bf16[2,64,768]{2,1,0:T(8,128)(2,1)S(1)}, bf16[2,64,768]{2,1,0:T(8,128)(2,1)S(1)}, u32[]{:S(2)}, u32[]{:S(2)}) collective-permute-start(bf16[2,64,768]{2,1,0:T(8,128)(2,1)S(1)} %get-tuple-element.33), channel_id=1, source_target_pairs={{0,24},{8,16},{16,8},{24,0},{1,25},{9,17},{17,9},{25,1},{2,26},{10... | collective-permute-start | bytes 589832 | tf_op jit(solution)/shard_map/ppermute | solution.py:15
  22.7 9.2 %collective-permute-done.1.refs_1_ = bf16[2,64,768]{2,1,0:T(8,128)(2,1)S(1)} collective-permute-done((bf16[2,64,768]{2,1,0:T(8,128)(2,1)S(1)}, bf16[2,64,768]{2,1,0:T(8,128)(2,1)S(1)}, u32[]{:S(2)}, u32[]{:S(2)}) %collective-permute-start.1) | collective-permute-done | bytes 196640 | tf_op jit(solution)/shard_map/ppermute | solution.py:15
  33.3 2.3 %gather_rows.1.expect_ref = bf16[2,256,896]{2,1,0:T(8,128)(2,1)} custom-call(s32[2]{0:T(128)} %pad_add_fusion.spot_ref, bf16[2,64,896]{2,1,0:T(8,128)(2,1)} %pad_maximum_fusion.own_ref, bf16[2,64,768]{2,1,0:T(8,128)(2,1)} %copy-done.4, bf16[2,64,768]{2,1,0:T(8,128)(2,1)} %copy-done.5, bf16[2,64,768]{2,1,0:T(8,128)(2,1)} %copy-done.6), custom_call_target="tpu_custom_call" | custom-call | tf_op jit(solution)/shard_map/gather_rows/pallas_call | solution.py:105
  36.3 7.2 %partial_1.1 = (f32[4,2,32,256]{3,2,1,0:T(8,128)}, f32[4,2,32,256]{3,2,1,0:T(8,128)}) custom-call(s32[2]{0:T(128)} %pad_add_fusion.spot_ref, bf16[2,256,896]{2,1,0:T(8,128)(2,1)} %gather_rows.1.expect_ref, f32[2,2,256,1]{3,2,1,0:T(8,128)} %copy-done, bf16[64,896]{1,0:T(8,128)(2,1)} %get-tuple-element.56.refs_0_, bf16[64,896]{1,0:T(8,128)(2,1)} %copy-done.7, ...), custom_call_target="tpu_custom_call" | custom-call | tf_op jit(solution)/shard_map/partial_1/pallas_call | solution.py:105
  44.2 2.8 %collective-permute-start.3 = (bf16[64,896]{1,0:T(8,128)(2,1)S(1)}, bf16[64,896]{1,0:T(8,128)(2,1)S(1)}, u32[]{:S(2)}, u32[]{:S(2)}) collective-permute-start(bf16[64,896]{1,0:T(8,128)(2,1)S(1)} %get-tuple-element.58), channel_id=1, source_target_pairs={{0,8},{8,0},{16,24},{24,16},{1,9},{9,1},{17,25},{25,17},{2,10},{10... | collective-permute-start | bytes 344072 | tf_op jit(solution)/shard_map/ppermute | solution.py:15
  47.0 1.0 %collective-permute-start.4 = (bf16[64,896]{1,0:T(8,128)(2,1)S(1)}, bf16[64,896]{1,0:T(8,128)(2,1)S(1)}, u32[]{:S(2)}, u32[]{:S(2)}) collective-permute-start(bf16[64,896]{1,0:T(8,128)(2,1)S(1)} %get-tuple-element.59), channel_id=1, source_target_pairs={{0,16},{8,24},{16,0},{24,8},{1,17},{9,25},{17,1},{25,9},{2,18},{10... | collective-permute-start | bytes 344072 | tf_op jit(solution)/shard_map/ppermute | solution.py:15
  48.0 1.5 %collective-permute-start.5 = (bf16[64,896]{1,0:T(8,128)(2,1)S(1)}, bf16[64,896]{1,0:T(8,128)(2,1)S(1)}, u32[]{:S(2)}, u32[]{:S(2)}) collective-permute-start(bf16[64,896]{1,0:T(8,128)(2,1)S(1)} %get-tuple-element.57), channel_id=1, source_target_pairs={{0,24},{8,16},{16,8},{24,0},{1,25},{9,17},{17,9},{25,1},{2,26},{10... | collective-permute-start | bytes 344072 | tf_op jit(solution)/shard_map/ppermute | solution.py:15
  49.5 1.3 %collective-permute-done.3.refs_1_ = bf16[64,896]{1,0:T(8,128)(2,1)S(1)} collective-permute-done((bf16[64,896]{1,0:T(8,128)(2,1)S(1)}, bf16[64,896]{1,0:T(8,128)(2,1)S(1)}, u32[]{:S(2)}, u32[]{:S(2)}) %collective-permute-start.3) | collective-permute-done | bytes 114720 | tf_op jit(solution)/shard_map/ppermute | solution.py:15
  50.8 8.0 %collective-permute-done.4.refs_2_ = bf16[64,896]{1,0:T(8,128)(2,1)S(1)} collective-permute-done((bf16[64,896]{1,0:T(8,128)(2,1)S(1)}, bf16[64,896]{1,0:T(8,128)(2,1)S(1)}, u32[]{:S(2)}, u32[]{:S(2)}) %collective-permute-start.4) | collective-permute-done | bytes 114720 | tf_op jit(solution)/shard_map/ppermute | solution.py:15
  59.5 7.2 %partial_0.1 = (f32[4,2,32,256]{3,2,1,0:T(8,128)}, f32[4,2,32,256]{3,2,1,0:T(8,128)}) custom-call(s32[2]{0:T(128)} %pad_add_fusion.spot_ref, bf16[2,256,896]{2,1,0:T(8,128)(2,1)} %gather_rows.1.expect_ref, f32[2,2,256,1]{3,2,1,0:T(8,128)} %copy-done, bf16[64,896]{1,0:T(8,128)(2,1)} %get-tuple-element.60.refs_0_, bf16[64,896]{1,0:T(8,128)(2,1)} %copy-done.10, ...), custom_call_target="tpu_custom_call" | custom-call | tf_op jit(solution)/shard_map/partial_0/pallas_call | solution.py:105
  67.5 1.5 %collective-permute-start.17 = (f32[2,32,256]{2,1,0:T(8,128)S(1)}, f32[2,32,256]{2,1,0:T(8,128)S(1)}, u32[]{:S(2)}, u32[]{:S(2)}) collective-permute-start(f32[2,32,256]{2,1,0:T(8,128)S(1)} %get-tuple-element.47), channel_id=1, source_target_pairs={{0,2},{1,3},{2,0},{3,1},{4,6},{5,7},{6,4},{7,5},{8,10},{9,11},{10,... | collective-permute-start | bytes 196616 | tf_op jit(solution)/shard_map/ppermute | solution.py:15
  69.0 1.5 %collective-permute-start.18 = (f32[2,32,256]{2,1,0:T(8,128)S(1)}, f32[2,32,256]{2,1,0:T(8,128)S(1)}, u32[]{:S(2)}, u32[]{:S(2)}) collective-permute-start(f32[2,32,256]{2,1,0:T(8,128)S(1)} %get-tuple-element.46), channel_id=1, source_target_pairs={{0,4},{1,5},{2,6},{3,7},{4,0},{5,1},{6,2},{7,3},{8,12},{9,13},{10,... | collective-permute-start | bytes 196616 | tf_op jit(solution)/shard_map/ppermute | solution.py:15
  71.7 1.5 %collective-permute-start.7 = (f32[2,32,256]{2,1,0:T(8,128)S(1)}, f32[2,32,256]{2,1,0:T(8,128)S(1)}, u32[]{:S(2)}, u32[]{:S(2)}) collective-permute-start(f32[2,32,256]{2,1,0:T(8,128)S(1)} %get-tuple-element.51), channel_id=1, source_target_pairs={{0,2},{1,3},{2,0},{3,1},{4,6},{5,7},{6,4},{7,5},{8,10},{9,11},{10,... | collective-permute-start | bytes 196616 | tf_op jit(solution)/shard_map/ppermute | solution.py:15
  73.2 1.5 %collective-permute-start.8 = (f32[2,32,256]{2,1,0:T(8,128)S(1)}, f32[2,32,256]{2,1,0:T(8,128)S(1)}, u32[]{:S(2)}, u32[]{:S(2)}) collective-permute-start(f32[2,32,256]{2,1,0:T(8,128)S(1)} %get-tuple-element.50), channel_id=1, source_target_pairs={{0,4},{1,5},{2,6},{3,7},{4,0},{5,1},{6,2},{7,3},{8,12},{9,13},{10,... | collective-permute-start | bytes 196616 | tf_op jit(solution)/shard_map/ppermute | solution.py:15
  75.2 1.2 %collective-permute-done.19.refs_3_ = f32[2,32,256]{2,1,0:T(8,128)S(1)} collective-permute-done((f32[2,32,256]{2,1,0:T(8,128)S(1)}, f32[2,32,256]{2,1,0:T(8,128)S(1)}, u32[]{:S(2)}, u32[]{:S(2)}) %collective-permute-start.19) | collective-permute-done | bytes 65568 | tf_op jit(solution)/shard_map/ppermute | solution.py:15
  77.1 1.7 %pack_1.1 = (f32[32,128]{1,0:T(8,128)}, f32[32,128]{1,0:T(8,128)}, f32[32,128]{1,0:T(8,128)}, f32[32,128]{1,0:T(8,128)}) custom-call(s32[2]{0:T(128)} %pad_add_fusion.spot_ref, f32[2,32,256]{2,1,0:T(8,128)} %get-tuple-element.48.refs_0_, f32[2,32,256]{2,1,0:T(8,128)} %copy-done.15, f32[2,32,256]{2,1,0:T(8,128)} %copy-done.16, f32[2,32,256]{2,1,0:T(8,128)} %copy-done.18), custom_call_target="tpu_custom_call" | custom-call | tf_op jit(solution)/shard_map/pack_1/pallas_call | solution.py:105
  78.7 2.3 %collective-permute-start.20 = (f32[32,128]{1,0:T(8,128)}, f32[32,128]{1,0:T(8,128)S(1)}, u32[]{:S(2)}, u32[]{:S(2)}) collective-permute-start(f32[32,128]{1,0:T(8,128)} %get-tuple-element.26), channel_id=1, source_target_pairs={{0,8},{8,0},{16,24},{24,16},{1,9},{9,1},{17,25},{25,17},{2,10},{10... | collective-permute-start | bytes 49160 | tf_op jit(solution)/shard_map/ppermute | solution.py:15
  81.0 1.0 %collective-permute-start.21 = (f32[32,128]{1,0:T(8,128)}, f32[32,128]{1,0:T(8,128)S(1)}, u32[]{:S(2)}, u32[]{:S(2)}) collective-permute-start(f32[32,128]{1,0:T(8,128)} %get-tuple-element.27), channel_id=1, source_target_pairs={{0,16},{8,24},{16,0},{24,8},{1,17},{9,25},{17,1},{25,9},{2,18},{10... | collective-permute-start | bytes 49160 | tf_op jit(solution)/shard_map/ppermute | solution.py:15
  82.0 1.5 %collective-permute-start.22 = (f32[32,128]{1,0:T(8,128)}, f32[32,128]{1,0:T(8,128)S(1)}, u32[]{:S(2)}, u32[]{:S(2)}) collective-permute-start(f32[32,128]{1,0:T(8,128)} %get-tuple-element.28), channel_id=1, source_target_pairs={{0,24},{8,16},{16,8},{24,0},{1,25},{9,17},{17,9},{25,1},{2,26},{10... | collective-permute-start | bytes 49160 | tf_op jit(solution)/shard_map/ppermute | solution.py:15
  84.2 1.7 %pack_0.1 = (f32[32,128]{1,0:T(8,128)}, f32[32,128]{1,0:T(8,128)}, f32[32,128]{1,0:T(8,128)}, f32[32,128]{1,0:T(8,128)}) custom-call(s32[2]{0:T(128)} %pad_add_fusion.spot_ref, f32[2,32,256]{2,1,0:T(8,128)} %get-tuple-element.52.refs_0_, f32[2,32,256]{2,1,0:T(8,128)} %copy-done.13, f32[2,32,256]{2,1,0:T(8,128)} %copy-done.14, f32[2,32,256]{2,1,0:T(8,128)} %copy-done.17), custom_call_target="tpu_custom_call" | custom-call | tf_op jit(solution)/shard_map/pack_0/pallas_call | solution.py:105
  85.8 1.0 collective-permute-start.10
  86.8 1.9 %collective-permute-start.11 = (f32[32,128]{1,0:T(8,128)}, f32[32,128]{1,0:T(8,128)S(1)}, u32[]{:S(2)}, u32[]{:S(2)}) collective-permute-start(f32[32,128]{1,0:T(8,128)} %get-tuple-element.21), channel_id=1, source_target_pairs={{0,16},{8,24},{16,0},{24,8},{1,17},{9,25},{17,1},{25,9},{2,18},{10... | collective-permute-start | bytes 49160 | tf_op jit(solution)/shard_map/ppermute | solution.py:15
  88.8 1.5 %collective-permute-start.12 = (f32[32,128]{1,0:T(8,128)}, f32[32,128]{1,0:T(8,128)S(1)}, u32[]{:S(2)}, u32[]{:S(2)}) collective-permute-start(f32[32,128]{1,0:T(8,128)} %get-tuple-element.22), channel_id=1, source_target_pairs={{0,24},{8,16},{16,8},{24,0},{1,25},{9,17},{17,9},{25,1},{2,26},{10... | collective-permute-start | bytes 49160 | tf_op jit(solution)/shard_map/ppermute | solution.py:15
  91.7 2.8 %collective-permute-done.12.refs_3_ = f32[32,128]{1,0:T(8,128)S(1)} collective-permute-done((f32[32,128]{1,0:T(8,128)}, f32[32,128]{1,0:T(8,128)S(1)}, u32[]{:S(2)}, u32[]{:S(2)}) %collective-permute-start.12) | collective-permute-done | bytes 16416 | tf_op jit(solution)/shard_map/ppermute | solution.py:15
  95.1 1.6 %finish.1 = f32[4,64,32]{2,1,0:T(8,128)} custom-call(s32[4,2]{1,0:T(4,128)} %copy.6.pair_ref, f32[32,128]{1,0:T(8,128)} %get-tuple-element.19.refs_0_, f32[32,128]{1,0:T(8,128)} %copy-done.22, f32[32,128]{1,0:T(8,128)} %copy-done.23, f32[32,128]{1,0:T(8,128)} %copy-done.24, f32[32,128]{1,0:T(8,128)} %get-tuple-element.25.refs_4_, f32[32,128]{1,0:T(8,128)} %copy-done.19, ...), custom_call_target="tpu_custom_call" | custom-call | tf_op jit(solution)/shard_map/finish/pallas_call | solution.py:105
  96.7 1.6 %copy.7 = f32[4,64,32]{1,2,0:T(8,128)} copy(f32[4,64,32]{2,1,0:T(8,128)} %finish.1) | data formatting | bytes 65536 | tf_op jit(solution)/shard_map/finish/pallas_call | solution.py:105
  (95 shorter events, 12.2 us)
Async XLA Ops:
  1.3 6.3 %copy-start.1 = (bf16[2,64,3200]{2,1,0:T(8,128)(2,1)S(1)}, bf16[2,64,3200]{2,1,0:T(8,128)(2,1)}, u32[]{:S(2)}) copy-start(bf16[2,64,3200]{2,1,0:T(8,128)(2,1)} %param.4) | copy-start | bytes 2457604
  2.1 33.5 %collective-permute-start.13 = (bf16[64,896]{1,0:T(8,128)(2,1)S(1)}, bf16[64,896]{1,0:T(8,128)(2,1)S(1)}, u32[]{:S(2)}, u32[]{:S(2)}) collective-permute-start(bf16[64,896]{1,0:T(8,128)(2,1)S(1)} %get-tuple-element.54), channel_id=1, source_target_pairs={{0,8},{8,0},{16,24},{24,16},{1,9},{9,1},{17,25},{25,17},{2,10},{10... | collective-permute-start | bytes 344072 | tf_op jit(solution)/shard_map/ppermute | solution.py:15
  5.1 30.5 %collective-permute-start.14 = (bf16[64,896]{1,0:T(8,128)(2,1)S(1)}, bf16[64,896]{1,0:T(8,128)(2,1)S(1)}, u32[]{:S(2)}, u32[]{:S(2)}) collective-permute-start(bf16[64,896]{1,0:T(8,128)(2,1)S(1)} %get-tuple-element.55), channel_id=1, source_target_pairs={{0,16},{8,24},{16,0},{24,8},{1,17},{9,25},{17,1},{25,9},{2,18},{10... | collective-permute-start | bytes 344072 | tf_op jit(solution)/shard_map/ppermute | solution.py:15
  7.7 27.9 %collective-permute-start.15 = (bf16[64,896]{1,0:T(8,128)(2,1)S(1)}, bf16[64,896]{1,0:T(8,128)(2,1)S(1)}, u32[]{:S(2)}, u32[]{:S(2)}) collective-permute-start(bf16[64,896]{1,0:T(8,128)(2,1)S(1)} %get-tuple-element.53), channel_id=1, source_target_pairs={{0,24},{8,16},{16,8},{24,0},{1,25},{9,17},{17,9},{25,1},{2,26},{10... | collective-permute-start | bytes 344072 | tf_op jit(solution)/shard_map/ppermute | solution.py:15
  7.7 10.7 %collective-permute-start = (bf16[2,64,768]{2,1,0:T(8,128)(2,1)S(1)}, bf16[2,64,768]{2,1,0:T(8,128)(2,1)S(1)}, u32[]{:S(2)}, u32[]{:S(2)}) collective-permute-start(bf16[2,64,768]{2,1,0:T(8,128)(2,1)S(1)} %get-tuple-element.34), channel_id=1, source_target_pairs={{0,8},{8,0},{16,24},{24,16},{1,9},{9,1},{17,25},{25,17},{2,10},{10... | collective-permute-start | bytes 589832 | tf_op jit(solution)/shard_map/ppermute | solution.py:15
  8.7 23.2 %collective-permute-start.1 = (bf16[2,64,768]{2,1,0:T(8,128)(2,1)S(1)}, bf16[2,64,768]{2,1,0:T(8,128)(2,1)S(1)}, u32[]{:S(2)}, u32[]{:S(2)}) collective-permute-start(bf16[2,64,768]{2,1,0:T(8,128)(2,1)S(1)} %get-tuple-element.36), channel_id=1, source_target_pairs={{0,16},{8,24},{16,0},{24,8},{1,17},{9,25},{17,1},{25,9},{2,18},{10... | collective-permute-start | bytes 589832 | tf_op jit(solution)/shard_map/ppermute | solution.py:15
  18.4 4.3 %copy-start.4 = (bf16[2,64,768]{2,1,0:T(8,128)(2,1)}, bf16[2,64,768]{2,1,0:T(8,128)(2,1)S(1)}, u32[]{:S(2)}) copy-start(bf16[2,64,768]{2,1,0:T(8,128)(2,1)S(1)} %collective-permute-done.refs_0_) | copy-start | bytes 589828
  18.4 13.5 %collective-permute-start.2 = (bf16[2,64,768]{2,1,0:T(8,128)(2,1)S(1)}, bf16[2,64,768]{2,1,0:T(8,128)(2,1)S(1)}, u32[]{:S(2)}, u32[]{:S(2)}) collective-permute-start(bf16[2,64,768]{2,1,0:T(8,128)(2,1)S(1)} %get-tuple-element.33), channel_id=1, source_target_pairs={{0,24},{8,16},{16,8},{24,0},{1,25},{9,17},{17,9},{25,1},{2,26},{10... | collective-permute-start | bytes 589832 | tf_op jit(solution)/shard_map/ppermute | solution.py:15
  22.7 12.8 %copy-start = (f32[2,2,256,1]{3,2,1,0:T(8,128)}, f32[2,2,256,1]{3,2,1,0:T(8,128)S(1)}, u32[]{:S(2)}) copy-start(f32[2,2,256,1]{3,2,1,0:T(8,128)S(1)} %constant_dynamic-update-slice_fusion.direct_ref) | copy-start | bytes 12292
  43.5 23.3 %collective-permute-start.16 = (f32[4,2,32,256]{3,2,1,0:T(8,128)}, f32[4,2,32,256]{3,2,1,0:T(8,128)S(1)}, u32[]{:S(2)}, u32[]{:S(2)}) collective-permute-start(f32[4,2,32,256]{3,2,1,0:T(8,128)} %get-tuple-element.24), channel_id=1, source_target_pairs={{0,1},{1,0},{2,3},{3,2},{4,5},{5,4},{6,7},{7,6},{8,9},{9,8},{10,11... | collective-permute-start | bytes 786440 | tf_op jit(solution)/shard_map/ppermute | solution.py:15
  44.2 6.6 %collective-permute-start.3 = (bf16[64,896]{1,0:T(8,128)(2,1)S(1)}, bf16[64,896]{1,0:T(8,128)(2,1)S(1)}, u32[]{:S(2)}, u32[]{:S(2)}) collective-permute-start(bf16[64,896]{1,0:T(8,128)(2,1)S(1)} %get-tuple-element.58), channel_id=1, source_target_pairs={{0,8},{8,0},{16,24},{24,16},{1,9},{9,1},{17,25},{25,17},{2,10},{10... | collective-permute-start | bytes 344072 | tf_op jit(solution)/shard_map/ppermute | solution.py:15
  47.0 11.8 %collective-permute-start.4 = (bf16[64,896]{1,0:T(8,128)(2,1)S(1)}, bf16[64,896]{1,0:T(8,128)(2,1)S(1)}, u32[]{:S(2)}, u32[]{:S(2)}) collective-permute-start(bf16[64,896]{1,0:T(8,128)(2,1)S(1)} %get-tuple-element.59), channel_id=1, source_target_pairs={{0,16},{8,24},{16,0},{24,8},{1,17},{9,25},{17,1},{25,9},{2,18},{10... | collective-permute-start | bytes 344072 | tf_op jit(solution)/shard_map/ppermute | solution.py:15
  48.0 10.8 %collective-permute-start.5 = (bf16[64,896]{1,0:T(8,128)(2,1)S(1)}, bf16[64,896]{1,0:T(8,128)(2,1)S(1)}, u32[]{:S(2)}, u32[]{:S(2)}) collective-permute-start(bf16[64,896]{1,0:T(8,128)(2,1)S(1)} %get-tuple-element.57), channel_id=1, source_target_pairs={{0,24},{8,16},{16,8},{24,0},{1,25},{9,17},{17,9},{25,1},{2,26},{10... | collective-permute-start | bytes 344072 | tf_op jit(solution)/shard_map/ppermute | solution.py:15
  50.8 8.0 %copy-start.10 = (bf16[64,896]{1,0:T(8,128)(2,1)}, bf16[64,896]{1,0:T(8,128)(2,1)S(1)}, u32[]{:S(2)}) copy-start(bf16[64,896]{1,0:T(8,128)(2,1)S(1)} %collective-permute-done.3.refs_1_) | copy-start | bytes 344068
  59.5 7.3 %copy-start.2 = (f32[4,2,32,256]{3,2,1,0:T(8,128)S(1)}, f32[4,2,32,256]{3,2,1,0:T(8,128)}, u32[]{:S(2)}) copy-start(f32[4,2,32,256]{3,2,1,0:T(8,128)} %get-tuple-element.23) | copy-start | bytes 786436
  66.8 4.2 %collective-permute-start.6 = (f32[4,2,32,256]{3,2,1,0:T(8,128)}, f32[4,2,32,256]{3,2,1,0:T(8,128)S(1)}, u32[]{:S(2)}, u32[]{:S(2)}) collective-permute-start(f32[4,2,32,256]{3,2,1,0:T(8,128)} %get-tuple-element.18), channel_id=1, source_target_pairs={{0,1},{1,0},{2,3},{3,2},{4,5},{5,4},{6,7},{7,6},{8,9},{9,8},{10,11... | collective-permute-start | bytes 786440 | tf_op jit(solution)/shard_map/ppermute | solution.py:15
  66.8 4.2 %copy-start.3 = (f32[4,2,32,256]{3,2,1,0:T(8,128)S(1)}, f32[4,2,32,256]{3,2,1,0:T(8,128)}, u32[]{:S(2)}) copy-start(f32[4,2,32,256]{3,2,1,0:T(8,128)} %get-tuple-element.17) | copy-start | bytes 786436
  67.5 7.2 %collective-permute-start.17 = (f32[2,32,256]{2,1,0:T(8,128)S(1)}, f32[2,32,256]{2,1,0:T(8,128)S(1)}, u32[]{:S(2)}, u32[]{:S(2)}) collective-permute-start(f32[2,32,256]{2,1,0:T(8,128)S(1)} %get-tuple-element.47), channel_id=1, source_target_pairs={{0,2},{1,3},{2,0},{3,1},{4,6},{5,7},{6,4},{7,5},{8,10},{9,11},{10,... | collective-permute-start | bytes 196616 | tf_op jit(solution)/shard_map/ppermute | solution.py:15
  69.0 6.2 %collective-permute-start.18 = (f32[2,32,256]{2,1,0:T(8,128)S(1)}, f32[2,32,256]{2,1,0:T(8,128)S(1)}, u32[]{:S(2)}, u32[]{:S(2)}) collective-permute-start(f32[2,32,256]{2,1,0:T(8,128)S(1)} %get-tuple-element.46), channel_id=1, source_target_pairs={{0,4},{1,5},{2,6},{3,7},{4,0},{5,1},{6,2},{7,3},{8,12},{9,13},{10,... | collective-permute-start | bytes 196616 | tf_op jit(solution)/shard_map/ppermute | solution.py:15
  70.5 5.9 %collective-permute-start.19 = (f32[2,32,256]{2,1,0:T(8,128)S(1)}, f32[2,32,256]{2,1,0:T(8,128)S(1)}, u32[]{:S(2)}, u32[]{:S(2)}) collective-permute-start(f32[2,32,256]{2,1,0:T(8,128)S(1)} %get-tuple-element.45), channel_id=1, source_target_pairs={{0,6},{1,7},{2,4},{3,5},{4,2},{5,3},{6,0},{7,1},{8,14},{9,15},{10,... | collective-permute-start | bytes 196616 | tf_op jit(solution)/shard_map/ppermute | solution.py:15
  71.7 10.3 %collective-permute-start.7 = (f32[2,32,256]{2,1,0:T(8,128)S(1)}, f32[2,32,256]{2,1,0:T(8,128)S(1)}, u32[]{:S(2)}, u32[]{:S(2)}) collective-permute-start(f32[2,32,256]{2,1,0:T(8,128)S(1)} %get-tuple-element.51), channel_id=1, source_target_pairs={{0,2},{1,3},{2,0},{3,1},{4,6},{5,7},{6,4},{7,5},{8,10},{9,11},{10,... | collective-permute-start | bytes 196616 | tf_op jit(solution)/shard_map/ppermute | solution.py:15
  73.2 10.3 %collective-permute-start.8 = (f32[2,32,256]{2,1,0:T(8,128)S(1)}, f32[2,32,256]{2,1,0:T(8,128)S(1)}, u32[]{:S(2)}, u32[]{:S(2)}) collective-permute-start(f32[2,32,256]{2,1,0:T(8,128)S(1)} %get-tuple-element.50), channel_id=1, source_target_pairs={{0,4},{1,5},{2,6},{3,7},{4,0},{5,1},{6,2},{7,3},{8,12},{9,13},{10,... | collective-permute-start | bytes 196616 | tf_op jit(solution)/shard_map/ppermute | solution.py:15
  74.7 8.8 %collective-permute-start.9 = (f32[2,32,256]{2,1,0:T(8,128)S(1)}, f32[2,32,256]{2,1,0:T(8,128)S(1)}, u32[]{:S(2)}, u32[]{:S(2)}) collective-permute-start(f32[2,32,256]{2,1,0:T(8,128)S(1)} %get-tuple-element.49), channel_id=1, source_target_pairs={{0,6},{1,7},{2,4},{3,5},{4,2},{5,3},{6,0},{7,1},{8,14},{9,15},{10,... | collective-permute-start | bytes 196616 | tf_op jit(solution)/shard_map/ppermute | solution.py:15
  78.7 10.1 %collective-permute-start.20 = (f32[32,128]{1,0:T(8,128)}, f32[32,128]{1,0:T(8,128)S(1)}, u32[]{:S(2)}, u32[]{:S(2)}) collective-permute-start(f32[32,128]{1,0:T(8,128)} %get-tuple-element.26), channel_id=1, source_target_pairs={{0,8},{8,0},{16,24},{24,16},{1,9},{9,1},{17,25},{25,17},{2,10},{10... | collective-permute-start | bytes 49160 | tf_op jit(solution)/shard_map/ppermute | solution.py:15
  81.0 9.9 %collective-permute-start.21 = (f32[32,128]{1,0:T(8,128)}, f32[32,128]{1,0:T(8,128)S(1)}, u32[]{:S(2)}, u32[]{:S(2)}) collective-permute-start(f32[32,128]{1,0:T(8,128)} %get-tuple-element.27), channel_id=1, source_target_pairs={{0,16},{8,24},{16,0},{24,8},{1,17},{9,25},{17,1},{25,9},{2,18},{10... | collective-permute-start | bytes 49160 | tf_op jit(solution)/shard_map/ppermute | solution.py:15
  82.0 8.9 %collective-permute-start.22 = (f32[32,128]{1,0:T(8,128)}, f32[32,128]{1,0:T(8,128)S(1)}, u32[]{:S(2)}, u32[]{:S(2)}) collective-permute-start(f32[32,128]{1,0:T(8,128)} %get-tuple-element.28), channel_id=1, source_target_pairs={{0,24},{8,16},{16,8},{24,0},{1,25},{9,17},{17,9},{25,1},{2,26},{10... | collective-permute-start | bytes 49160 | tf_op jit(solution)/shard_map/ppermute | solution.py:15
  85.8 5.1 %collective-permute-start.10 = (f32[32,128]{1,0:T(8,128)}, f32[32,128]{1,0:T(8,128)S(1)}, u32[]{:S(2)}, u32[]{:S(2)}) collective-permute-start(f32[32,128]{1,0:T(8,128)} %get-tuple-element.20), channel_id=1, source_target_pairs={{0,8},{8,0},{16,24},{24,16},{1,9},{9,1},{17,25},{25,17},{2,10},{10... | collective-permute-start | bytes 49160 | tf_op jit(solution)/shard_map/ppermute | solution.py:15
  86.8 4.8 %collective-permute-start.11 = (f32[32,128]{1,0:T(8,128)}, f32[32,128]{1,0:T(8,128)S(1)}, u32[]{:S(2)}, u32[]{:S(2)}) collective-permute-start(f32[32,128]{1,0:T(8,128)} %get-tuple-element.21), channel_id=1, source_target_pairs={{0,16},{8,24},{16,0},{24,8},{1,17},{9,25},{17,1},{25,9},{2,18},{10... | collective-permute-start | bytes 49160 | tf_op jit(solution)/shard_map/ppermute | solution.py:15
  88.8 5.8 %copy-start.19 = (f32[32,128]{1,0:T(8,128)}, f32[32,128]{1,0:T(8,128)S(1)}, u32[]{:S(2)}) copy-start(f32[32,128]{1,0:T(8,128)S(1)} %collective-permute-done.20.refs_5_) | copy-start | bytes 49156
  88.8 5.7 %collective-permute-start.12 = (f32[32,128]{1,0:T(8,128)}, f32[32,128]{1,0:T(8,128)S(1)}, u32[]{:S(2)}, u32[]{:S(2)}) collective-permute-start(f32[32,128]{1,0:T(8,128)} %get-tuple-element.22), channel_id=1, source_target_pairs={{0,24},{8,16},{16,8},{24,0},{1,25},{9,17},{17,9},{25,1},{2,26},{10... | collective-permute-start | bytes 49160 | tf_op jit(solution)/shard_map/ppermute | solution.py:15
  90.9 3.6 %copy-start.20 = (f32[32,128]{1,0:T(8,128)}, f32[32,128]{1,0:T(8,128)S(1)}, u32[]{:S(2)}) copy-start(f32[32,128]{1,0:T(8,128)S(1)} %collective-permute-done.21.refs_6_) | copy-start | bytes 49156
  90.9 3.6 %copy-start.21 = (f32[32,128]{1,0:T(8,128)}, f32[32,128]{1,0:T(8,128)S(1)}, u32[]{:S(2)}) copy-start(f32[32,128]{1,0:T(8,128)S(1)} %collective-permute-done.22.refs_7_) | copy-start | bytes 49156
  (19 other events, 23.0 us)

commit v2 on v1

v2 whole, which is shorter than its diff:
```python
import functools
import math

import jax
import jax.numpy as jnp
from jax import lax
from jax.experimental import pallas as pl
from jax.experimental.pallas import tpu as pltpu
from jax.sharding import PartitionSpec as P

LANES = 128


def swap(block, axis, mask):
    return lax.ppermute(block, axis, [(i, i ^ mask) for i in range(lax.axis_size(axis))])


def add_diagonals(block):
    rows, dates = block.shape
    row_id = lax.broadcasted_iota(jnp.int32, (rows, dates), 0)
    date_id = lax.broadcasted_iota(jnp.int32, (rows, dates), 1)
    least = jnp.minimum(row_id, date_id)
    offset = 1
    while offset < rows:
        moved = pltpu.roll(pltpu.roll(block, offset, 1), offset, 0)
        block = block + jnp.where(least >= offset, moved, 0.0)
        offset = offset * 2
    return block, row_id, date_id


def partial_sums(shock, spot_ref, expect_at, direct_ref, keep_ref, give_ref, responses, products):
    horizon = products.shape[0]
    half = keep_ref.shape[2]
    step = min(horizon, 256)
    z = spot_ref[0]
    core = spot_ref[1]
    mine = pl.ds(pl.multiple_of(spot_ref[2] * half, half), half)
    first = lax.broadcasted_iota(jnp.int32, (half, LANES), 1) == 0
    for output in range(keep_ref.shape[1]):
        for start in range(0, horizon, step):
            products[start : start + step, :] = lax.dot_general(
                responses[start : start + step, :],
                expect_at(output),
                (((1,), (1,)), ((), ())),
                preferred_element_type=jnp.float32,
            )
        column = shock * keep_ref.shape[1] + output
        added = jnp.where(first & (z == 0), direct_ref[:, column : column + 1], 0.0)
        products[mine, :LANES] = products[mine, :LANES] + added
        last = None
        for start in range(0, horizon, step):
            block, row_id, date_id = add_diagonals(products[start : start + step, :])
            if last is not None:
                spread = jnp.broadcast_to(last, block.shape)
                moved = pltpu.roll(spread, 1, 1, stride=1, stride_axis=0)
                block = block + jnp.where(date_id > row_id, moved, 0.0)
            last = block[step - 1 :]
            for pair in range(step // (2 * half)):
                low = block[2 * pair * half : (2 * pair + 1) * half]
                high = block[(2 * pair + 1) * half : (2 * pair + 2) * half]
                keep_ref[start // (2 * half) + pair, output] = jnp.where(core == 0, low, high)
                give_ref[start // (2 * half) + pair, output] = jnp.where(core == 0, high, low)


def place(z, mask, rows):
    return pl.ds(pl.multiple_of((z ^ mask) * rows, rows), rows)


def first_kernel(width, planes, spot_ref, direct_ref, *refs):
    pieces = refs[:planes]
    expect_ref, keep_ref, give_ref, responses, products = refs[planes:]
    outputs = expect_ref.shape[0]
    rows = pieces[0].shape[0]
    z = spot_ref[0]
    expect_ref[:, :, width:] = jnp.zeros_like(expect_ref[:, :, width:])
    for mask, ref in enumerate(pieces):
        for output in range(outputs):
            expect_ref[output, place(z, mask, rows), :width] = ref[
                :, output * width : (output + 1) * width
            ]
        responses[place(z, mask, rows), :] = ref[:, outputs * width : outputs * width + responses.shape[1]]
    rest = responses.shape[1] - width
    for output in range(outputs):
        begin = outputs * width + responses.shape[1] + output * rest
        expect_ref[output, place(z, 0, rows), width:] = pieces[0][:, begin : begin + rest]
    partial_sums(
        0, spot_ref, lambda o: expect_ref[o], direct_ref, keep_ref, give_ref, responses, products
    )


def next_kernel(shock, planes, spot_ref, direct_ref, expect_ref, *refs):
    pieces = refs[:planes]
    keep_ref, give_ref, responses, products = refs[planes:]
    rows = pieces[0].shape[0]
    z = spot_ref[0]
    for mask, ref in enumerate(pieces):
        responses[place(z, mask, rows), :] = ref[...]
    partial_sums(
        shock, spot_ref, lambda o: expect_ref[o], direct_ref, keep_ref, give_ref, responses, products
    )


def pack_kernel(chips, planes, spot_ref, *refs):
    parts, outs, cut = refs[: len(refs) - 1 - planes], refs[-1 - planes : -1], refs[-1]
    z = spot_ref[0]
    for shock in range(len(parts) // chips):
        total = parts[shock * chips][...]
        for ref in parts[shock * chips + 1 : (shock + 1) * chips]:
            total = total + ref[...]
        width = total.shape[2] // planes
        for plane in range(planes):
            piece = total[:, :, plane * width : (plane + 1) * width]
            cut[plane, shock] = jnp.concatenate([piece[o] for o in range(piece.shape[0])], axis=1)
    for mask, ref in enumerate(outs):
        ref[...] = cut[z ^ mask]


def finish_kernel(pair_ref, *refs):
    *parts, out_ref, picked = refs
    rows = out_ref.shape[2]
    total = parts[0][...]
    for ref in parts[1:]:
        total = total + ref[...]
    for output in range(picked.shape[1]):
        picked[:, output] = total[:, :, output * rows : (output + 1) * rows]
    for pair in range(out_ref.shape[0]):
        out_ref[pair] = picked[pair_ref[pair, 0], pair_ref[pair, 1]]


def size_of(leaf):
    shape = leaf.shape[:-1] + (-(-leaf.shape[-1] // LANES) * LANES,)
    return math.prod(shape) * leaf.dtype.itemsize


def call(kernel, name, out_shape, scalars, arrays, scratch):
    held = sum(size_of(leaf) for leaf in jax.tree.leaves((arrays, out_shape)))
    held += sum(size_of(leaf) for leaf in scratch)
    return pl.pallas_call(
        kernel,
        name=name,
        out_shape=out_shape,
        in_specs=[pl.BlockSpec(memory_space=pltpu.SMEM)]
        + [pl.BlockSpec(memory_space=pltpu.VMEM)] * len(arrays),
        out_specs=jax.tree.map(lambda _: pl.BlockSpec(memory_space=pltpu.VMEM), out_shape),
        scratch_shapes=scratch,
        compiler_params=pltpu.CompilerParams(vmem_limit_bytes=held * 3 // 2 + (4 << 20)),
    )(scalars, *arrays)


def shards(expect, distrib, direct, pair_index):
    planes = lax.axis_size("hrow")
    col_devices = lax.axis_size("hcol")
    chips = col_devices // 2
    outputs, rows, grid = expect.shape
    shocks = distrib.shape[0]
    horizon = rows * planes
    cols = horizon // col_devices
    pairs = pair_index.shape[0]
    z = lax.axis_index("hrow")
    c = lax.axis_index("hcol")
    chip = c // 2
    spot = jnp.stack([z, c % 2, c]).astype(jnp.int32)

    width = grid // LANES // planes * LANES
    rest = grid - width * planes

    def cut(values, plane):
        return lax.dynamic_slice_in_dim(values, plane * width, width, axis=-1)

    def responses(shock, plane):
        return [cut(distrib[shock], plane), distrib[shock, :, grid - rest :]]

    def first_message(plane):
        return [cut(expect[o], plane) for o in range(outputs)] + responses(0, plane)

    masks = range(1, planes)
    own = jnp.concatenate(first_message(z) + [expect[o, :, grid - rest :] for o in range(outputs)], axis=1)
    pieces = [own] + [
        swap(jnp.concatenate(first_message(z ^ m), axis=1), "hrow", m) for m in masks
    ]
    later = [
        [jnp.concatenate(responses(shock, z), axis=1)]
        + [swap(jnp.concatenate(responses(shock, z ^ m), axis=1), "hrow", m) for m in masks]
        for shock in range(1, shocks)
    ]
    flat = direct.reshape(shocks * outputs, cols).T

    part = jax.ShapeDtypeStruct((chips, outputs, cols, horizon), jnp.float32)
    scratch = [
        pltpu.VMEM((horizon, width + rest), distrib.dtype),
        pltpu.VMEM((horizon, horizon), jnp.float32),
    ]
    parts = []
    for shock in range(shocks):
        if shock == 0:
            expect_all, keep, give = call(
                functools.partial(first_kernel, width, planes),
                "partial_0",
                (jax.ShapeDtypeStruct((outputs, horizon, width + rest), expect.dtype), part, part),
                spot,
                [flat] + pieces,
                scratch,
            )
        else:
            keep, give = call(
                functools.partial(next_kernel, shock, planes),
                f"partial_{shock}",
                (part, part),
                spot,
                [flat, expect_all] + later[shock - 1],
                scratch,
            )
        chip_sums = keep + swap(give, "hcol", 1)

        def of_chip(index):
            return lax.dynamic_index_in_dim(chip_sums, index, 0, False)

        parts += [of_chip(chip)] + [swap(of_chip(chip ^ m), "hcol", 2 * m) for m in range(1, chips)]

    packed = jax.ShapeDtypeStruct((shocks, cols, outputs * rows), jnp.float32)
    cuts = call(
        functools.partial(pack_kernel, chips, planes),
        "pack",
        (packed,) * planes,
        spot,
        parts,
        [pltpu.VMEM((planes, shocks, cols, outputs * rows), jnp.float32)],
    )
    turned = call(
        finish_kernel,
        "finish",
        jax.ShapeDtypeStruct((pairs, cols, rows), jnp.float32),
        pair_index,
        [cuts[0]] + [swap(cuts[m], "hrow", m) for m in masks],
        [pltpu.VMEM((shocks, outputs, cols, rows), jnp.float32)],
    )
    return jnp.swapaxes(turned, 1, 2)


def solution(mesh):
    placed = (P(None, "hrow", "hcol"), P(None, "hrow", "hcol"), P(None, None, "hcol"), P())
    return jax.shard_map(
        shards, mesh=mesh, in_specs=placed, out_specs=P(None, "hrow", "hcol"), check_vma=False
    )
```

time: 98.8 us -> 77 us (0.78)
  Pallas kernels: 21.7 us -> 5.97 us
  waiting for transfers between devices: 28.1 us -> 38.8 us
  starting transfers between devices: 35 us -> 26 us
  local copies, waits for them, and re-layouts: 10.5 us -> 4.55 us
  other arithmetic: 2.77 us -> 1.18 us
    pallas_call x6 -> x4, Pallas kernels: 21.7 us -> 5.97 us  [call(): pl.pallas_call(kernel, name=name, out_shape=out_shape, in_specs=[pl.Block...]
    ppermute x23 -> x17, waiting for transfers between devices: 28.1 us -> 38.8 us  [swap(): lax.ppermute(block, axis, [(i, i ^ mask) for i in range(lax.axis_size(axi...]
    ppermute x23 -> x17, starting transfers between devices: 35 us -> 26 us  [swap(): lax.ppermute(block, axis, [(i, i ^ mask) for i in range(lax.axis_size(axi...]
    unnamed x55 -> x16, local copies, waits for them, and re-layouts: 5.31 us -> 1.55 us
    pallas_call x1 -> x0, local copies, waits for them, and re-layouts: 1.62 us -> none  [call(): pl.pallas_call(kernel, name=name, out_shape=out_shape, in_specs=specs, ou...]
    squeeze x2, local copies, waits for them, and re-layouts: 1.31 us -> 0.06 us  [of_chip(): return lax.dynamic_index_in_dim(chip_sums, index, 0, False)]
    concatenate x3 -> x2, other arithmetic: 2.07 us -> 1.02 us  [the longest x1 0.99 us: shards(): jnp.concatenate(first_message(z ^ m), axis=1)]
    slice x5 -> x2, local copies, waits for them, and re-layouts: 2 us -> 1.31 us  [the longest x1 1.26 us: responses(): return [cut(distrib[shock], plane), distrib[shock, :, grid - rest:]]]
  transfers between devices with their start and end apart: 23 -> 17, of which waited for: 7 -> 9; matrix products, arithmetic and copies ran while one was open for 4% -> 2% of each run, Pallas kernels for 13% -> 3%
where the time goes in v2:
time: 77 us; the launch traced here: 76.7 us
  waiting for transfers between devices  38.8 us (50%)
  starting transfers between devices  26 us (34%)
  Pallas kernels  5.97 us (8%)
  local copies, waits for them, and re-layouts  4.55 us (6%)
  other arithmetic  1.18 us (2%)
    ppermute x17, waiting for transfers between devices, swap(): lax.ppermute(block, axis, [(i, i ^ mask) for i in range(lax.axis_size(axi...  38.8 us
    ppermute x17, starting transfers between devices, swap(): lax.ppermute(block, axis, [(i, i ^ mask) for i in range(lax.axis_size(axi...  26 us
    pallas_call x4, Pallas kernels, call(): pl.pallas_call(kernel, name=name, out_shape=out_shape, in_specs=[pl.Block...  5.97 us
    unnamed x16, local copies, waits for them, and re-layouts  1.55 us
  transfers between devices with their start and end apart: 17, of which 9 were waited for; matrix products, arithmetic and copies ran while one was open for 2% of the time, Pallas kernels for 3%

profile of v2, /device:TPU:0, one launch (start us, length us, event | category | flops | bytes accessed | tf_op | source)
XLA Modules:
  0.0 76.7 jit_solution(5883201357896232161)
XLA Ops:
  0.0 1.3 %fusion = (bf16[1,64,3200]{2,1,0:T(8,128)(2,1)S(1)}, bf16[1,64,3200]{2,1,0:T(8,128)(2,1)S(1)}) fusion(bf16[2,64,3200]{2,1,0:T(8,128)(2,1)} %param.5), kind=kLoop, calls=%fused_computation.37 | loop fusion | bytes 1638400 | tf_op jit(solution)/shard_map/slice | solution.py:171
  1.3 0.7 slice_bitcast_fusion
  2.1 0.7 dynamic-slice_bitcast_fusion
  2.9 1.0 %pad_maximum_fusion = (bf16[64,2432]{1,0:T(8,128)(2,1)}, bf16[64,2432]{1,0:T(8,128)(2,1)}, bf16[64,2432]{1,0:T(8,128)(2,1)}) fusion(bf16[64,128]{1,0:T(8,128)(2,1)S(1)} %get-tuple-element.26, bf16[64,768]{1,0:T(8,128)(2,1)S(1)} %get-tuple-element.62, bf16[64,768]{1,0:T(8,128)(2,1)S(1)} %get-tuple-element.36, bf16[64,768]{1,0:T(8,128)(2,1)S(1)} %get-tuple-element.59, ...), kind=kLoop, calls=%fused_computation | loop fusion | flops 3424256 | bytes 1835008 | tf_op jit(solution)/shard_map/concatenate | solution.py:179
  3.9 3.0 %collective-permute-start = (bf16[64,2432]{1,0:T(8,128)(2,1)}, bf16[64,2432]{1,0:T(8,128)(2,1)S(1)}, u32[]{:S(2)}, u32[]{:S(2)}) collective-permute-start(bf16[64,2432]{1,0:T(8,128)(2,1)} %get-tuple-element.55), channel_id=1, source_target_pairs={{0,8},{8,0},{16,24},{24,16},{1,9},{9,1},{17,25},{25,17},{2,10},{10... | collective-permute-start | bytes 933896 | tf_op jit(solution)/shard_map/ppermute | solution.py:15
  6.9 2.6 %collective-permute-start.1 = (bf16[64,2432]{1,0:T(8,128)(2,1)}, bf16[64,2432]{1,0:T(8,128)(2,1)S(1)}, u32[]{:S(2)}, u32[]{:S(2)}) collective-permute-start(bf16[64,2432]{1,0:T(8,128)(2,1)} %get-tuple-element.56), channel_id=1, source_target_pairs={{0,16},{8,24},{16,0},{24,8},{1,17},{9,25},{17,1},{25,9},{2,18},{10... | collective-permute-start | bytes 933896 | tf_op jit(solution)/shard_map/ppermute | solution.py:15
  9.5 0.7 copy-done.3
  10.3 0.7 constant_dynamic-update-slice_fusion
  11.1 9.2 %collective-permute-done.refs_1_ = bf16[64,2432]{1,0:T(8,128)(2,1)S(1)} collective-permute-done((bf16[64,2432]{1,0:T(8,128)(2,1)}, bf16[64,2432]{1,0:T(8,128)(2,1)S(1)}, u32[]{:S(2)}, u32[]{:S(2)}) %collective-permute-start) | collective-permute-done | bytes 311328 | tf_op jit(solution)/shard_map/ppermute | solution.py:15
  20.4 11.3 %collective-permute-done.1.refs_2_ = bf16[64,2432]{1,0:T(8,128)(2,1)S(1)} collective-permute-done((bf16[64,2432]{1,0:T(8,128)(2,1)}, bf16[64,2432]{1,0:T(8,128)(2,1)S(1)}, u32[]{:S(2)}, u32[]{:S(2)}) %collective-permute-start.1) | collective-permute-done | bytes 311328 | tf_op jit(solution)/shard_map/ppermute | solution.py:15
  31.6 2.1 %partial_0.1 = (bf16[2,256,896]{2,1,0:T(8,128)(2,1)S(1)}, f32[4,2,32,256]{3,2,1,0:T(8,128)S(1)}, f32[4,2,32,256]{3,2,1,0:T(8,128)S(1)}) custom-call(s32[3]{0:T(128)S(1)} %pad_add_fusion.spot_ref, f32[32,4]{1,0:T(8,128)S(1)} %bitcast.64, bf16[64,2688]{1,0:T(8,128)(2,1)S(1)} %bitcast_dynamic-update-slice_fusion.3.refs_0_, ...), custom_call_target="tpu_custom_call" | custom-call | tf_op jit(solution)/shard_map/partial_0/pallas_call | solution.py:138
  33.9 5.9 %collective-permute-start.7 = (bf16[64,896]{1,0:T(8,128)(2,1)S(1)}, bf16[64,896]{1,0:T(8,128)(2,1)S(1)}, u32[]{:S(2)}, u32[]{:S(2)}) collective-permute-start(bf16[64,896]{1,0:T(8,128)(2,1)S(1)} %get-tuple-element.51), channel_id=1, source_target_pairs={{0,8},{8,0},{16,24},{24,16},{1,9},{9,1},{17,25},{25,17},{2,10},{10... | collective-permute-start | bytes 344072 | tf_op jit(solution)/shard_map/ppermute | solution.py:15
  39.7 1.1 %collective-permute-start.8 = (bf16[64,896]{1,0:T(8,128)(2,1)S(1)}, bf16[64,896]{1,0:T(8,128)(2,1)S(1)}, u32[]{:S(2)}, u32[]{:S(2)}) collective-permute-start(bf16[64,896]{1,0:T(8,128)(2,1)S(1)} %get-tuple-element.52), channel_id=1, source_target_pairs={{0,16},{8,24},{16,0},{24,8},{1,17},{9,25},{17,1},{25,9},{2,18},{10... | collective-permute-start | bytes 344072 | tf_op jit(solution)/shard_map/ppermute | solution.py:15
  40.8 1.4 %collective-permute-start.9 = (bf16[64,896]{1,0:T(8,128)(2,1)S(1)}, bf16[64,896]{1,0:T(8,128)(2,1)S(1)}, u32[]{:S(2)}, u32[]{:S(2)}) collective-permute-start(bf16[64,896]{1,0:T(8,128)(2,1)S(1)} %get-tuple-element.50), channel_id=1, source_target_pairs={{0,24},{8,16},{16,8},{24,0},{1,25},{9,17},{17,9},{25,1},{2,26},{10... | collective-permute-start | bytes 344072 | tf_op jit(solution)/shard_map/ppermute | solution.py:15
  42.2 1.3 %collective-permute-done.7.refs_1_ = bf16[64,896]{1,0:T(8,128)(2,1)S(1)} collective-permute-done((bf16[64,896]{1,0:T(8,128)(2,1)S(1)}, bf16[64,896]{1,0:T(8,128)(2,1)S(1)}, u32[]{:S(2)}, u32[]{:S(2)}) %collective-permute-start.7) | collective-permute-done | bytes 114720 | tf_op jit(solution)/shard_map/ppermute | solution.py:15
  43.5 8.0 %collective-permute-done.8.refs_2_ = bf16[64,896]{1,0:T(8,128)(2,1)S(1)} collective-permute-done((bf16[64,896]{1,0:T(8,128)(2,1)S(1)}, bf16[64,896]{1,0:T(8,128)(2,1)S(1)}, u32[]{:S(2)}, u32[]{:S(2)}) %collective-permute-start.8) | collective-permute-done | bytes 114720 | tf_op jit(solution)/shard_map/ppermute | solution.py:15
  51.6 2.0 %partial_1.1 = (f32[4,2,32,256]{3,2,1,0:T(8,128)S(1)}, f32[4,2,32,256]{3,2,1,0:T(8,128)S(1)}) custom-call(s32[3]{0:T(128)S(1)} %pad_add_fusion.spot_ref, f32[32,4]{1,0:T(8,128)S(1)} %bitcast.65, bf16[2,256,896]{2,1,0:T(8,128)(2,1)S(1)} %get-tuple-element.16.expect_ref, bf16[64,896]{1,0:T(8,128)(2,1)S(1)} %get-tuple-element.53.refs_0_, ...), custom_call_target="tpu_custom_call" | custom-call | tf_op jit(solution)/shard_map/partial_1/pallas_call | solution.py:138
  53.8 1.5 %collective-permute-start.4 = (f32[2,32,256]{2,1,0:T(8,128)S(1)}, f32[2,32,256]{2,1,0:T(8,128)S(1)}, u32[]{:S(2)}, u32[]{:S(2)}) collective-permute-start(f32[2,32,256]{2,1,0:T(8,128)S(1)} %get-tuple-element.48), channel_id=1, source_target_pairs={{0,2},{1,3},{2,0},{3,1},{4,6},{5,7},{6,4},{7,5},{8,10},{9,11},{10,... | collective-permute-start | bytes 196616 | tf_op jit(solution)/shard_map/ppermute | solution.py:15
  55.3 1.5 %collective-permute-start.5 = (f32[2,32,256]{2,1,0:T(8,128)S(1)}, f32[2,32,256]{2,1,0:T(8,128)S(1)}, u32[]{:S(2)}, u32[]{:S(2)}) collective-permute-start(f32[2,32,256]{2,1,0:T(8,128)S(1)} %get-tuple-element.47), channel_id=1, source_target_pairs={{0,4},{1,5},{2,6},{3,7},{4,0},{5,1},{6,2},{7,3},{8,12},{9,13},{10,... | collective-permute-start | bytes 196616 | tf_op jit(solution)/shard_map/ppermute | solution.py:15
  56.8 0.5 collective-permute-start.6
  57.4 1.5 %collective-permute-start.11 = (f32[2,32,256]{2,1,0:T(8,128)S(1)}, f32[2,32,256]{2,1,0:T(8,128)S(1)}, u32[]{:S(2)}, u32[]{:S(2)}) collective-permute-start(f32[2,32,256]{2,1,0:T(8,128)S(1)} %get-tuple-element.44), channel_id=1, source_target_pairs={{0,2},{1,3},{2,0},{3,1},{4,6},{5,7},{6,4},{7,5},{8,10},{9,11},{10,... | collective-permute-start | bytes 196616 | tf_op jit(solution)/shard_map/ppermute | solution.py:15
  58.9 1.5 %collective-permute-start.12 = (f32[2,32,256]{2,1,0:T(8,128)S(1)}, f32[2,32,256]{2,1,0:T(8,128)S(1)}, u32[]{:S(2)}, u32[]{:S(2)}) collective-permute-start(f32[2,32,256]{2,1,0:T(8,128)S(1)} %get-tuple-element.43), channel_id=1, source_target_pairs={{0,4},{1,5},{2,6},{3,7},{4,0},{5,1},{6,2},{7,3},{8,12},{9,13},{10,... | collective-permute-start | bytes 196616 | tf_op jit(solution)/shard_map/ppermute | solution.py:15
  61.0 1.4 %collective-permute-done.6.refs_3_ = f32[2,32,256]{2,1,0:T(8,128)S(1)} collective-permute-done((f32[2,32,256]{2,1,0:T(8,128)S(1)}, f32[2,32,256]{2,1,0:T(8,128)S(1)}, u32[]{:S(2)}, u32[]{:S(2)}) %collective-permute-start.6) | collective-permute-done | bytes 65568 | tf_op jit(solution)/shard_map/ppermute | solution.py:15
  62.3 1.6 %collective-permute-done.12.refs_6_ = f32[2,32,256]{2,1,0:T(8,128)S(1)} collective-permute-done((f32[2,32,256]{2,1,0:T(8,128)S(1)}, f32[2,32,256]{2,1,0:T(8,128)S(1)}, u32[]{:S(2)}, u32[]{:S(2)}) %collective-permute-start.12) | collective-permute-done | bytes 65568 | tf_op jit(solution)/shard_map/ppermute | solution.py:15
  63.9 1.7 %collective-permute-done.13.refs_7_ = f32[2,32,256]{2,1,0:T(8,128)S(1)} collective-permute-done((f32[2,32,256]{2,1,0:T(8,128)S(1)}, f32[2,32,256]{2,1,0:T(8,128)S(1)}, u32[]{:S(2)}, u32[]{:S(2)}) %collective-permute-start.13) | collective-permute-done | bytes 65568 | tf_op jit(solution)/shard_map/ppermute | solution.py:15
  65.6 0.7 pack.1
  66.3 2.3 %collective-permute-start.14 = (f32[2,32,128]{2,1,0:T(8,128)S(1)}, f32[2,32,128]{2,1,0:T(8,128)S(1)}, u32[]{:S(2)}, u32[]{:S(2)}) collective-permute-start(f32[2,32,128]{2,1,0:T(8,128)S(1)} %get-tuple-element.20), channel_id=1, source_target_pairs={{0,8},{8,0},{16,24},{24,16},{1,9},{9,1},{17,25},{25,17},{2,10},{10... | collective-permute-start | bytes 98312 | tf_op jit(solution)/shard_map/ppermute | solution.py:15
  68.6 1.1 %collective-permute-start.15 = (f32[2,32,128]{2,1,0:T(8,128)S(1)}, f32[2,32,128]{2,1,0:T(8,128)S(1)}, u32[]{:S(2)}, u32[]{:S(2)}) collective-permute-start(f32[2,32,128]{2,1,0:T(8,128)S(1)} %get-tuple-element.21), channel_id=1, source_target_pairs={{0,16},{8,24},{16,0},{24,8},{1,17},{9,25},{17,1},{25,9},{2,18},{10... | collective-permute-start | bytes 98312 | tf_op jit(solution)/shard_map/ppermute | solution.py:15
  69.7 1.4 %collective-permute-start.16 = (f32[2,32,128]{2,1,0:T(8,128)S(1)}, f32[2,32,128]{2,1,0:T(8,128)S(1)}, u32[]{:S(2)}, u32[]{:S(2)}) collective-permute-start(f32[2,32,128]{2,1,0:T(8,128)S(1)} %get-tuple-element.22), channel_id=1, source_target_pairs={{0,24},{8,16},{16,8},{24,0},{1,25},{9,17},{17,9},{25,1},{2,26},{10... | collective-permute-start | bytes 98312 | tf_op jit(solution)/shard_map/ppermute | solution.py:15
  71.2 2.5 %collective-permute-done.15.refs_2_ = f32[2,32,128]{2,1,0:T(8,128)S(1)} collective-permute-done((f32[2,32,128]{2,1,0:T(8,128)S(1)}, f32[2,32,128]{2,1,0:T(8,128)S(1)}, u32[]{:S(2)}, u32[]{:S(2)}) %collective-permute-start.15) | collective-permute-done | bytes 32800 | tf_op jit(solution)/shard_map/ppermute | solution.py:15
  73.7 1.8 %collective-permute-done.16.refs_3_ = f32[2,32,128]{2,1,0:T(8,128)S(1)} collective-permute-done((f32[2,32,128]{2,1,0:T(8,128)S(1)}, f32[2,32,128]{2,1,0:T(8,128)S(1)}, u32[]{:S(2)}, u32[]{:S(2)}) %collective-permute-start.16) | collective-permute-done | bytes 32800 | tf_op jit(solution)/shard_map/ppermute | solution.py:15
  75.4 1.3 %finish.1 = f32[4,32,64]{2,1,0:T(8,128)} custom-call(s32[4,2]{1,0:T(4,128)S(1)} %copy.6.pair_ref, f32[2,32,128]{2,1,0:T(8,128)S(1)} %get-tuple-element.19.refs_0_, f32[2,32,128]{2,1,0:T(8,128)S(1)} %collective-permute-done.14.refs_1_, f32[2,32,128]{2,1,0:T(8,128)S(1)} %collective-permute-done.15.refs_2_, f32[2,32,128]{2,1,0:T(8,128)S(1)} %collective-permute-done.16.refs_3_), custom_call_target="tpu_custom_call" | custom-call | tf_op jit(solution)/shard_map/finish/pallas_call | solution.py:138
  (36 shorter events, 1.3 us)
Async XLA Ops:
  0.0 2.0 %copy-start = (bf16[2,64,3200]{2,1,0:T(8,128)(2,1)S(1)}, bf16[2,64,3200]{2,1,0:T(8,128)(2,1)}, u32[]{:S(2)}) copy-start(bf16[2,64,3200]{2,1,0:T(8,128)(2,1)} %param.4) | copy-start | bytes 2457604
  3.9 16.5 %collective-permute-start = (bf16[64,2432]{1,0:T(8,128)(2,1)}, bf16[64,2432]{1,0:T(8,128)(2,1)S(1)}, u32[]{:S(2)}, u32[]{:S(2)}) collective-permute-start(bf16[64,2432]{1,0:T(8,128)(2,1)} %get-tuple-element.55), channel_id=1, source_target_pairs={{0,8},{8,0},{16,24},{24,16},{1,9},{9,1},{17,25},{25,17},{2,10},{10... | collective-permute-start | bytes 933896 | tf_op jit(solution)/shard_map/ppermute | solution.py:15
  6.9 24.7 %collective-permute-start.1 = (bf16[64,2432]{1,0:T(8,128)(2,1)}, bf16[64,2432]{1,0:T(8,128)(2,1)S(1)}, u32[]{:S(2)}, u32[]{:S(2)}) collective-permute-start(bf16[64,2432]{1,0:T(8,128)(2,1)} %get-tuple-element.56), channel_id=1, source_target_pairs={{0,16},{8,24},{16,0},{24,8},{1,17},{9,25},{17,1},{25,9},{2,18},{10... | collective-permute-start | bytes 933896 | tf_op jit(solution)/shard_map/ppermute | solution.py:15
  9.5 22.1 %collective-permute-start.2 = (bf16[64,2432]{1,0:T(8,128)(2,1)}, bf16[64,2432]{1,0:T(8,128)(2,1)S(1)}, u32[]{:S(2)}, u32[]{:S(2)}) collective-permute-start(bf16[64,2432]{1,0:T(8,128)(2,1)} %get-tuple-element.54), channel_id=1, source_target_pairs={{0,24},{8,16},{16,8},{24,0},{1,25},{9,17},{17,9},{25,1},{2,26},{10... | collective-permute-start | bytes 933896 | tf_op jit(solution)/shard_map/ppermute | solution.py:15
  9.5 0.7 copy-start.3
  31.6 2.1 %copy-start.1 = (bf16[64,768]{1,0:T(8,128)(2,1)S(1)}, bf16[64,768]{1,0:T(8,128)(2,1)}, u32[]{:S(2)}) copy-start(bf16[64,768]{1,0:T(8,128)(2,1)} %get-tuple-element.31) | copy-start | bytes 294916
  31.6 2.2 %copy-start.2 = (bf16[64,768]{1,0:T(8,128)(2,1)S(1)}, bf16[64,768]{1,0:T(8,128)(2,1)}, u32[]{:S(2)}) copy-start(bf16[64,768]{1,0:T(8,128)(2,1)} %get-tuple-element.32) | copy-start | bytes 294916
  33.7 20.0 %collective-permute-start.3 = (f32[4,2,32,256]{3,2,1,0:T(8,128)S(1)}, f32[4,2,32,256]{3,2,1,0:T(8,128)S(1)}, u32[]{:S(2)}, u32[]{:S(2)}) collective-permute-start(f32[4,2,32,256]{3,2,1,0:T(8,128)S(1)} %get-tuple-element.15), channel_id=1, source_target_pairs={{0,1},{1,0},{2,3},{3,2},{4,5},{5,4},{6,7},{7,6},{8,9},{9,8},{10,11... | collective-permute-start | bytes 786440 | tf_op jit(solution)/shard_map/ppermute | solution.py:15
  33.9 9.7 %collective-permute-start.7 = (bf16[64,896]{1,0:T(8,128)(2,1)S(1)}, bf16[64,896]{1,0:T(8,128)(2,1)S(1)}, u32[]{:S(2)}, u32[]{:S(2)}) collective-permute-start(bf16[64,896]{1,0:T(8,128)(2,1)S(1)} %get-tuple-element.51), channel_id=1, source_target_pairs={{0,8},{8,0},{16,24},{24,16},{1,9},{9,1},{17,25},{25,17},{2,10},{10... | collective-permute-start | bytes 344072 | tf_op jit(solution)/shard_map/ppermute | solution.py:15
  39.7 11.8 %collective-permute-start.8 = (bf16[64,896]{1,0:T(8,128)(2,1)S(1)}, bf16[64,896]{1,0:T(8,128)(2,1)S(1)}, u32[]{:S(2)}, u32[]{:S(2)}) collective-permute-start(bf16[64,896]{1,0:T(8,128)(2,1)S(1)} %get-tuple-element.52), channel_id=1, source_target_pairs={{0,16},{8,24},{16,0},{24,8},{1,17},{9,25},{17,1},{25,9},{2,18},{10... | collective-permute-start | bytes 344072 | tf_op jit(solution)/shard_map/ppermute | solution.py:15
  40.8 10.8 %collective-permute-start.9 = (bf16[64,896]{1,0:T(8,128)(2,1)S(1)}, bf16[64,896]{1,0:T(8,128)(2,1)S(1)}, u32[]{:S(2)}, u32[]{:S(2)}) collective-permute-start(bf16[64,896]{1,0:T(8,128)(2,1)S(1)} %get-tuple-element.50), channel_id=1, source_target_pairs={{0,24},{8,16},{16,8},{24,0},{1,25},{9,17},{17,9},{25,1},{2,26},{10... | collective-permute-start | bytes 344072 | tf_op jit(solution)/shard_map/ppermute | solution.py:15
  53.6 3.8 %collective-permute-start.10 = (f32[4,2,32,256]{3,2,1,0:T(8,128)S(1)}, f32[4,2,32,256]{3,2,1,0:T(8,128)S(1)}, u32[]{:S(2)}, u32[]{:S(2)}) collective-permute-start(f32[4,2,32,256]{3,2,1,0:T(8,128)S(1)} %get-tuple-element.18), channel_id=1, source_target_pairs={{0,1},{1,0},{2,3},{3,2},{4,5},{5,4},{6,7},{7,6},{8,9},{9,8},{10,11... | collective-permute-start | bytes 786440 | tf_op jit(solution)/shard_map/ppermute | solution.py:15
  53.8 6.7 %collective-permute-start.4 = (f32[2,32,256]{2,1,0:T(8,128)S(1)}, f32[2,32,256]{2,1,0:T(8,128)S(1)}, u32[]{:S(2)}, u32[]{:S(2)}) collective-permute-start(f32[2,32,256]{2,1,0:T(8,128)S(1)} %get-tuple-element.48), channel_id=1, source_target_pairs={{0,2},{1,3},{2,0},{3,1},{4,6},{5,7},{6,4},{7,5},{8,10},{9,11},{10,... | collective-permute-start | bytes 196616 | tf_op jit(solution)/shard_map/ppermute | solution.py:15
  55.3 5.7 %collective-permute-start.5 = (f32[2,32,256]{2,1,0:T(8,128)S(1)}, f32[2,32,256]{2,1,0:T(8,128)S(1)}, u32[]{:S(2)}, u32[]{:S(2)}) collective-permute-start(f32[2,32,256]{2,1,0:T(8,128)S(1)} %get-tuple-element.47), channel_id=1, source_target_pairs={{0,4},{1,5},{2,6},{3,7},{4,0},{5,1},{6,2},{7,3},{8,12},{9,13},{10,... | collective-permute-start | bytes 196616 | tf_op jit(solution)/shard_map/ppermute | solution.py:15
  56.8 5.5 %collective-permute-start.6 = (f32[2,32,256]{2,1,0:T(8,128)S(1)}, f32[2,32,256]{2,1,0:T(8,128)S(1)}, u32[]{:S(2)}, u32[]{:S(2)}) collective-permute-start(f32[2,32,256]{2,1,0:T(8,128)S(1)} %get-tuple-element.46), channel_id=1, source_target_pairs={{0,6},{1,7},{2,4},{3,5},{4,2},{5,3},{6,0},{7,1},{8,14},{9,15},{10,... | collective-permute-start | bytes 196616 | tf_op jit(solution)/shard_map/ppermute | solution.py:15
  57.4 4.9 %collective-permute-start.11 = (f32[2,32,256]{2,1,0:T(8,128)S(1)}, f32[2,32,256]{2,1,0:T(8,128)S(1)}, u32[]{:S(2)}, u32[]{:S(2)}) collective-permute-start(f32[2,32,256]{2,1,0:T(8,128)S(1)} %get-tuple-element.44), channel_id=1, source_target_pairs={{0,2},{1,3},{2,0},{3,1},{4,6},{5,7},{6,4},{7,5},{8,10},{9,11},{10,... | collective-permute-start | bytes 196616 | tf_op jit(solution)/shard_map/ppermute | solution.py:15
  58.9 5.0 %collective-permute-start.12 = (f32[2,32,256]{2,1,0:T(8,128)S(1)}, f32[2,32,256]{2,1,0:T(8,128)S(1)}, u32[]{:S(2)}, u32[]{:S(2)}) collective-permute-start(f32[2,32,256]{2,1,0:T(8,128)S(1)} %get-tuple-element.43), channel_id=1, source_target_pairs={{0,4},{1,5},{2,6},{3,7},{4,0},{5,1},{6,2},{7,3},{8,12},{9,13},{10,... | collective-permute-start | bytes 196616 | tf_op jit(solution)/shard_map/ppermute | solution.py:15
  60.5 5.2 %collective-permute-start.13 = (f32[2,32,256]{2,1,0:T(8,128)S(1)}, f32[2,32,256]{2,1,0:T(8,128)S(1)}, u32[]{:S(2)}, u32[]{:S(2)}) collective-permute-start(f32[2,32,256]{2,1,0:T(8,128)S(1)} %get-tuple-element.42), channel_id=1, source_target_pairs={{0,6},{1,7},{2,4},{3,5},{4,2},{5,3},{6,0},{7,1},{8,14},{9,15},{10,... | collective-permute-start | bytes 196616 | tf_op jit(solution)/shard_map/ppermute | solution.py:15
  66.3 4.9 %collective-permute-start.14 = (f32[2,32,128]{2,1,0:T(8,128)S(1)}, f32[2,32,128]{2,1,0:T(8,128)S(1)}, u32[]{:S(2)}, u32[]{:S(2)}) collective-permute-start(f32[2,32,128]{2,1,0:T(8,128)S(1)} %get-tuple-element.20), channel_id=1, source_target_pairs={{0,8},{8,0},{16,24},{24,16},{1,9},{9,1},{17,25},{25,17},{2,10},{10... | collective-permute-start | bytes 98312 | tf_op jit(solution)/shard_map/ppermute | solution.py:15
  68.6 2.5 %copy-start.4 = (s32[4,2]{0,1:T(2,128)S(1)}, s32[4,2]{0,1:T(2,128)}, u32[]{:S(2)}) copy-start(s32[4,2]{0,1:T(2,128)} %param.7) | copy-start | bytes 100
  68.6 5.0 %collective-permute-start.15 = (f32[2,32,128]{2,1,0:T(8,128)S(1)}, f32[2,32,128]{2,1,0:T(8,128)S(1)}, u32[]{:S(2)}, u32[]{:S(2)}) collective-permute-start(f32[2,32,128]{2,1,0:T(8,128)S(1)} %get-tuple-element.21), channel_id=1, source_target_pairs={{0,16},{8,24},{16,0},{24,8},{1,17},{9,25},{17,1},{25,9},{2,18},{10... | collective-permute-start | bytes 98312 | tf_op jit(solution)/shard_map/ppermute | solution.py:15
  69.7 5.7 %collective-permute-start.16 = (f32[2,32,128]{2,1,0:T(8,128)S(1)}, f32[2,32,128]{2,1,0:T(8,128)S(1)}, u32[]{:S(2)}, u32[]{:S(2)}) collective-permute-start(f32[2,32,128]{2,1,0:T(8,128)S(1)} %get-tuple-element.22), channel_id=1, source_target_pairs={{0,24},{8,16},{16,8},{24,0},{1,25},{9,17},{17,9},{25,1},{2,26},{10... | collective-permute-start | bytes 98312 | tf_op jit(solution)/shard_map/ppermute | solution.py:15

commit v3 on v0

v3 whole, which is shorter than its diff:
```python
import functools
import math

import jax
import jax.numpy as jnp
from jax import lax
from jax.experimental import pallas as pl
from jax.experimental.pallas import tpu as pltpu
from jax.sharding import PartitionSpec as P

LANES = 128
FIRST = 1


def swap(block, axis, mask):
    return lax.ppermute(block, axis, [(i, i ^ mask) for i in range(lax.axis_size(axis))])


def add_diagonals(block):
    rows, dates = block.shape
    row_id = lax.broadcasted_iota(jnp.int32, (rows, dates), 0)
    date_id = lax.broadcasted_iota(jnp.int32, (rows, dates), 1)
    least = jnp.minimum(row_id, date_id)
    offset = 1
    while offset < rows:
        moved = pltpu.roll(pltpu.roll(block, offset, 1), offset, 0)
        block = block + jnp.where(least >= offset, moved, 0.0)
        offset = offset * 2
    return block, row_id, date_id


def cut_kernel(width, planes, masks, rests, counts, *refs):
    arrays = refs[: len(rests)]
    *messages, sems = refs[len(rests) :]
    grid = arrays[0].shape[1]
    rest = grid - width * planes
    z = lax.axis_index("hrow")
    copies = []

    def copy(source, begin, size, goal, column):
        part = source.at[:, pl.ds(begin, size)]
        copies.append(pltpu.make_async_copy(part, goal.at[:, pl.ds(column, size)], sems.at[len(copies)]))
        copies[-1].start()

    for message, mask, count in zip(messages, masks, counts):
        begin = pl.multiple_of((z ^ mask) * width, LANES)
        column = 0
        for source, with_rest in zip(arrays[:count], rests):
            copy(source, begin, width, message, column)
            column = column + width
            if with_rest or mask == 0:
                copy(source, grid - rest, rest, message, column)
                column = column + rest
    for one in copies:
        one.wait()


def partial_sums(shocks, expect_ref, direct_ref, keep_ref, give_ref, responses, products):
    outputs, horizon = products.shape[:2]
    chips, planes, _, half, lanes = keep_ref.shape
    width = lanes // outputs
    step = min(horizon, 256)
    z = lax.axis_index("hrow")
    c = lax.axis_index("hcol")
    core = c % 2
    mine = pl.ds(pl.multiple_of(c * half, half), half)
    first = lax.broadcasted_iota(jnp.int32, (half, LANES), 1) == 0
    for index, shock in enumerate(shocks):
        for output in range(outputs):
            for start in range(0, horizon, step):
                products[output, start : start + step, :] = lax.dot_general(
                    responses[index, start : start + step, :],
                    expect_ref[output],
                    (((1,), (1,)), ((), ())),
                    preferred_element_type=jnp.float32,
                )
            added = jnp.where(first & (z == 0), direct_ref[shock * outputs + output], 0.0)
            products[output, mine, :LANES] = products[output, mine, :LANES] + added
        last = [None] * outputs
        for start in range(0, horizon, step):
            blocks = []
            for output in range(outputs):
                block, row_id, date_id = add_diagonals(products[output, start : start + step, :])
                if last[output] is not None:
                    spread = jnp.broadcast_to(last[output], block.shape)
                    moved = pltpu.roll(spread, 1, 1, stride=1, stride_axis=0)
                    block = block + jnp.where(date_id > row_id, moved, 0.0)
                last[output] = block[step - 1 :]
                blocks.append(block)
            for plane in range(planes):
                dates = slice(plane * width, (plane + 1) * width)
                both = jnp.concatenate([block[:, dates] for block in blocks], axis=1)
                for part in range(step // (2 * half)):
                    low = both[2 * part * half : (2 * part + 1) * half]
                    high = both[(2 * part + 1) * half : (2 * part + 2) * half]
                    chip = start // (2 * half) + part
                    keep_ref[chip, plane, index] = jnp.where(core == 0, low, high)
                    give_ref[chip, plane, index] = jnp.where(core == 0, high, low)


def place(z, mask, rows):
    return pl.ds(pl.multiple_of((z ^ mask) * rows, rows), rows)


def first_kernel(width, planes, shocks, direct_ref, *refs):
    messages = refs[:planes]
    expect_ref, keep_ref, give_ref, responses, products = refs[planes:]
    outputs, _, depth = expect_ref.shape
    rows = messages[0].shape[0]
    z = lax.axis_index("hrow")
    expect_ref[:, :, width:] = jnp.zeros_like(expect_ref[:, :, width:])
    for mask, ref in enumerate(messages):
        size = width if mask else depth
        for o in range(outputs):
            expect_ref[o, place(z, mask, rows), :size] = ref[:, o * size : (o + 1) * size]
        for index in range(len(shocks)):
            begin = outputs * size + index * depth
            responses[index, place(z, mask, rows), :] = ref[:, begin : begin + depth]
    partial_sums(shocks, expect_ref, direct_ref, keep_ref, give_ref, responses, products)


def next_kernel(begins, shocks, direct_ref, expect_ref, *refs):
    messages = refs[: len(begins)]
    keep_ref, give_ref, responses, products = refs[len(begins) :]
    rows, depth = messages[0].shape[0], responses.shape[2]
    z = lax.axis_index("hrow")
    for mask, (ref, begin) in enumerate(zip(messages, begins)):
        for index in range(len(shocks)):
            column = begin + index * depth
            responses[index, place(z, mask, rows), :] = ref[:, column : column + depth]
    partial_sums(shocks, expect_ref, direct_ref, keep_ref, give_ref, responses, products)


def size_of(leaf):
    shape = leaf.shape[:-1] + (-(-leaf.shape[-1] // LANES) * LANES,)
    return math.prod(shape) * leaf.dtype.itemsize


def call(kernel, name, out_shape, arrays, scratch=(), scalars=(), flops=0, source=pltpu.VMEM):
    held = sum(size_of(leaf) for leaf in jax.tree.leaves((arrays, out_shape)))
    taken = held + sum(size_of(leaf) for leaf in scratch if isinstance(leaf, jax.ShapeDtypeStruct) or jnp.issubdtype(leaf.dtype, jnp.number))
    return pl.pallas_call(
        kernel,
        name=name,
        out_shape=out_shape,
        in_specs=[pl.BlockSpec(memory_space=pltpu.SMEM)] * len(scalars)
        + [pl.BlockSpec(memory_space=source)] * len(arrays),
        out_specs=jax.tree.map(lambda _: pl.BlockSpec(memory_space=pltpu.VMEM), out_shape),
        scratch_shapes=scratch,
        cost_estimate=pl.CostEstimate(flops=flops, bytes_accessed=held, transcendentals=0),
        compiler_params=pltpu.CompilerParams(vmem_limit_bytes=taken * 3 // 2 + (4 << 20)),
    )(*scalars, *arrays)


def shards(expect, distrib, direct, pair_index):
    planes = lax.axis_size("hrow")
    col_devices = lax.axis_size("hcol")
    chips = col_devices // 2
    outputs, rows, grid = expect.shape
    shocks = distrib.shape[0]
    horizon = rows * planes
    cols = horizon // col_devices
    pairs = pair_index.shape[0]
    width = grid // LANES // planes * LANES
    rest = grid - width * planes
    depth = width + rest
    masks = range(1, planes)

    def cut(name, arrays, rests, sent, counts):
        shapes = [
            jax.ShapeDtypeStruct(
                (rows, sum(depth if with_rest or m == 0 else width for with_rest in rests[:count])),
                expect.dtype,
            )
            for m, count in zip(sent, counts)
        ]
        return call(
            functools.partial(cut_kernel, width, planes, sent, rests, counts),
            name,
            shapes,
            arrays,
            [pltpu.SemaphoreType.DMA((2 * sum(counts),))],
            source=pl.ANY,
        )

    def to_planes(messages, sent):
        return [swap(message, "hrow", m) if m else message for m, message in zip(sent, messages)]

    z = lax.axis_index("hrow")
    chip = lax.axis_index("hcol") // 2
    flat = direct.reshape(shocks * outputs, cols, 1)

    def kernel_call(kernel, name, group, arrays, extra=()):
        part = jax.ShapeDtypeStruct((chips, planes, len(group), cols, outputs * rows), jnp.float32)
        return call(
            kernel,
            name,
            (*extra, part, part),
            arrays,
            [
                pltpu.VMEM((len(group), horizon, depth), distrib.dtype),
                pltpu.VMEM((outputs, horizon, horizon), jnp.float32),
            ],
            flops=2 * len(group) * outputs * horizon * horizon * depth,
        )

    def scattered(values, own, axis, masks, scale, joined):
        def block(index):
            return jnp.concatenate(
                [lax.dynamic_index_in_dim(value, index, 0, False) for value in values], axis=joined
            )

        return functools.reduce(
            jnp.add, [block(own)] + [swap(block(own ^ m), axis, scale * m) for m in masks]
        )

    def over_cores(keep, give):
        return keep + swap(give, "hcol", 1)

    group = range(FIRST)
    rest_group = range(FIRST, shocks)
    arrays = [expect[o] for o in range(outputs)] + [distrib[s] for s in range(shocks)]
    rests = (False,) * outputs + (True,) * shocks
    some = outputs + len(group)
    counts = [len(arrays) if m < 2 else some for m in range(planes)]
    first = to_planes(cut("cut_0", arrays, rests, range(planes), counts), range(planes))
    if rest_group:
        later = cut("cut_1", arrays[some:], rests[some:], range(2, planes), [len(rest_group)] * (planes - 2))
        later = first[:2] + to_planes(later, range(2, planes))
    whole = jax.ShapeDtypeStruct((outputs, horizon, depth), expect.dtype)
    expect_all, *parts = kernel_call(
        functools.partial(first_kernel, width, planes, group), "partial_0", group, [flat] + first, [whole]
    )
    sums = [over_cores(*parts)]
    if rest_group:
        begins = [some * depth, outputs * width + len(group) * depth] + [0] * (planes - 2)
        parts = kernel_call(
            functools.partial(next_kernel, begins, rest_group),
            "partial_1",
            rest_group,
            [flat, expect_all] + later,
        )
        sums.append(over_cores(*parts))

    chip_sum = scattered(sums, chip, "hcol", range(1, chips), 2, 1)
    total = scattered([chip_sum], z, "hrow", range(1, planes), 1, 0)
    shock_of = pair_index[:, 0, None, None]
    output_of = pair_index[:, 1, None, None]
    picked = jnp.zeros((pairs, cols, rows), jnp.float32)
    for s in range(shocks):
        for o in range(outputs):
            one = total[s, :, o * rows : (o + 1) * rows]
            picked = jnp.where((shock_of == s) & (output_of == o), one, picked)
    return jnp.swapaxes(picked, 1, 2)


def solution(mesh):
    placed = (P(None, "hrow", "hcol"), P(None, "hrow", "hcol"), P(None, None, "hcol"), P())
    return jax.shard_map(
        shards, mesh=mesh, in_specs=placed, out_specs=P(None, "hrow", "hcol"), check_vma=False
    )
```

time: 196 us -> 65.3 us (0.33); the launches traced: 193 us -> 65.2 us
  waiting for transfers between devices: 130 us -> 40 us
  starting transfers between devices: 37.3 us -> 18.3 us
  between operations: 14.2 us -> 0.12 us
  Pallas kernels: 0 us -> 4.09 us
  local copies, waits for them, and re-layouts: 5.68 us -> 1.75 us
  matrix products: 3.11 us -> 0 us
    all_gather x1 -> x0, waiting for transfers between devices: 66.3 us -> none  [shards(): lax.all_gather(distrib, 'hrow', axis=1, tiled=True)]
    unnamed x3 -> x0, waiting for transfers between devices: 54 us -> none
    ppermute x10 -> x13, waiting for transfers between devices: 9.65 us -> 40 us  [swap(): lax.ppermute(block, axis, [(i, i ^ mask) for i in range(lax.axis_size(axi...]
    ppermute x10 -> x13, starting transfers between devices: 37.2 us -> 18.3 us  [swap(): lax.ppermute(block, axis, [(i, i ^ mask) for i in range(lax.axis_size(axi...]
    pallas_call x0 -> x4, Pallas kernels: none -> 4.09 us  [call(): pl.pallas_call(kernel, name=name, out_shape=out_shape, in_specs=[pl.Block...]
    dot_general x1 -> x0, matrix products: 3.11 us -> none  [shards(): jnp.einsum('orn,scn->osrc', expect, lax.all_gather(distrib, 'hrow', axis=...]
    unnamed x4, local copies, waits for them, and re-layouts: 2.11 us -> 0.01 us
  transfers between devices with their start and end apart: 12 -> 13, of which waited for: 10 -> 11; matrix products, arithmetic and copies ran while one was open for 2% -> 0% of each run, Pallas kernels for 0% -> 3%
where the time goes in v3:
time: 65.3 us; the launch traced here: 65.2 us
  waiting for transfers between devices  40 us (61%)
  starting transfers between devices  18.3 us (28%)
  Pallas kernels  4.09 us (6%)
  local copies, waits for them, and re-layouts  1.75 us (3%)
  other arithmetic  0.88 us (1%)
    ppermute x13, waiting for transfers between devices, swap(): lax.ppermute(block, axis, [(i, i ^ mask) for i in range(lax.axis_size(axi...  40 us
    ppermute x13, starting transfers between devices, swap(): lax.ppermute(block, axis, [(i, i ^ mask) for i in range(lax.axis_size(axi...  18.3 us
    pallas_call x4, Pallas kernels, call(): pl.pallas_call(kernel, name=name, out_shape=out_shape, in_specs=[pl.Block...  4.09 us
    squeeze x1, local copies, waits for them, and re-layouts, shards(): distrib[s]  1.49 us
  transfers between devices with their start and end apart: 13, of which 11 were waited for; matrix products, arithmetic and copies ran while one was open for 0% of the time, Pallas kernels for 3%

profile of v3, /device:TPU:0, one launch (start us, length us, event | category | flops | bytes accessed | tf_op | source)
XLA Modules:
  0.0 65.2 jit_solution(9362536895202470824)
XLA Ops:
  0.0 1.5 %slice_bitcast_fusion = (bf16[64,3200]{1,0:T(8,128)(2,1)S(1)}, bf16[64,3200]{1,0:T(8,128)(2,1)S(1)}, bf16[64,3200]{1,0:T(8,128)(2,1)S(1)}, bf16[64,3200]{1,0:T(8,128)(2,1)S(1)}) fusion(bf16[2,64,3200]{2,1,0:T(8,128)(2,1)} %param.5, bf16[2,64,3200]{2,1,0:T(8,128)(2,1)} %param.4), kind=kLoop, calls=%fused_computation | loop fusion | bytes 3276800 | tf_op jit(solution)/shard_map/squeeze | solution.py:222
  1.5 0.6 cut_0.1
  2.1 3.1 %collective-permute-start = (bf16[64,3328]{1,0:T(8,128)(2,1)S(1)}, bf16[64,3328]{1,0:T(8,128)(2,1)S(1)}, u32[]{:S(2)}, u32[]{:S(2)}) collective-permute-start(bf16[64,3328]{1,0:T(8,128)(2,1)S(1)} %get-tuple-element.17), channel_id=1, source_target_pairs={{0,8},{8,0},{16,24},{24,16},{1,9},{9,1},{17,25},{25,17},{2,10},{10... | collective-permute-start | bytes 1277960 | tf_op jit(solution)/shard_map/ppermute | solution.py:16
  5.1 2.6 %collective-permute-start.1 = (bf16[64,2432]{1,0:T(8,128)(2,1)S(1)}, bf16[64,2432]{1,0:T(8,128)(2,1)S(1)}, u32[]{:S(2)}, u32[]{:S(2)}) collective-permute-start(bf16[64,2432]{1,0:T(8,128)(2,1)S(1)} %get-tuple-element.18), channel_id=1, source_target_pairs={{0,16},{8,24},{16,0},{24,8},{1,17},{9,25},{17,1},{25,9},{2,18},{10... | collective-permute-start | bytes 933896 | tf_op jit(solution)/shard_map/ppermute | solution.py:16
  7.7 0.1 cut_1.1
  7.8 0.0 copy-start
  7.8 2.0 %collective-permute-start.4 = (bf16[64,896]{1,0:T(8,128)(2,1)S(1)}, bf16[64,896]{1,0:T(8,128)(2,1)S(1)}, u32[]{:S(2)}, u32[]{:S(2)}) collective-permute-start(bf16[64,896]{1,0:T(8,128)(2,1)S(1)} %get-tuple-element.23), channel_id=1, source_target_pairs={{0,16},{8,24},{16,0},{24,8},{1,17},{9,25},{17,1},{25,9},{2,18},{10... | collective-permute-start | bytes 344072 | tf_op jit(solution)/shard_map/ppermute | solution.py:16
  9.8 2.0 %collective-permute-start.5 = (bf16[64,896]{1,0:T(8,128)(2,1)S(1)}, bf16[64,896]{1,0:T(8,128)(2,1)S(1)}, u32[]{:S(2)}, u32[]{:S(2)}) collective-permute-start(bf16[64,896]{1,0:T(8,128)(2,1)S(1)} %get-tuple-element.24), channel_id=1, source_target_pairs={{0,24},{8,16},{16,8},{24,0},{1,25},{9,17},{17,9},{25,1},{2,26},{10... | collective-permute-start | bytes 344072 | tf_op jit(solution)/shard_map/ppermute | solution.py:16
  11.8 0.1 copy.5.direct_ref
  11.9 10.2 %collective-permute-done.1.refs_2_ = bf16[64,2432]{1,0:T(8,128)(2,1)S(1)} collective-permute-done((bf16[64,2432]{1,0:T(8,128)(2,1)S(1)}, bf16[64,2432]{1,0:T(8,128)(2,1)S(1)}, u32[]{:S(2)}, u32[]{:S(2)}) %collective-permute-start.1) | collective-permute-done | bytes 311328 | tf_op jit(solution)/shard_map/ppermute | solution.py:16
  22.1 9.7 %collective-permute-done.2.refs_3_ = bf16[64,2432]{1,0:T(8,128)(2,1)S(1)} collective-permute-done((bf16[64,2432]{1,0:T(8,128)(2,1)S(1)}, bf16[64,2432]{1,0:T(8,128)(2,1)S(1)}, u32[]{:S(2)}, u32[]{:S(2)}) %collective-permute-start.2) | collective-permute-done | bytes 311328 | tf_op jit(solution)/shard_map/ppermute | solution.py:16
  31.7 1.8 %partial_0.1 = (bf16[2,256,896]{2,1,0:T(8,128)(2,1)S(1)}, f32[4,4,1,32,128]{4,3,2,1,0:T(8,128)S(1)}, f32[4,4,1,32,128]{4,3,2,1,0:T(8,128)S(1)}) custom-call(f32[4,32,1]{2,1,0:T(8,128)S(1)} %copy.5.direct_ref, bf16[64,3584]{1,0:T(8,128)(2,1)S(1)} %get-tuple-element.16.refs_0_, bf16[64,3328]{1,0:T(8,128)(2,1)S(1)} %collective-permute-done.refs_1_, ...), custom_call_target="tpu_custom_call" | custom-call | flops 234881024 | bytes 3014656 | tf_op jit(solution)/shard_map/partial_0/pallas_call | solution.py:142
  33.5 10.0 %collective-permute-done.4.refs_2_ = bf16[64,896]{1,0:T(8,128)(2,1)S(1)} collective-permute-done((bf16[64,896]{1,0:T(8,128)(2,1)S(1)}, bf16[64,896]{1,0:T(8,128)(2,1)S(1)}, u32[]{:S(2)}, u32[]{:S(2)}) %collective-permute-start.4) | collective-permute-done | bytes 114720 | tf_op jit(solution)/shard_map/ppermute | solution.py:16
  43.5 1.7 %partial_1.1 = (f32[4,4,1,32,128]{4,3,2,1,0:T(8,128)S(1)}, f32[4,4,1,32,128]{4,3,2,1,0:T(8,128)S(1)}) custom-call(f32[4,32,1]{2,1,0:T(8,128)S(1)} %copy.5.direct_ref, bf16[2,256,896]{2,1,0:T(8,128)(2,1)S(1)} %get-tuple-element.22.expect_ref, bf16[64,3584]{1,0:T(8,128)(2,1)S(1)} %get-tuple-element.16.refs_0_, ...), custom_call_target="tpu_custom_call" | custom-call | flops 234881024 | bytes 2621440 | tf_op jit(solution)/shard_map/partial_1/pallas_call | solution.py:142
  45.2 0.1 collective-permute-start.6
  45.3 0.5 collective-permute-start.3
  45.8 1.0 %collective-permute-done.6 = f32[4,4,1,32,128]{4,3,2,1,0:T(8,128)S(1)} collective-permute-done((f32[4,4,1,32,128]{4,3,2,1,0:T(8,128)S(1)}, f32[4,4,1,32,128]{4,3,2,1,0:T(8,128)S(1)}, u32[]{:S(2)}, u32[]{:S(2)}) %collective-permute-start.6) | collective-permute-done | bytes 262176 | tf_op jit(solution)/shard_map/ppermute | solution.py:16
  46.9 0.3 collective-permute-done.3
  47.3 2.5 %collective-permute-start.9 = (f32[4,2,32,128]{3,2,0,1:T(8,128)S(1)}, f32[4,2,32,128]{3,2,0,1:T(8,128)S(1)}, u32[]{:S(2)}, u32[]{:S(2)}) collective-permute-start(f32[4,2,32,128]{3,2,0,1:T(8,128)S(1)} %pad_maximum_fusion.2), channel_id=1, source_target_pairs={{0,6},{1,7},{2,4},{3,5},{4,2},{5,3},{6,0},{7,1},{8,14},{9,15},{10,... | collective-permute-start | bytes 393224 | tf_op jit(solution)/shard_map/ppermute | solution.py:16
  49.8 0.6 collective-permute-start.8
  50.4 0.6 collective-permute-start.7
  51.0 2.9 %collective-permute-done.9 = f32[4,2,32,128]{3,2,0,1:T(8,128)S(1)} collective-permute-done((f32[4,2,32,128]{3,2,0,1:T(8,128)S(1)}, f32[4,2,32,128]{3,2,0,1:T(8,128)S(1)}, u32[]{:S(2)}, u32[]{:S(2)}) %collective-permute-start.9) | collective-permute-done | bytes 131104 | tf_op jit(solution)/shard_map/ppermute | solution.py:16
  53.9 2.7 %collective-permute-done.8 = f32[4,2,32,128]{3,2,0,1:T(8,128)S(1)} collective-permute-done((f32[4,2,32,128]{3,2,0,1:T(8,128)S(1)}, f32[4,2,32,128]{3,2,0,1:T(8,128)S(1)}, u32[]{:S(2)}, u32[]{:S(2)}) %collective-permute-start.8) | collective-permute-done | bytes 131104 | tf_op jit(solution)/shard_map/ppermute | solution.py:16
  56.6 0.1 collective-permute-done.7
  56.8 2.5 %collective-permute-start.12 = (f32[2,32,128]{2,1,0:T(8,128)S(1)}, f32[2,32,128]{2,1,0:T(8,128)S(1)}, u32[]{:S(2)}, u32[]{:S(2)}) collective-permute-start(f32[2,32,128]{2,1,0:T(8,128)S(1)} %get-tuple-element.40), channel_id=1, source_target_pairs={{0,24},{8,16},{16,8},{24,0},{1,25},{9,17},{17,9},{25,1},{2,26},{10... | collective-permute-start | bytes 98312 | tf_op jit(solution)/shard_map/ppermute | solution.py:16
  59.3 0.8 %collective-permute-start.11 = (f32[2,32,128]{2,1,0:T(8,128)S(1)}, f32[2,32,128]{2,1,0:T(8,128)S(1)}, u32[]{:S(2)}, u32[]{:S(2)}) collective-permute-start(f32[2,32,128]{2,1,0:T(8,128)S(1)} %get-tuple-element.41), channel_id=1, source_target_pairs={{0,16},{8,24},{16,0},{24,8},{1,17},{9,25},{17,1},{25,9},{2,18},{10... | collective-permute-start | bytes 98312 | tf_op jit(solution)/shard_map/ppermute | solution.py:16
  60.1 1.1 %collective-permute-start.10 = (f32[2,32,128]{2,1,0:T(8,128)S(1)}, f32[2,32,128]{2,1,0:T(8,128)S(1)}, u32[]{:S(2)}, u32[]{:S(2)}) collective-permute-start(f32[2,32,128]{2,1,0:T(8,128)S(1)} %get-tuple-element.39), channel_id=1, source_target_pairs={{0,8},{8,0},{16,24},{24,16},{1,9},{9,1},{17,25},{25,17},{2,10},{10... | collective-permute-start | bytes 98312 | tf_op jit(solution)/shard_map/ppermute | solution.py:16
  61.2 1.4 %collective-permute-done.12 = f32[2,32,128]{2,1,0:T(8,128)S(1)} collective-permute-done((f32[2,32,128]{2,1,0:T(8,128)S(1)}, f32[2,32,128]{2,1,0:T(8,128)S(1)}, u32[]{:S(2)}, u32[]{:S(2)}) %collective-permute-start.12) | collective-permute-done | bytes 32800 | tf_op jit(solution)/shard_map/ppermute | solution.py:16
  62.6 1.6 %collective-permute-done.11 = f32[2,32,128]{2,1,0:T(8,128)S(1)} collective-permute-done((f32[2,32,128]{2,1,0:T(8,128)S(1)}, f32[2,32,128]{2,1,0:T(8,128)S(1)}, u32[]{:S(2)}, u32[]{:S(2)}) %collective-permute-start.11) | collective-permute-done | bytes 32800 | tf_op jit(solution)/shard_map/ppermute | solution.py:16
  64.2 0.1 collective-permute-done.10
  64.4 0.1 slice_bitcast_fusion.7
  64.4 0.7 %select_select_fusion = f32[4,64,32]{1,2,0:T(8,128)} fusion(f32[64,32]{0,1:T(8,128)S(1)} %get-tuple-element.43, f32[64,32]{0,1:T(8,128)S(1)} %get-tuple-element.44, f32[64,32]{0,1:T(8,128)S(1)} %get-tuple-element.45, f32[64,32]{0,1:T(8,128)S(1)} %get-tuple-element.42, pred[4]{0:T(512)(128)(4,1)S(1)} %get-tuple-element.47, ...), kind=kLoop, calls=%fused_computation.10 | loop fusion | flops 32768 | bytes 65552 | tf_op jit(solution)/shard_map/jit(_where)/select_n | solution.py:253
  (17 shorter events, 0.2 us)
Async XLA Ops:
  2.1 29.7 %collective-permute-start = (bf16[64,3328]{1,0:T(8,128)(2,1)S(1)}, bf16[64,3328]{1,0:T(8,128)(2,1)S(1)}, u32[]{:S(2)}, u32[]{:S(2)}) collective-permute-start(bf16[64,3328]{1,0:T(8,128)(2,1)S(1)} %get-tuple-element.17), channel_id=1, source_target_pairs={{0,8},{8,0},{16,24},{24,16},{1,9},{9,1},{17,25},{25,17},{2,10},{10... | collective-permute-start | bytes 1277960 | tf_op jit(solution)/shard_map/ppermute | solution.py:16
  5.1 16.9 %collective-permute-start.1 = (bf16[64,2432]{1,0:T(8,128)(2,1)S(1)}, bf16[64,2432]{1,0:T(8,128)(2,1)S(1)}, u32[]{:S(2)}, u32[]{:S(2)}) collective-permute-start(bf16[64,2432]{1,0:T(8,128)(2,1)S(1)} %get-tuple-element.18), channel_id=1, source_target_pairs={{0,16},{8,24},{16,0},{24,8},{1,17},{9,25},{17,1},{25,9},{2,18},{10... | collective-permute-start | bytes 933896 | tf_op jit(solution)/shard_map/ppermute | solution.py:16
  7.7 24.0 %collective-permute-start.2 = (bf16[64,2432]{1,0:T(8,128)(2,1)S(1)}, bf16[64,2432]{1,0:T(8,128)(2,1)S(1)}, u32[]{:S(2)}, u32[]{:S(2)}) collective-permute-start(bf16[64,2432]{1,0:T(8,128)(2,1)S(1)} %get-tuple-element.19), channel_id=1, source_target_pairs={{0,24},{8,16},{16,8},{24,0},{1,25},{9,17},{17,9},{25,1},{2,26},{10... | collective-permute-start | bytes 933896 | tf_op jit(solution)/shard_map/ppermute | solution.py:16
  7.8 4.0 %copy-start = (f32[2,2,32]{2,1,0:T(2,128)S(1)}, f32[2,2,32]{2,1,0:T(2,128)}, u32[]{:S(2)}) copy-start(f32[2,2,32]{2,1,0:T(2,128)} %param.6) | copy-start | bytes 1540
  7.8 35.7 %collective-permute-start.4 = (bf16[64,896]{1,0:T(8,128)(2,1)S(1)}, bf16[64,896]{1,0:T(8,128)(2,1)S(1)}, u32[]{:S(2)}, u32[]{:S(2)}) collective-permute-start(bf16[64,896]{1,0:T(8,128)(2,1)S(1)} %get-tuple-element.23), channel_id=1, source_target_pairs={{0,16},{8,24},{16,0},{24,8},{1,17},{9,25},{17,1},{25,9},{2,18},{10... | collective-permute-start | bytes 344072 | tf_op jit(solution)/shard_map/ppermute | solution.py:16
  9.8 33.7 %collective-permute-start.5 = (bf16[64,896]{1,0:T(8,128)(2,1)S(1)}, bf16[64,896]{1,0:T(8,128)(2,1)S(1)}, u32[]{:S(2)}, u32[]{:S(2)}) collective-permute-start(bf16[64,896]{1,0:T(8,128)(2,1)S(1)} %get-tuple-element.24), channel_id=1, source_target_pairs={{0,24},{8,16},{16,8},{24,0},{1,25},{9,17},{17,9},{25,1},{2,26},{10... | collective-permute-start | bytes 344072 | tf_op jit(solution)/shard_map/ppermute | solution.py:16
  45.2 1.6 %collective-permute-start.6 = (f32[4,4,1,32,128]{4,3,2,1,0:T(8,128)S(1)}, f32[4,4,1,32,128]{4,3,2,1,0:T(8,128)S(1)}, u32[]{:S(2)}, u32[]{:S(2)}) collective-permute-start(f32[4,4,1,32,128]{4,3,2,1,0:T(8,128)S(1)} %get-tuple-element.26), channel_id=1, source_target_pairs={{0,1},{1,0},{2,3},{3,2},{4,5},{5,4},{6,7},{7,6},{8,9},{9,8},{10,11... | collective-permute-start | bytes 786440 | tf_op jit(solution)/shard_map/ppermute | solution.py:16
  45.3 1.9 %collective-permute-start.3 = (f32[4,4,1,32,128]{4,3,2,1,0:T(8,128)S(1)}, f32[4,4,1,32,128]{4,3,2,1,0:T(8,128)S(1)}, u32[]{:S(2)}, u32[]{:S(2)}) collective-permute-start(f32[4,4,1,32,128]{4,3,2,1,0:T(8,128)S(1)} %get-tuple-element.21), channel_id=1, source_target_pairs={{0,1},{1,0},{2,3},{3,2},{4,5},{5,4},{6,7},{7,6},{8,9},{9,8},{10,11... | collective-permute-start | bytes 786440 | tf_op jit(solution)/shard_map/ppermute | solution.py:16
  47.3 6.6 %collective-permute-start.9 = (f32[4,2,32,128]{3,2,0,1:T(8,128)S(1)}, f32[4,2,32,128]{3,2,0,1:T(8,128)S(1)}, u32[]{:S(2)}, u32[]{:S(2)}) collective-permute-start(f32[4,2,32,128]{3,2,0,1:T(8,128)S(1)} %pad_maximum_fusion.2), channel_id=1, source_target_pairs={{0,6},{1,7},{2,4},{3,5},{4,2},{5,3},{6,0},{7,1},{8,14},{9,15},{10,... | collective-permute-start | bytes 393224 | tf_op jit(solution)/shard_map/ppermute | solution.py:16
  49.8 6.8 %collective-permute-start.8 = (f32[4,2,32,128]{3,2,0,1:T(8,128)S(1)}, f32[4,2,32,128]{3,2,0,1:T(8,128)S(1)}, u32[]{:S(2)}, u32[]{:S(2)}) collective-permute-start(f32[4,2,32,128]{3,2,0,1:T(8,128)S(1)} %pad_maximum_fusion.1), channel_id=1, source_target_pairs={{0,4},{1,5},{2,6},{3,7},{4,0},{5,1},{6,2},{7,3},{8,12},{9,13},{10,... | collective-permute-start | bytes 393224 | tf_op jit(solution)/shard_map/ppermute | solution.py:16
  50.4 6.3 %collective-permute-start.7 = (f32[4,2,32,128]{3,2,0,1:T(8,128)S(1)}, f32[4,2,32,128]{3,2,0,1:T(8,128)S(1)}, u32[]{:S(2)}, u32[]{:S(2)}) collective-permute-start(f32[4,2,32,128]{3,2,0,1:T(8,128)S(1)} %pad_maximum_fusion), channel_id=1, source_target_pairs={{0,2},{1,3},{2,0},{3,1},{4,6},{5,7},{6,4},{7,5},{8,10},{9,11},{10,... | collective-permute-start | bytes 393224 | tf_op jit(solution)/shard_map/ppermute | solution.py:16
  56.8 5.9 %collective-permute-start.12 = (f32[2,32,128]{2,1,0:T(8,128)S(1)}, f32[2,32,128]{2,1,0:T(8,128)S(1)}, u32[]{:S(2)}, u32[]{:S(2)}) collective-permute-start(f32[2,32,128]{2,1,0:T(8,128)S(1)} %get-tuple-element.40), channel_id=1, source_target_pairs={{0,24},{8,16},{16,8},{24,0},{1,25},{9,17},{17,9},{25,1},{2,26},{10... | collective-permute-start | bytes 98312 | tf_op jit(solution)/shard_map/ppermute | solution.py:16
  59.3 1.9 %copy-start.1 = (s32[4,2]{0,1:T(2,128)S(1)}, s32[4,2]{0,1:T(2,128)}, u32[]{:S(2)}) copy-start(s32[4,2]{0,1:T(2,128)} %param.7) | copy-start | bytes 100
  59.3 4.9 %collective-permute-start.11 = (f32[2,32,128]{2,1,0:T(8,128)S(1)}, f32[2,32,128]{2,1,0:T(8,128)S(1)}, u32[]{:S(2)}, u32[]{:S(2)}) collective-permute-start(f32[2,32,128]{2,1,0:T(8,128)S(1)} %get-tuple-element.41), channel_id=1, source_target_pairs={{0,16},{8,24},{16,0},{24,8},{1,17},{9,25},{17,1},{25,9},{2,18},{10... | collective-permute-start | bytes 98312 | tf_op jit(solution)/shard_map/ppermute | solution.py:16
  60.1 4.3 %collective-permute-start.10 = (f32[2,32,128]{2,1,0:T(8,128)S(1)}, f32[2,32,128]{2,1,0:T(8,128)S(1)}, u32[]{:S(2)}, u32[]{:S(2)}) collective-permute-start(f32[2,32,128]{2,1,0:T(8,128)S(1)} %get-tuple-element.39), channel_id=1, source_target_pairs={{0,8},{8,0},{16,24},{24,16},{1,9},{9,1},{17,25},{25,17},{2,10},{10... | collective-permute-start | bytes 98312 | tf_op jit(solution)/shard_map/ppermute | solution.py:16

commit v4 on v3

--- a/solution.py
+++ b/solution.py
@@ -29,11 +29,17 @@
     return block, row_id, date_id
 
 
-def cut_kernel(width, planes, masks, rests, counts, *refs):
-    arrays = refs[: len(rests)]
-    *messages, sems = refs[len(rests) :]
-    grid = arrays[0].shape[1]
+def packed_share(planes, arrays, rest):
+    share = rest // planes
+    return share if rest == LANES and share * arrays <= LANES and share * planes == rest else 0
+
+
+def cut_kernel(width, planes, masks, counts, tail_at, *refs):
+    arrays = list(refs[: len(refs) - len(masks) - 1])
+    *messages, sems = refs[len(arrays) :]
+    rows, grid = arrays[0].shape
     rest = grid - width * planes
+    share = packed_share(planes, len(arrays), rest)
     z = lax.axis_index("hrow")
     copies = []
 
@@ -44,13 +50,22 @@
 
     for message, mask, count in zip(messages, masks, counts):
         begin = pl.multiple_of((z ^ mask) * width, LANES)
-        column = 0
-        for source, with_rest in zip(arrays[:count], rests):
-            copy(source, begin, width, message, column)
-            column = column + width
-            if with_rest or mask == 0:
-                copy(source, grid - rest, rest, message, column)
-                column = column + rest
+        for index, source in enumerate(arrays[:count]):
+            copy(source, begin, width, message, index * width)
+        if tail_at is not None and not share:
+            last = arrays[tail_at:] + (arrays[:tail_at] if mask == 0 else [])
+            for index, source in enumerate(last):
+                copy(source, grid - rest, rest, message, count * width + index * rest)
+    if tail_at is not None and share:
+        spot = lax.broadcasted_iota(jnp.int32, (rows, LANES), 1)
+        tails = [source[:, grid - rest :].astype(jnp.float32) for source in arrays]
+        for message, mask, count in zip(messages, masks, counts):
+            tile = jnp.zeros((rows, LANES), jnp.float32)
+            for index, tail in enumerate(tails):
+                shift = lax.rem(index * share + LANES - (z ^ mask) * share, LANES)
+                inside = (spot >= index * share) & (spot < (index + 1) * share)
+                tile = jnp.where(inside, pltpu.roll(tail, shift, 1), tile)
+            message[:, count * width : count * width + LANES] = tile.astype(message.dtype)
     for one in copies:
         one.wait()
 
@@ -102,32 +117,56 @@
     return pl.ds(pl.multiple_of((z ^ mask) * rows, rows), rows)
 
 
-def first_kernel(width, planes, shocks, direct_ref, *refs):
+def first_kernel(width, planes, counts, shocks, direct_ref, *refs):
     messages = refs[:planes]
-    expect_ref, keep_ref, give_ref, responses, products = refs[planes:]
-    outputs, _, depth = expect_ref.shape
+    expect_ref, tails_ref, keep_ref, give_ref, responses, products = refs[planes:]
+    outputs = expect_ref.shape[0]
     rows = messages[0].shape[0]
-    z = lax.axis_index("hrow")
-    expect_ref[:, :, width:] = jnp.zeros_like(expect_ref[:, :, width:])
-    for mask, ref in enumerate(messages):
-        size = width if mask else depth
+    rest = tails_ref.shape[2]
+    arrays = outputs + tails_ref.shape[0]
+    share = packed_share(planes, arrays, rest)
+    z = lax.axis_index("hrow")
+    inside = lax.broadcasted_iota(jnp.int32, (rows, rest), 1) < share
+    if not share:
+        expect_ref[:, :, width:] = jnp.zeros_like(expect_ref[:, :, width:])
+    for mask, (ref, count) in enumerate(zip(messages, counts)):
+        spot = place(z, mask, rows)
         for o in range(outputs):
-            expect_ref[o, place(z, mask, rows), :size] = ref[:, o * size : (o + 1) * size]
+            expect_ref[o, spot, :width] = ref[:, o * width : (o + 1) * width]
         for index in range(len(shocks)):
-            begin = outputs * size + index * depth
-            responses[index, place(z, mask, rows), :] = ref[:, begin : begin + depth]
+            responses[index, spot, :width] = ref[:, (outputs + index) * width : (outputs + index + 1) * width]
+        tail = count * width
+        if share:
+            tile = ref[:, tail : tail + rest].astype(jnp.float32)
+            for index in range(arrays):
+                moved = tile if index == 0 else pltpu.roll(tile, LANES - index * share, 1)
+                moved = jnp.where(inside, moved, 0.0).astype(ref.dtype)
+                if index < outputs:
+                    expect_ref[index, spot, width:] = moved
+                else:
+                    tails_ref[index - outputs, spot, :] = moved
+        else:
+            for index in range(arrays if mask == 0 else arrays - outputs):
+                moved = ref[:, tail + index * rest : tail + (index + 1) * rest]
+                if index < arrays - outputs:
+                    tails_ref[index, spot, :] = moved
+                else:
+                    expect_ref[index - arrays + outputs, spot, width:] = moved
+    for index, shock in enumerate(shocks):
+        responses[index, :, width:] = tails_ref[shock]
     partial_sums(shocks, expect_ref, direct_ref, keep_ref, give_ref, responses, products)
 
 
-def next_kernel(begins, shocks, direct_ref, expect_ref, *refs):
+def next_kernel(width, begins, shocks, direct_ref, expect_ref, tails_ref, *refs):
     messages = refs[: len(begins)]
     keep_ref, give_ref, responses, products = refs[len(begins) :]
-    rows, depth = messages[0].shape[0], responses.shape[2]
-    z = lax.axis_index("hrow")
-    for mask, (ref, begin) in enumerate(zip(messages, begins)):
-        for index in range(len(shocks)):
-            column = begin + index * depth
-            responses[index, place(z, mask, rows), :] = ref[:, column : column + depth]
+    rows = messages[0].shape[0]
+    z = lax.axis_index("hrow")
+    for index, shock in enumerate(shocks):
+        for mask, (ref, begin) in enumerate(zip(messages, begins)):
+            column = begin + index * width
+            responses[index, place(z, mask, rows), :width] = ref[:, column : column + width]
+        responses[index, :, width:] = tails_ref[shock]
     partial_sums(shocks, expect_ref, direct_ref, keep_ref, give_ref, responses, products)
 
 
@@ -136,7 +175,7 @@
     return math.prod(shape) * leaf.dtype.itemsize
 
 
-def call(kernel, name, out_shape, arrays, scratch=(), scalars=(), flops=0, source=pltpu.VMEM):
+def call(kernel, name, out_shape, arrays, scratch=(), scalars=(), flops=0):
     held = sum(size_of(leaf) for leaf in jax.tree.leaves((arrays, out_shape)))
     taken = held + sum(size_of(leaf) for leaf in scratch if isinstance(leaf, jax.ShapeDtypeStruct) or jnp.issubdtype(leaf.dtype, jnp.number))
     return pl.pallas_call(
@@ -144,7 +183,7 @@
         name=name,
         out_shape=out_shape,
         in_specs=[pl.BlockSpec(memory_space=pltpu.SMEM)] * len(scalars)
-        + [pl.BlockSpec(memory_space=source)] * len(arrays),
+        + [pl.BlockSpec(memory_space=pltpu.VMEM)] * len(arrays),
         out_specs=jax.tree.map(lambda _: pl.BlockSpec(memory_space=pltpu.VMEM), out_shape),
         scratch_shapes=scratch,
         cost_estimate=pl.CostEstimate(flops=flops, bytes_accessed=held, transcendentals=0),
@@ -164,23 +203,20 @@
     width = grid // LANES // planes * LANES
     rest = grid - width * planes
     depth = width + rest
-    masks = range(1, planes)
-
-    def cut(name, arrays, rests, sent, counts):
-        shapes = [
-            jax.ShapeDtypeStruct(
-                (rows, sum(depth if with_rest or m == 0 else width for with_rest in rests[:count])),
-                expect.dtype,
-            )
-            for m, count in zip(sent, counts)
-        ]
+    share = packed_share(planes, outputs + shocks, rest)
+
+    def cut(name, arrays, sent, counts, tail_at=None):
+        def columns(m, count):
+            if tail_at is None or share:
+                return count * width + (0 if tail_at is None else LANES)
+            return count * width + (len(arrays) if m == 0 else len(arrays) - tail_at) * rest
+
         return call(
-            functools.partial(cut_kernel, width, planes, sent, rests, counts),
+            functools.partial(cut_kernel, width, planes, sent, counts, tail_at),
             name,
-            shapes,
+            [jax.ShapeDtypeStruct((rows, columns(m, count)), expect.dtype) for m, count in zip(sent, counts)],
             arrays,
-            [pltpu.SemaphoreType.DMA((2 * sum(counts),))],
-            source=pl.ANY,
+            [pltpu.SemaphoreType.DMA((sum(counts) + len(sent) * len(arrays),))],
         )
 
     def to_planes(messages, sent):
@@ -220,30 +256,35 @@
     group = range(FIRST)
     rest_group = range(FIRST, shocks)
     arrays = [expect[o] for o in range(outputs)] + [distrib[s] for s in range(shocks)]
-    rests = (False,) * outputs + (True,) * shocks
     some = outputs + len(group)
     counts = [len(arrays) if m < 2 else some for m in range(planes)]
-    first = to_planes(cut("cut_0", arrays, rests, range(planes), counts), range(planes))
+    first = to_planes(cut("cut_0", arrays, range(planes), counts, outputs), range(planes))
     if rest_group:
-        later = cut("cut_1", arrays[some:], rests[some:], range(2, planes), [len(rest_group)] * (planes - 2))
+        later = cut("cut_1", arrays[some:], range(2, planes), [len(rest_group)] * (planes - 2))
         later = first[:2] + to_planes(later, range(2, planes))
-    whole = jax.ShapeDtypeStruct((outputs, horizon, depth), expect.dtype)
-    expect_all, *parts = kernel_call(
-        functools.partial(first_kernel, width, planes, group), "partial_0", group, [flat] + first, [whole]
+    expect_all, tails, *parts = kernel_call(
+        functools.partial(first_kernel, width, planes, counts, group),
+        "partial_0",
+        group,
+        [flat] + first,
+        [
+            jax.ShapeDtypeStruct((outputs, horizon, depth), expect.dtype),
+            jax.ShapeDtypeStruct((shocks, horizon, rest), distrib.dtype),
+        ],
     )
     sums = [over_cores(*parts)]
     if rest_group:
-        begins = [some * depth, outputs * width + len(group) * depth] + [0] * (planes - 2)
+        begins = [some * width] * 2 + [0] * (planes - 2)
         parts = kernel_call(
-            functools.partial(next_kernel, begins, rest_group),
+            functools.partial(next_kernel, width, begins, rest_group),
             "partial_1",
             rest_group,
-            [flat, expect_all] + later,
+            [flat, expect_all, tails] + later,
         )
         sums.append(over_cores(*parts))
 
-    chip_sum = scattered(sums, chip, "hcol", range(1, chips), 2, 1)
-    total = scattered([chip_sum], z, "hrow", range(1, planes), 1, 0)
+    chip_sum = scattered(sums, chip, "hcol", range(chips - 1, 0, -1), 2, 1)
+    total = scattered([chip_sum], z, "hrow", [planes - 1, *range(1, planes - 1)], 1, 0)
     shock_of = pair_index[:, 0, None, None]
     output_of = pair_index[:, 1, None, None]
     picked = jnp.zeros((pairs, cols, rows), jnp.float32)

time: 65.3 us -> 63.9 us (0.979)
  waiting for transfers between devices: 40 us -> 38.8 us
    ppermute x13, waiting for transfers between devices: 40 us -> 38.8 us  [swap(): lax.ppermute(block, axis, [(i, i ^ mask) for i in range(lax.axis_size(axi...]
  transfers between devices with their start and end apart: 13 -> 13, of which waited for: 11 -> 9; matrix products, arithmetic and copies ran while one was open for 0% -> 0% of each run, Pallas kernels for 3% -> 6%
where the time goes in v4:
time: 63.9 us; the launch traced here: 63.8 us
  waiting for transfers between devices  38.8 us (61%)
  starting transfers between devices  17.9 us (28%)
  Pallas kernels  4.28 us (7%)
  local copies, waits for them, and re-layouts  1.75 us (3%)
  other arithmetic  0.88 us (1%)
    ppermute x13, waiting for transfers between devices, swap(): lax.ppermute(block, axis, [(i, i ^ mask) for i in range(lax.axis_size(axi...  38.8 us
    ppermute x13, starting transfers between devices, swap(): lax.ppermute(block, axis, [(i, i ^ mask) for i in range(lax.axis_size(axi...  17.9 us
    pallas_call x4, Pallas kernels, call(): pl.pallas_call(kernel, name=name, out_shape=out_shape, in_specs=[pl.Block...  4.28 us
    squeeze x1, local copies, waits for them, and re-layouts, shards(): distrib[s]  1.49 us
  transfers between devices with their start and end apart: 13, of which 9 were waited for; matrix products, arithmetic and copies ran while one was open for 0% of the time, Pallas kernels for 6%

profile of v4, /device:TPU:0, one launch (start us, length us, event | category | flops | bytes accessed | tf_op | source)
XLA Modules:
  0.0 63.8 jit_solution(17653448153468037383)
XLA Ops:
  0.0 1.5 %slice_bitcast_fusion = (bf16[64,3200]{1,0:T(8,128)(2,1)S(1)}, bf16[64,3200]{1,0:T(8,128)(2,1)S(1)}, bf16[64,3200]{1,0:T(8,128)(2,1)S(1)}, bf16[64,3200]{1,0:T(8,128)(2,1)S(1)}) fusion(bf16[2,64,3200]{2,1,0:T(8,128)(2,1)} %param.5, bf16[2,64,3200]{2,1,0:T(8,128)(2,1)} %param.4), kind=kLoop, calls=%fused_computation | loop fusion | bytes 3276800 | tf_op jit(solution)/shard_map/squeeze | solution.py:258
  1.5 0.7 %cut_0.1 = (bf16[64,3200]{1,0:T(8,128)(2,1)S(1)}, bf16[64,3200]{1,0:T(8,128)(2,1)S(1)}, bf16[64,2432]{1,0:T(8,128)(2,1)S(1)}, bf16[64,2432]{1,0:T(8,128)(2,1)S(1)}) custom-call(bf16[64,3200]{1,0:T(8,128)(2,1)S(1)} %get-tuple-element.52.refs_0_, bf16[64,3200]{1,0:T(8,128)(2,1)S(1)} %get-tuple-element.53.refs_1_, ...), custom_call_target="tpu_custom_call" | custom-call | bytes 3080192 | tf_op jit(solution)/shard_map/cut_0/pallas_call | solution.py:181
  2.2 3.1 %collective-permute-start = (bf16[64,3200]{1,0:T(8,128)(2,1)S(1)}, bf16[64,3200]{1,0:T(8,128)(2,1)S(1)}, u32[]{:S(2)}, u32[]{:S(2)}) collective-permute-start(bf16[64,3200]{1,0:T(8,128)(2,1)S(1)} %get-tuple-element.18), channel_id=1, source_target_pairs={{0,8},{8,0},{16,24},{24,16},{1,9},{9,1},{17,25},{25,17},{2,10},{10... | collective-permute-start | bytes 1228808 | tf_op jit(solution)/shard_map/ppermute | solution.py:16
  5.3 2.6 %collective-permute-start.1 = (bf16[64,2432]{1,0:T(8,128)(2,1)S(1)}, bf16[64,2432]{1,0:T(8,128)(2,1)S(1)}, u32[]{:S(2)}, u32[]{:S(2)}) collective-permute-start(bf16[64,2432]{1,0:T(8,128)(2,1)S(1)} %get-tuple-element.19), channel_id=1, source_target_pairs={{0,16},{8,24},{16,0},{24,8},{1,17},{9,25},{17,1},{25,9},{2,18},{10... | collective-permute-start | bytes 933896 | tf_op jit(solution)/shard_map/ppermute | solution.py:16
  7.9 0.1 cut_1.1
  7.9 0.0 copy-start
  7.9 2.0 %collective-permute-start.4 = (bf16[64,768]{1,0:T(8,128)(2,1)S(1)}, bf16[64,768]{1,0:T(8,128)(2,1)S(1)}, u32[]{:S(2)}, u32[]{:S(2)}) collective-permute-start(bf16[64,768]{1,0:T(8,128)(2,1)S(1)} %get-tuple-element.25), channel_id=1, source_target_pairs={{0,16},{8,24},{16,0},{24,8},{1,17},{9,25},{17,1},{25,9},{2,18},{10... | collective-permute-start | bytes 294920 | tf_op jit(solution)/shard_map/ppermute | solution.py:16
  9.9 2.0 %collective-permute-start.5 = (bf16[64,768]{1,0:T(8,128)(2,1)S(1)}, bf16[64,768]{1,0:T(8,128)(2,1)S(1)}, u32[]{:S(2)}, u32[]{:S(2)}) collective-permute-start(bf16[64,768]{1,0:T(8,128)(2,1)S(1)} %get-tuple-element.26), channel_id=1, source_target_pairs={{0,24},{8,16},{16,8},{24,0},{1,25},{9,17},{17,9},{25,1},{2,26},{10... | collective-permute-start | bytes 294920 | tf_op jit(solution)/shard_map/ppermute | solution.py:16
  11.9 0.1 copy.5.direct_ref
  12.0 9.8 %collective-permute-done.1.refs_2_ = bf16[64,2432]{1,0:T(8,128)(2,1)S(1)} collective-permute-done((bf16[64,2432]{1,0:T(8,128)(2,1)S(1)}, bf16[64,2432]{1,0:T(8,128)(2,1)S(1)}, u32[]{:S(2)}, u32[]{:S(2)}) %collective-permute-start.1) | collective-permute-done | bytes 311328 | tf_op jit(solution)/shard_map/ppermute | solution.py:16
  21.9 9.7 %collective-permute-done.2.refs_3_ = bf16[64,2432]{1,0:T(8,128)(2,1)S(1)} collective-permute-done((bf16[64,2432]{1,0:T(8,128)(2,1)S(1)}, bf16[64,2432]{1,0:T(8,128)(2,1)S(1)}, u32[]{:S(2)}, u32[]{:S(2)}) %collective-permute-start.2) | collective-permute-done | bytes 311328 | tf_op jit(solution)/shard_map/ppermute | solution.py:16
  31.5 0.0 collective-permute-done.refs_1_
  31.5 1.8 %partial_0.1 = (bf16[2,256,896]{2,1,0:T(8,128)(2,1)S(1)}, bf16[2,256,128]{2,1,0:T(8,128)(2,1)S(1)}, f32[4,4,1,32,128]{4,3,2,1,0:T(8,128)S(1)}, f32[4,4,1,32,128]{4,3,2,1,0:T(8,128)S(1)}) custom-call(f32[4,32,1]{2,1,0:T(8,128)S(1)} %copy.5.direct_ref, bf16[64,3200]{1,0:T(8,128)(2,1)S(1)} %get-tuple-element.17.refs_0_, ...), custom_call_target="tpu_custom_call" | custom-call | flops 234881024 | bytes 3080192 | tf_op jit(solution)/shard_map/partial_0/pallas_call | solution.py:181
  33.4 0.1 collective-permute-start.3
  33.4 9.0 %collective-permute-done.4.refs_2_ = bf16[64,768]{1,0:T(8,128)(2,1)S(1)} collective-permute-done((bf16[64,768]{1,0:T(8,128)(2,1)S(1)}, bf16[64,768]{1,0:T(8,128)(2,1)S(1)}, u32[]{:S(2)}, u32[]{:S(2)}) %collective-permute-start.4) | collective-permute-done | bytes 98336 | tf_op jit(solution)/shard_map/ppermute | solution.py:16
  42.4 1.7 %partial_1.1 = (f32[4,4,1,32,128]{4,3,2,1,0:T(8,128)S(1)}, f32[4,4,1,32,128]{4,3,2,1,0:T(8,128)S(1)}) custom-call(f32[4,32,1]{2,1,0:T(8,128)S(1)} %copy.5.direct_ref, bf16[2,256,896]{2,1,0:T(8,128)(2,1)S(1)} %get-tuple-element.23.expect_ref, bf16[2,256,128]{2,1,0:T(8,128)(2,1)S(1)} %get-tuple-element.24.tails_ref, ...), custom_call_target="tpu_custom_call" | custom-call | flops 234881024 | bytes 2654208 | tf_op jit(solution)/shard_map/partial_1/pallas_call | solution.py:181
  44.1 0.1 collective-permute-start.6
  44.3 1.4 %collective-permute-done.6 = f32[4,4,1,32,128]{4,3,2,1,0:T(8,128)S(1)} collective-permute-done((f32[4,4,1,32,128]{4,3,2,1,0:T(8,128)S(1)}, f32[4,4,1,32,128]{4,3,2,1,0:T(8,128)S(1)}, u32[]{:S(2)}, u32[]{:S(2)}) %collective-permute-start.6) | collective-permute-done | bytes 262176 | tf_op jit(solution)/shard_map/ppermute | solution.py:16
  45.8 2.5 %collective-permute-start.7 = (f32[4,2,32,128]{3,2,0,1:T(8,128)S(1)}, f32[4,2,32,128]{3,2,0,1:T(8,128)S(1)}, u32[]{:S(2)}, u32[]{:S(2)}) collective-permute-start(f32[4,2,32,128]{3,2,0,1:T(8,128)S(1)} %pad_maximum_fusion), channel_id=1, source_target_pairs={{0,6},{1,7},{2,4},{3,5},{4,2},{5,3},{6,0},{7,1},{8,14},{9,15},{10,... | collective-permute-start | bytes 393224 | tf_op jit(solution)/shard_map/ppermute | solution.py:16
  48.3 0.6 collective-permute-start.8
  48.9 0.6 collective-permute-start.9
  49.5 2.9 %collective-permute-done.7 = f32[4,2,32,128]{3,2,0,1:T(8,128)S(1)} collective-permute-done((f32[4,2,32,128]{3,2,0,1:T(8,128)S(1)}, f32[4,2,32,128]{3,2,0,1:T(8,128)S(1)}, u32[]{:S(2)}, u32[]{:S(2)}) %collective-permute-start.7) | collective-permute-done | bytes 131104 | tf_op jit(solution)/shard_map/ppermute | solution.py:16
  52.5 2.7 %collective-permute-done.8 = f32[4,2,32,128]{3,2,0,1:T(8,128)S(1)} collective-permute-done((f32[4,2,32,128]{3,2,0,1:T(8,128)S(1)}, f32[4,2,32,128]{3,2,0,1:T(8,128)S(1)}, u32[]{:S(2)}, u32[]{:S(2)}) %collective-permute-start.8) | collective-permute-done | bytes 131104 | tf_op jit(solution)/shard_map/ppermute | solution.py:16
  55.1 0.1 collective-permute-done.9
  55.3 2.5 %collective-permute-start.10 = (f32[2,32,128]{2,1,0:T(8,128)S(1)}, f32[2,32,128]{2,1,0:T(8,128)S(1)}, u32[]{:S(2)}, u32[]{:S(2)}) collective-permute-start(f32[2,32,128]{2,1,0:T(8,128)S(1)} %get-tuple-element.41), channel_id=1, source_target_pairs={{0,24},{8,16},{16,8},{24,0},{1,25},{9,17},{17,9},{25,1},{2,26},{10... | collective-permute-start | bytes 98312 | tf_op jit(solution)/shard_map/ppermute | solution.py:16
  57.8 0.6 collective-permute-start.12
  58.4 1.3 %collective-permute-start.11 = (f32[2,32,128]{2,1,0:T(8,128)S(1)}, f32[2,32,128]{2,1,0:T(8,128)S(1)}, u32[]{:S(2)}, u32[]{:S(2)}) collective-permute-start(f32[2,32,128]{2,1,0:T(8,128)S(1)} %get-tuple-element.43), channel_id=1, source_target_pairs={{0,8},{8,0},{16,24},{24,16},{1,9},{9,1},{17,25},{25,17},{2,10},{10... | collective-permute-start | bytes 98312 | tf_op jit(solution)/shard_map/ppermute | solution.py:16
  59.7 1.4 %collective-permute-done.10 = f32[2,32,128]{2,1,0:T(8,128)S(1)} collective-permute-done((f32[2,32,128]{2,1,0:T(8,128)S(1)}, f32[2,32,128]{2,1,0:T(8,128)S(1)}, u32[]{:S(2)}, u32[]{:S(2)}) %collective-permute-start.10) | collective-permute-done | bytes 32800 | tf_op jit(solution)/shard_map/ppermute | solution.py:16
  61.1 1.9 %collective-permute-done.12 = f32[2,32,128]{2,1,0:T(8,128)S(1)} collective-permute-done((f32[2,32,128]{2,1,0:T(8,128)S(1)}, f32[2,32,128]{2,1,0:T(8,128)S(1)}, u32[]{:S(2)}, u32[]{:S(2)}) %collective-permute-start.12) | collective-permute-done | bytes 32800 | tf_op jit(solution)/shard_map/ppermute | solution.py:16
  63.0 0.0 collective-permute-done.11
  63.0 0.1 slice_bitcast_fusion.7
  63.1 0.7 %select_select_fusion = f32[4,64,32]{1,2,0:T(8,128)} fusion(f32[64,32]{0,1:T(8,128)S(1)} %get-tuple-element.45, f32[64,32]{0,1:T(8,128)S(1)} %get-tuple-element.46, f32[64,32]{0,1:T(8,128)S(1)} %get-tuple-element.47, f32[64,32]{0,1:T(8,128)S(1)} %get-tuple-element.44, pred[4]{0:T(512)(128)(4,1)S(1)} %get-tuple-element.49, ...), kind=kLoop, calls=%fused_computation.10 | loop fusion | flops 32768 | bytes 65552 | tf_op jit(solution)/shard_map/jit(_where)/select_n | solution.py:294
  (17 shorter events, 0.3 us)
Async XLA Ops:
  2.2 29.3 %collective-permute-start = (bf16[64,3200]{1,0:T(8,128)(2,1)S(1)}, bf16[64,3200]{1,0:T(8,128)(2,1)S(1)}, u32[]{:S(2)}, u32[]{:S(2)}) collective-permute-start(bf16[64,3200]{1,0:T(8,128)(2,1)S(1)} %get-tuple-element.18), channel_id=1, source_target_pairs={{0,8},{8,0},{16,24},{24,16},{1,9},{9,1},{17,25},{25,17},{2,10},{10... | collective-permute-start | bytes 1228808 | tf_op jit(solution)/shard_map/ppermute | solution.py:16
  5.3 16.6 %collective-permute-start.1 = (bf16[64,2432]{1,0:T(8,128)(2,1)S(1)}, bf16[64,2432]{1,0:T(8,128)(2,1)S(1)}, u32[]{:S(2)}, u32[]{:S(2)}) collective-permute-start(bf16[64,2432]{1,0:T(8,128)(2,1)S(1)} %get-tuple-element.19), channel_id=1, source_target_pairs={{0,16},{8,24},{16,0},{24,8},{1,17},{9,25},{17,1},{25,9},{2,18},{10... | collective-permute-start | bytes 933896 | tf_op jit(solution)/shard_map/ppermute | solution.py:16
  7.9 23.7 %collective-permute-start.2 = (bf16[64,2432]{1,0:T(8,128)(2,1)S(1)}, bf16[64,2432]{1,0:T(8,128)(2,1)S(1)}, u32[]{:S(2)}, u32[]{:S(2)}) collective-permute-start(bf16[64,2432]{1,0:T(8,128)(2,1)S(1)} %get-tuple-element.20), channel_id=1, source_target_pairs={{0,24},{8,16},{16,8},{24,0},{1,25},{9,17},{17,9},{25,1},{2,26},{10... | collective-permute-start | bytes 933896 | tf_op jit(solution)/shard_map/ppermute | solution.py:16
  7.9 4.0 %copy-start = (f32[2,2,32]{2,1,0:T(2,128)S(1)}, f32[2,2,32]{2,1,0:T(2,128)}, u32[]{:S(2)}) copy-start(f32[2,2,32]{2,1,0:T(2,128)} %param.6) | copy-start | bytes 1540
  7.9 34.5 %collective-permute-start.4 = (bf16[64,768]{1,0:T(8,128)(2,1)S(1)}, bf16[64,768]{1,0:T(8,128)(2,1)S(1)}, u32[]{:S(2)}, u32[]{:S(2)}) collective-permute-start(bf16[64,768]{1,0:T(8,128)(2,1)S(1)} %get-tuple-element.25), channel_id=1, source_target_pairs={{0,16},{8,24},{16,0},{24,8},{1,17},{9,25},{17,1},{25,9},{2,18},{10... | collective-permute-start | bytes 294920 | tf_op jit(solution)/shard_map/ppermute | solution.py:16
  9.9 32.5 %collective-permute-start.5 = (bf16[64,768]{1,0:T(8,128)(2,1)S(1)}, bf16[64,768]{1,0:T(8,128)(2,1)S(1)}, u32[]{:S(2)}, u32[]{:S(2)}) collective-permute-start(bf16[64,768]{1,0:T(8,128)(2,1)S(1)} %get-tuple-element.26), channel_id=1, source_target_pairs={{0,24},{8,16},{16,8},{24,0},{1,25},{9,17},{17,9},{25,1},{2,26},{10... | collective-permute-start | bytes 294920 | tf_op jit(solution)/shard_map/ppermute | solution.py:16
  33.4 10.9 %collective-permute-start.3 = (f32[4,4,1,32,128]{4,3,2,1,0:T(8,128)S(1)}, f32[4,4,1,32,128]{4,3,2,1,0:T(8,128)S(1)}, u32[]{:S(2)}, u32[]{:S(2)}) collective-permute-start(f32[4,4,1,32,128]{4,3,2,1,0:T(8,128)S(1)} %get-tuple-element.22), channel_id=1, source_target_pairs={{0,1},{1,0},{2,3},{3,2},{4,5},{5,4},{6,7},{7,6},{8,9},{9,8},{10,11... | collective-permute-start | bytes 786440 | tf_op jit(solution)/shard_map/ppermute | solution.py:16
  44.1 1.6 %collective-permute-start.6 = (f32[4,4,1,32,128]{4,3,2,1,0:T(8,128)S(1)}, f32[4,4,1,32,128]{4,3,2,1,0:T(8,128)S(1)}, u32[]{:S(2)}, u32[]{:S(2)}) collective-permute-start(f32[4,4,1,32,128]{4,3,2,1,0:T(8,128)S(1)} %get-tuple-element.28), channel_id=1, source_target_pairs={{0,1},{1,0},{2,3},{3,2},{4,5},{5,4},{6,7},{7,6},{8,9},{9,8},{10,11... | collective-permute-start | bytes 786440 | tf_op jit(solution)/shard_map/ppermute | solution.py:16
  45.8 6.6 %collective-permute-start.7 = (f32[4,2,32,128]{3,2,0,1:T(8,128)S(1)}, f32[4,2,32,128]{3,2,0,1:T(8,128)S(1)}, u32[]{:S(2)}, u32[]{:S(2)}) collective-permute-start(f32[4,2,32,128]{3,2,0,1:T(8,128)S(1)} %pad_maximum_fusion), channel_id=1, source_target_pairs={{0,6},{1,7},{2,4},{3,5},{4,2},{5,3},{6,0},{7,1},{8,14},{9,15},{10,... | collective-permute-start | bytes 393224 | tf_op jit(solution)/shard_map/ppermute | solution.py:16
  48.3 6.8 %collective-permute-start.8 = (f32[4,2,32,128]{3,2,0,1:T(8,128)S(1)}, f32[4,2,32,128]{3,2,0,1:T(8,128)S(1)}, u32[]{:S(2)}, u32[]{:S(2)}) collective-permute-start(f32[4,2,32,128]{3,2,0,1:T(8,128)S(1)} %pad_maximum_fusion.1), channel_id=1, source_target_pairs={{0,4},{1,5},{2,6},{3,7},{4,0},{5,1},{6,2},{7,3},{8,12},{9,13},{10,... | collective-permute-start | bytes 393224 | tf_op jit(solution)/shard_map/ppermute | solution.py:16
  48.9 6.3 %collective-permute-start.9 = (f32[4,2,32,128]{3,2,0,1:T(8,128)S(1)}, f32[4,2,32,128]{3,2,0,1:T(8,128)S(1)}, u32[]{:S(2)}, u32[]{:S(2)}) collective-permute-start(f32[4,2,32,128]{3,2,0,1:T(8,128)S(1)} %pad_maximum_fusion.2), channel_id=1, source_target_pairs={{0,2},{1,3},{2,0},{3,1},{4,6},{5,7},{6,4},{7,5},{8,10},{9,11},{10,... | collective-permute-start | bytes 393224 | tf_op jit(solution)/shard_map/ppermute | solution.py:16
  55.3 5.8 %collective-permute-start.10 = (f32[2,32,128]{2,1,0:T(8,128)S(1)}, f32[2,32,128]{2,1,0:T(8,128)S(1)}, u32[]{:S(2)}, u32[]{:S(2)}) collective-permute-start(f32[2,32,128]{2,1,0:T(8,128)S(1)} %get-tuple-element.41), channel_id=1, source_target_pairs={{0,24},{8,16},{16,8},{24,0},{1,25},{9,17},{17,9},{25,1},{2,26},{10... | collective-permute-start | bytes 98312 | tf_op jit(solution)/shard_map/ppermute | solution.py:16
  57.8 1.9 %copy-start.1 = (s32[4,2]{0,1:T(2,128)S(1)}, s32[4,2]{0,1:T(2,128)}, u32[]{:S(2)}) copy-start(s32[4,2]{0,1:T(2,128)} %param.7) | copy-start | bytes 100
  57.8 5.2 %collective-permute-start.12 = (f32[2,32,128]{2,1,0:T(8,128)S(1)}, f32[2,32,128]{2,1,0:T(8,128)S(1)}, u32[]{:S(2)}, u32[]{:S(2)}) collective-permute-start(f32[2,32,128]{2,1,0:T(8,128)S(1)} %get-tuple-element.42), channel_id=1, source_target_pairs={{0,16},{8,24},{16,0},{24,8},{1,17},{9,25},{17,1},{25,9},{2,18},{10... | collective-permute-start | bytes 98312 | tf_op jit(solution)/shard_map/ppermute | solution.py:16
  58.4 4.6 %collective-permute-start.11 = (f32[2,32,128]{2,1,0:T(8,128)S(1)}, f32[2,32,128]{2,1,0:T(8,128)S(1)}, u32[]{:S(2)}, u32[]{:S(2)}) collective-permute-start(f32[2,32,128]{2,1,0:T(8,128)S(1)} %get-tuple-element.43), channel_id=1, source_target_pairs={{0,8},{8,0},{16,24},{24,16},{1,9},{9,1},{17,25},{25,17},{2,10},{10... | collective-permute-start | bytes 98312 | tf_op jit(solution)/shard_map/ppermute | solution.py:16

commit v5 on v4

--- a/solution.py
+++ b/solution.py
@@ -118,7 +118,7 @@
 
 
 def first_kernel(width, planes, counts, shocks, direct_ref, *refs):
-    messages = refs[:planes]
+    messages = refs[:planes][::-1]
     expect_ref, tails_ref, keep_ref, give_ref, responses, products = refs[planes:]
     outputs = expect_ref.shape[0]
     rows = messages[0].shape[0]
@@ -204,6 +204,7 @@
     rest = grid - width * planes
     depth = width + rest
     share = packed_share(planes, outputs + shocks, rest)
+    masks = range(1, planes)
 
     def cut(name, arrays, sent, counts, tail_at=None):
         def columns(m, count):
@@ -257,16 +258,16 @@
     rest_group = range(FIRST, shocks)
     arrays = [expect[o] for o in range(outputs)] + [distrib[s] for s in range(shocks)]
     some = outputs + len(group)
-    counts = [len(arrays) if m < 2 else some for m in range(planes)]
+    counts = [len(arrays)] + [some] * (planes - 1)
     first = to_planes(cut("cut_0", arrays, range(planes), counts, outputs), range(planes))
     if rest_group:
-        later = cut("cut_1", arrays[some:], range(2, planes), [len(rest_group)] * (planes - 2))
-        later = first[:2] + to_planes(later, range(2, planes))
+        later = cut("cut_1", arrays[some:], masks, [len(rest_group)] * len(masks))
+        later = first[:1] + to_planes(later, masks)
     expect_all, tails, *parts = kernel_call(
         functools.partial(first_kernel, width, planes, counts, group),
         "partial_0",
         group,
-        [flat] + first,
+        [flat] + first[::-1],
         [
             jax.ShapeDtypeStruct((outputs, horizon, depth), expect.dtype),
             jax.ShapeDtypeStruct((shocks, horizon, rest), distrib.dtype),
@@ -274,7 +275,7 @@
     )
     sums = [over_cores(*parts)]
     if rest_group:
-        begins = [some * width] * 2 + [0] * (planes - 2)
+        begins = [some * width] + [0] * len(masks)
         parts = kernel_call(
             functools.partial(next_kernel, width, begins, rest_group),
             "partial_1",

time: 63.9 us -> 62.9 us (0.984)
  waiting for transfers between devices: 38.8 us -> 33.2 us
  starting transfers between devices: 17.9 us -> 22.5 us
    ppermute x13 -> x14, waiting for transfers between devices: 38.8 us -> 33.2 us  [swap(): lax.ppermute(block, axis, [(i, i ^ mask) for i in range(lax.axis_size(axi...]
    ppermute x13 -> x14, starting transfers between devices: 17.9 us -> 22.5 us  [swap(): lax.ppermute(block, axis, [(i, i ^ mask) for i in range(lax.axis_size(axi...]
  transfers between devices with their start and end apart: 13 -> 14, of which waited for: 9 -> 9; matrix products, arithmetic and copies ran while one was open for 0% -> 0% of each run, Pallas kernels for 6% -> 6%
where the time goes in v5:
time: 62.9 us; the launch traced here: 62.8 us
  waiting for transfers between devices  33.2 us (53%)
  starting transfers between devices  22.5 us (36%)
  Pallas kernels  4.29 us (7%)
  local copies, waits for them, and re-layouts  1.75 us (3%)
  other arithmetic  0.88 us (1%)
    ppermute x14, waiting for transfers between devices, swap(): lax.ppermute(block, axis, [(i, i ^ mask) for i in range(lax.axis_size(axi...  33.2 us
    ppermute x14, starting transfers between devices, swap(): lax.ppermute(block, axis, [(i, i ^ mask) for i in range(lax.axis_size(axi...  22.5 us
    pallas_call x4, Pallas kernels, call(): pl.pallas_call(kernel, name=name, out_shape=out_shape, in_specs=[pl.Block...  4.29 us
    squeeze x1, local copies, waits for them, and re-layouts, shards(): distrib[s]  1.49 us
  transfers between devices with their start and end apart: 14, of which 9 were waited for; matrix products, arithmetic and copies ran while one was open for 0% of the time, Pallas kernels for 6%

profile of v5, /device:TPU:0, one launch (start us, length us, event | category | flops | bytes accessed | tf_op | source)
XLA Modules:
  0.0 62.8 jit_solution(234523610443726556)
XLA Ops:
  0.0 1.5 %slice_bitcast_fusion = (bf16[64,3200]{1,0:T(8,128)(2,1)S(1)}, bf16[64,3200]{1,0:T(8,128)(2,1)S(1)}, bf16[64,3200]{1,0:T(8,128)(2,1)S(1)}, bf16[64,3200]{1,0:T(8,128)(2,1)S(1)}) fusion(bf16[2,64,3200]{2,1,0:T(8,128)(2,1)} %param.5, bf16[2,64,3200]{2,1,0:T(8,128)(2,1)} %param.4), kind=kLoop, calls=%fused_computation | loop fusion | bytes 3276800 | tf_op jit(solution)/shard_map/squeeze | solution.py:259
  1.5 0.6 %cut_0.1 = (bf16[64,3200]{1,0:T(8,128)(2,1)S(1)}, bf16[64,2432]{1,0:T(8,128)(2,1)S(1)}, bf16[64,2432]{1,0:T(8,128)(2,1)S(1)}, bf16[64,2432]{1,0:T(8,128)(2,1)S(1)}) custom-call(bf16[64,3200]{1,0:T(8,128)(2,1)S(1)} %get-tuple-element.54.refs_0_, bf16[64,3200]{1,0:T(8,128)(2,1)S(1)} %get-tuple-element.55.refs_1_, ...), custom_call_target="tpu_custom_call" | custom-call | bytes 2981888 | tf_op jit(solution)/shard_map/cut_0/pallas_call | solution.py:181
  2.1 5.1 %collective-permute-start = (bf16[64,2432]{1,0:T(8,128)(2,1)S(1)}, bf16[64,2432]{1,0:T(8,128)(2,1)S(1)}, u32[]{:S(2)}, u32[]{:S(2)}) collective-permute-start(bf16[64,2432]{1,0:T(8,128)(2,1)S(1)} %get-tuple-element.18), channel_id=1, source_target_pairs={{0,24},{8,16},{16,8},{24,0},{1,25},{9,17},{17,9},{25,1},{2,26},{10... | collective-permute-start | bytes 933896 | tf_op jit(solution)/shard_map/ppermute | solution.py:16
  7.3 0.0 collective-permute-start.1
  7.3 0.6 %collective-permute-start.2 = (bf16[64,2432]{1,0:T(8,128)(2,1)S(1)}, bf16[64,2432]{1,0:T(8,128)(2,1)S(1)}, u32[]{:S(2)}, u32[]{:S(2)}) collective-permute-start(bf16[64,2432]{1,0:T(8,128)(2,1)S(1)} %get-tuple-element.20), channel_id=1, source_target_pairs={{0,8},{8,0},{16,24},{24,16},{1,9},{9,1},{17,25},{25,17},{2,10},{10... | collective-permute-start | bytes 933896 | tf_op jit(solution)/shard_map/ppermute | solution.py:16
  7.9 0.1 cut_1.1
  8.0 0.0 copy-start
  8.0 1.5 %collective-permute-start.4 = (bf16[64,768]{1,0:T(8,128)(2,1)S(1)}, bf16[64,768]{1,0:T(8,128)(2,1)S(1)}, u32[]{:S(2)}, u32[]{:S(2)}) collective-permute-start(bf16[64,768]{1,0:T(8,128)(2,1)S(1)} %get-tuple-element.26), channel_id=1, source_target_pairs={{0,8},{8,0},{16,24},{24,16},{1,9},{9,1},{17,25},{25,17},{2,10},{10... | collective-permute-start | bytes 294920 | tf_op jit(solution)/shard_map/ppermute | solution.py:16
  9.5 2.9 %collective-permute-start.5 = (bf16[64,768]{1,0:T(8,128)(2,1)S(1)}, bf16[64,768]{1,0:T(8,128)(2,1)S(1)}, u32[]{:S(2)}, u32[]{:S(2)}) collective-permute-start(bf16[64,768]{1,0:T(8,128)(2,1)S(1)} %get-tuple-element.27), channel_id=1, source_target_pairs={{0,16},{8,24},{16,0},{24,8},{1,17},{9,25},{17,1},{25,9},{2,18},{10... | collective-permute-start | bytes 294920 | tf_op jit(solution)/shard_map/ppermute | solution.py:16
  12.4 0.1 copy.5.direct_ref
  12.5 3.1 %collective-permute-done.refs_0_ = bf16[64,2432]{1,0:T(8,128)(2,1)S(1)} collective-permute-done((bf16[64,2432]{1,0:T(8,128)(2,1)S(1)}, bf16[64,2432]{1,0:T(8,128)(2,1)S(1)}, u32[]{:S(2)}, u32[]{:S(2)}) %collective-permute-start) | collective-permute-done | bytes 311328 | tf_op jit(solution)/shard_map/ppermute | solution.py:16
  15.6 3.8 %collective-permute-start.6 = (bf16[64,768]{1,0:T(8,128)(2,1)S(1)}, bf16[64,768]{1,0:T(8,128)(2,1)S(1)}, u32[]{:S(2)}, u32[]{:S(2)}) collective-permute-start(bf16[64,768]{1,0:T(8,128)(2,1)S(1)} %get-tuple-element.28), channel_id=1, source_target_pairs={{0,24},{8,16},{16,8},{24,0},{1,25},{9,17},{17,9},{25,1},{2,26},{10... | collective-permute-start | bytes 294920 | tf_op jit(solution)/shard_map/ppermute | solution.py:16
  19.4 19.6 %collective-permute-done.1.refs_1_ = bf16[64,2432]{1,0:T(8,128)(2,1)S(1)} collective-permute-done((bf16[64,2432]{1,0:T(8,128)(2,1)S(1)}, bf16[64,2432]{1,0:T(8,128)(2,1)S(1)}, u32[]{:S(2)}, u32[]{:S(2)}) %collective-permute-start.1) | collective-permute-done | bytes 311328 | tf_op jit(solution)/shard_map/ppermute | solution.py:16
  39.0 1.8 %partial_0.1 = (bf16[2,256,896]{2,1,0:T(8,128)(2,1)S(1)}, bf16[2,256,128]{2,1,0:T(8,128)(2,1)S(1)}, f32[4,4,1,32,128]{4,3,2,1,0:T(8,128)S(1)}, f32[4,4,1,32,128]{4,3,2,1,0:T(8,128)S(1)}) custom-call(f32[4,32,1]{2,1,0:T(8,128)S(1)} %copy.5.direct_ref, bf16[64,2432]{1,0:T(8,128)(2,1)S(1)} %collective-permute-done.refs_0_, ...), custom_call_target="tpu_custom_call" | custom-call | flops 234881024 | bytes 2981888 | tf_op jit(solution)/shard_map/partial_0/pallas_call | solution.py:181
  40.8 0.1 collective-permute-start.3
  40.9 0.2 collective-permute-done.5.refs_2_
  41.1 1.7 %partial_1.1 = (f32[4,4,1,32,128]{4,3,2,1,0:T(8,128)S(1)}, f32[4,4,1,32,128]{4,3,2,1,0:T(8,128)S(1)}) custom-call(f32[4,32,1]{2,1,0:T(8,128)S(1)} %copy.5.direct_ref, bf16[2,256,896]{2,1,0:T(8,128)(2,1)S(1)} %get-tuple-element.24.expect_ref, bf16[2,256,128]{2,1,0:T(8,128)(2,1)S(1)} %get-tuple-element.25.tails_ref, ...), custom_call_target="tpu_custom_call" | custom-call | flops 234881024 | bytes 2342912 | tf_op jit(solution)/shard_map/partial_1/pallas_call | solution.py:181
  42.8 0.4 collective-permute-start.7
  43.2 1.1 %collective-permute-done.7 = f32[4,4,1,32,128]{4,3,2,1,0:T(8,128)S(1)} collective-permute-done((f32[4,4,1,32,128]{4,3,2,1,0:T(8,128)S(1)}, f32[4,4,1,32,128]{4,3,2,1,0:T(8,128)S(1)}, u32[]{:S(2)}, u32[]{:S(2)}) %collective-permute-start.7) | collective-permute-done | bytes 262176 | tf_op jit(solution)/shard_map/ppermute | solution.py:16
  44.5 2.5 %collective-permute-start.8 = (f32[4,2,32,128]{3,2,0,1:T(8,128)S(1)}, f32[4,2,32,128]{3,2,0,1:T(8,128)S(1)}, u32[]{:S(2)}, u32[]{:S(2)}) collective-permute-start(f32[4,2,32,128]{3,2,0,1:T(8,128)S(1)} %pad_maximum_fusion), channel_id=1, source_target_pairs={{0,6},{1,7},{2,4},{3,5},{4,2},{5,3},{6,0},{7,1},{8,14},{9,15},{10,... | collective-permute-start | bytes 393224 | tf_op jit(solution)/shard_map/ppermute | solution.py:16
  47.0 0.6 collective-permute-start.9
  47.6 0.6 collective-permute-start.10
  48.2 3.1 %collective-permute-done.8 = f32[4,2,32,128]{3,2,0,1:T(8,128)S(1)} collective-permute-done((f32[4,2,32,128]{3,2,0,1:T(8,128)S(1)}, f32[4,2,32,128]{3,2,0,1:T(8,128)S(1)}, u32[]{:S(2)}, u32[]{:S(2)}) %collective-permute-start.8) | collective-permute-done | bytes 131104 | tf_op jit(solution)/shard_map/ppermute | solution.py:16
  51.3 2.7 %collective-permute-done.9 = f32[4,2,32,128]{3,2,0,1:T(8,128)S(1)} collective-permute-done((f32[4,2,32,128]{3,2,0,1:T(8,128)S(1)}, f32[4,2,32,128]{3,2,0,1:T(8,128)S(1)}, u32[]{:S(2)}, u32[]{:S(2)}) %collective-permute-start.9) | collective-permute-done | bytes 131104 | tf_op jit(solution)/shard_map/ppermute | solution.py:16
  54.0 0.1 collective-permute-done.10
  54.1 2.7 %collective-permute-start.11 = (f32[2,32,128]{2,1,0:T(8,128)S(1)}, f32[2,32,128]{2,1,0:T(8,128)S(1)}, u32[]{:S(2)}, u32[]{:S(2)}) collective-permute-start(f32[2,32,128]{2,1,0:T(8,128)S(1)} %get-tuple-element.43), channel_id=1, source_target_pairs={{0,24},{8,16},{16,8},{24,0},{1,25},{9,17},{17,9},{25,1},{2,26},{10... | collective-permute-start | bytes 98312 | tf_op jit(solution)/shard_map/ppermute | solution.py:16
  56.9 0.3 collective-permute-start.13
  57.2 1.4 %collective-permute-start.12 = (f32[2,32,128]{2,1,0:T(8,128)S(1)}, f32[2,32,128]{2,1,0:T(8,128)S(1)}, u32[]{:S(2)}, u32[]{:S(2)}) collective-permute-start(f32[2,32,128]{2,1,0:T(8,128)S(1)} %get-tuple-element.45), channel_id=1, source_target_pairs={{0,8},{8,0},{16,24},{24,16},{1,9},{9,1},{17,25},{25,17},{2,10},{10... | collective-permute-start | bytes 98312 | tf_op jit(solution)/shard_map/ppermute | solution.py:16
  58.6 1.4 %collective-permute-done.11 = f32[2,32,128]{2,1,0:T(8,128)S(1)} collective-permute-done((f32[2,32,128]{2,1,0:T(8,128)S(1)}, f32[2,32,128]{2,1,0:T(8,128)S(1)}, u32[]{:S(2)}, u32[]{:S(2)}) %collective-permute-start.11) | collective-permute-done | bytes 32800 | tf_op jit(solution)/shard_map/ppermute | solution.py:16
  60.0 2.0 %collective-permute-done.13 = f32[2,32,128]{2,1,0:T(8,128)S(1)} collective-permute-done((f32[2,32,128]{2,1,0:T(8,128)S(1)}, f32[2,32,128]{2,1,0:T(8,128)S(1)}, u32[]{:S(2)}, u32[]{:S(2)}) %collective-permute-start.13) | collective-permute-done | bytes 32800 | tf_op jit(solution)/shard_map/ppermute | solution.py:16
  62.0 0.1 slice_bitcast_fusion.7
  62.0 0.7 %select_select_fusion = f32[4,64,32]{1,2,0:T(8,128)} fusion(f32[64,32]{0,1:T(8,128)S(1)} %get-tuple-element.47, f32[64,32]{0,1:T(8,128)S(1)} %get-tuple-element.48, f32[64,32]{0,1:T(8,128)S(1)} %get-tuple-element.49, f32[64,32]{0,1:T(8,128)S(1)} %get-tuple-element.46, pred[4]{0:T(512)(128)(4,1)S(1)} %get-tuple-element.51, ...), kind=kLoop, calls=%fused_computation.10 | loop fusion | flops 32768 | bytes 65552 | tf_op jit(solution)/shard_map/jit(_where)/select_n | solution.py:295
  (19 shorter events, 0.3 us)
Async XLA Ops:
  2.1 13.4 %collective-permute-start = (bf16[64,2432]{1,0:T(8,128)(2,1)S(1)}, bf16[64,2432]{1,0:T(8,128)(2,1)S(1)}, u32[]{:S(2)}, u32[]{:S(2)}) collective-permute-start(bf16[64,2432]{1,0:T(8,128)(2,1)S(1)} %get-tuple-element.18), channel_id=1, source_target_pairs={{0,24},{8,16},{16,8},{24,0},{1,25},{9,17},{17,9},{25,1},{2,26},{10... | collective-permute-start | bytes 933896 | tf_op jit(solution)/shard_map/ppermute | solution.py:16
  7.3 31.7 %collective-permute-start.1 = (bf16[64,2432]{1,0:T(8,128)(2,1)S(1)}, bf16[64,2432]{1,0:T(8,128)(2,1)S(1)}, u32[]{:S(2)}, u32[]{:S(2)}) collective-permute-start(bf16[64,2432]{1,0:T(8,128)(2,1)S(1)} %get-tuple-element.19), channel_id=1, source_target_pairs={{0,16},{8,24},{16,0},{24,8},{1,17},{9,25},{17,1},{25,9},{2,18},{10... | collective-permute-start | bytes 933896 | tf_op jit(solution)/shard_map/ppermute | solution.py:16
  7.3 31.7 %collective-permute-start.2 = (bf16[64,2432]{1,0:T(8,128)(2,1)S(1)}, bf16[64,2432]{1,0:T(8,128)(2,1)S(1)}, u32[]{:S(2)}, u32[]{:S(2)}) collective-permute-start(bf16[64,2432]{1,0:T(8,128)(2,1)S(1)} %get-tuple-element.20), channel_id=1, source_target_pairs={{0,8},{8,0},{16,24},{24,16},{1,9},{9,1},{17,25},{25,17},{2,10},{10... | collective-permute-start | bytes 933896 | tf_op jit(solution)/shard_map/ppermute | solution.py:16
  8.0 4.4 %copy-start = (f32[2,2,32]{2,1,0:T(2,128)S(1)}, f32[2,2,32]{2,1,0:T(2,128)}, u32[]{:S(2)}) copy-start(f32[2,2,32]{2,1,0:T(2,128)} %param.6) | copy-start | bytes 1540
  8.0 32.9 %collective-permute-start.4 = (bf16[64,768]{1,0:T(8,128)(2,1)S(1)}, bf16[64,768]{1,0:T(8,128)(2,1)S(1)}, u32[]{:S(2)}, u32[]{:S(2)}) collective-permute-start(bf16[64,768]{1,0:T(8,128)(2,1)S(1)} %get-tuple-element.26), channel_id=1, source_target_pairs={{0,8},{8,0},{16,24},{24,16},{1,9},{9,1},{17,25},{25,17},{2,10},{10... | collective-permute-start | bytes 294920 | tf_op jit(solution)/shard_map/ppermute | solution.py:16
  9.5 31.6 %collective-permute-start.5 = (bf16[64,768]{1,0:T(8,128)(2,1)S(1)}, bf16[64,768]{1,0:T(8,128)(2,1)S(1)}, u32[]{:S(2)}, u32[]{:S(2)}) collective-permute-start(bf16[64,768]{1,0:T(8,128)(2,1)S(1)} %get-tuple-element.27), channel_id=1, source_target_pairs={{0,16},{8,24},{16,0},{24,8},{1,17},{9,25},{17,1},{25,9},{2,18},{10... | collective-permute-start | bytes 294920 | tf_op jit(solution)/shard_map/ppermute | solution.py:16
  15.6 25.5 %collective-permute-start.6 = (bf16[64,768]{1,0:T(8,128)(2,1)S(1)}, bf16[64,768]{1,0:T(8,128)(2,1)S(1)}, u32[]{:S(2)}, u32[]{:S(2)}) collective-permute-start(bf16[64,768]{1,0:T(8,128)(2,1)S(1)} %get-tuple-element.28), channel_id=1, source_target_pairs={{0,24},{8,16},{16,8},{24,0},{1,25},{9,17},{17,9},{25,1},{2,26},{10... | collective-permute-start | bytes 294920 | tf_op jit(solution)/shard_map/ppermute | solution.py:16
  40.8 2.4 %collective-permute-start.3 = (f32[4,4,1,32,128]{4,3,2,1,0:T(8,128)S(1)}, f32[4,4,1,32,128]{4,3,2,1,0:T(8,128)S(1)}, u32[]{:S(2)}, u32[]{:S(2)}) collective-permute-start(f32[4,4,1,32,128]{4,3,2,1,0:T(8,128)S(1)} %get-tuple-element.23), channel_id=1, source_target_pairs={{0,1},{1,0},{2,3},{3,2},{4,5},{5,4},{6,7},{7,6},{8,9},{9,8},{10,11... | collective-permute-start | bytes 786440 | tf_op jit(solution)/shard_map/ppermute | solution.py:16
  42.8 1.6 %collective-permute-start.7 = (f32[4,4,1,32,128]{4,3,2,1,0:T(8,128)S(1)}, f32[4,4,1,32,128]{4,3,2,1,0:T(8,128)S(1)}, u32[]{:S(2)}, u32[]{:S(2)}) collective-permute-start(f32[4,4,1,32,128]{4,3,2,1,0:T(8,128)S(1)} %get-tuple-element.30), channel_id=1, source_target_pairs={{0,1},{1,0},{2,3},{3,2},{4,5},{5,4},{6,7},{7,6},{8,9},{9,8},{10,11... | collective-permute-start | bytes 786440 | tf_op jit(solution)/shard_map/ppermute | solution.py:16
  44.5 6.8 %collective-permute-start.8 = (f32[4,2,32,128]{3,2,0,1:T(8,128)S(1)}, f32[4,2,32,128]{3,2,0,1:T(8,128)S(1)}, u32[]{:S(2)}, u32[]{:S(2)}) collective-permute-start(f32[4,2,32,128]{3,2,0,1:T(8,128)S(1)} %pad_maximum_fusion), channel_id=1, source_target_pairs={{0,6},{1,7},{2,4},{3,5},{4,2},{5,3},{6,0},{7,1},{8,14},{9,15},{10,... | collective-permute-start | bytes 393224 | tf_op jit(solution)/shard_map/ppermute | solution.py:16
  47.0 7.0 %collective-permute-start.9 = (f32[4,2,32,128]{3,2,0,1:T(8,128)S(1)}, f32[4,2,32,128]{3,2,0,1:T(8,128)S(1)}, u32[]{:S(2)}, u32[]{:S(2)}) collective-permute-start(f32[4,2,32,128]{3,2,0,1:T(8,128)S(1)} %pad_maximum_fusion.1), channel_id=1, source_target_pairs={{0,4},{1,5},{2,6},{3,7},{4,0},{5,1},{6,2},{7,3},{8,12},{9,13},{10,... | collective-permute-start | bytes 393224 | tf_op jit(solution)/shard_map/ppermute | solution.py:16
  47.6 6.5 %collective-permute-start.10 = (f32[4,2,32,128]{3,2,0,1:T(8,128)S(1)}, f32[4,2,32,128]{3,2,0,1:T(8,128)S(1)}, u32[]{:S(2)}, u32[]{:S(2)}) collective-permute-start(f32[4,2,32,128]{3,2,0,1:T(8,128)S(1)} %pad_maximum_fusion.2), channel_id=1, source_target_pairs={{0,2},{1,3},{2,0},{3,1},{4,6},{5,7},{6,4},{7,5},{8,10},{9,11},{10,... | collective-permute-start | bytes 393224 | tf_op jit(solution)/shard_map/ppermute | solution.py:16
  54.1 5.8 %collective-permute-start.11 = (f32[2,32,128]{2,1,0:T(8,128)S(1)}, f32[2,32,128]{2,1,0:T(8,128)S(1)}, u32[]{:S(2)}, u32[]{:S(2)}) collective-permute-start(f32[2,32,128]{2,1,0:T(8,128)S(1)} %get-tuple-element.43), channel_id=1, source_target_pairs={{0,24},{8,16},{16,8},{24,0},{1,25},{9,17},{17,9},{25,1},{2,26},{10... | collective-permute-start | bytes 98312 | tf_op jit(solution)/shard_map/ppermute | solution.py:16
  56.9 1.7 %copy-start.1 = (s32[4,2]{0,1:T(2,128)S(1)}, s32[4,2]{0,1:T(2,128)}, u32[]{:S(2)}) copy-start(s32[4,2]{0,1:T(2,128)} %param.7) | copy-start | bytes 100
  56.9 5.1 %collective-permute-start.13 = (f32[2,32,128]{2,1,0:T(8,128)S(1)}, f32[2,32,128]{2,1,0:T(8,128)S(1)}, u32[]{:S(2)}, u32[]{:S(2)}) collective-permute-start(f32[2,32,128]{2,1,0:T(8,128)S(1)} %get-tuple-element.44), channel_id=1, source_target_pairs={{0,16},{8,24},{16,0},{24,8},{1,17},{9,25},{17,1},{25,9},{2,18},{10... | collective-permute-start | bytes 98312 | tf_op jit(solution)/shard_map/ppermute | solution.py:16
  57.2 4.8 %collective-permute-start.12 = (f32[2,32,128]{2,1,0:T(8,128)S(1)}, f32[2,32,128]{2,1,0:T(8,128)S(1)}, u32[]{:S(2)}, u32[]{:S(2)}) collective-permute-start(f32[2,32,128]{2,1,0:T(8,128)S(1)} %get-tuple-element.45), channel_id=1, source_target_pairs={{0,8},{8,0},{16,24},{24,16},{1,9},{9,1},{17,25},{25,17},{2,10},{10... | collective-permute-start | bytes 98312 | tf_op jit(solution)/shard_map/ppermute | solution.py:16

commit v6 on v5

--- a/solution.py
+++ b/solution.py
@@ -18,15 +18,28 @@
 
 def add_diagonals(block):
     rows, dates = block.shape
-    row_id = lax.broadcasted_iota(jnp.int32, (rows, dates), 0)
-    date_id = lax.broadcasted_iota(jnp.int32, (rows, dates), 1)
-    least = jnp.minimum(row_id, date_id)
+    lane = lax.broadcasted_iota(jnp.int32, (rows, LANES), 1)
+    top_row = lax.broadcasted_iota(jnp.int32, (8, LANES), 0)
+    tiles = [block[:, start : start + LANES] for start in range(0, dates, LANES)]
     offset = 1
     while offset < rows:
-        moved = pltpu.roll(pltpu.roll(block, offset, 1), offset, 0)
-        block = block + jnp.where(least >= offset, moved, 0.0)
+        moved = tiles
+        if offset % LANES:
+            turned = [pltpu.roll(tile, offset % LANES, 1) for tile in tiles]
+            behind = [jnp.zeros_like(turned[0])] + turned[:-1]
+            moved = [jnp.where(lane < offset % LANES, low, high) for low, high in zip(behind, turned)]
+        past = offset // LANES
+        sums = tiles[:past]
+        for tile, more in zip(tiles[past:], moved[: len(tiles) - past]):
+            if offset % 8:
+                more = pltpu.roll(more, offset, 0)
+                more = jnp.concatenate([jnp.where(top_row < offset, 0.0, more[:8]), more[8:]], axis=0)
+                sums.append(tile + more)
+            else:
+                sums.append(jnp.concatenate([tile[:offset], tile[offset:] + more[: rows - offset]], axis=0))
+        tiles = sums
         offset = offset * 2
-    return block, row_id, date_id
+    return jnp.concatenate(tiles, axis=1)
 
 
 def packed_share(planes, arrays, rest):
@@ -95,10 +108,12 @@
         for start in range(0, horizon, step):
             blocks = []
             for output in range(outputs):
-                block, row_id, date_id = add_diagonals(products[output, start : start + step, :])
+                block = add_diagonals(products[output, start : start + step, :])
                 if last[output] is not None:
                     spread = jnp.broadcast_to(last[output], block.shape)
                     moved = pltpu.roll(spread, 1, 1, stride=1, stride_axis=0)
+                    row_id = lax.broadcasted_iota(jnp.int32, block.shape, 0)
+                    date_id = lax.broadcasted_iota(jnp.int32, block.shape, 1)
                     block = block + jnp.where(date_id > row_id, moved, 0.0)
                 last[output] = block[step - 1 :]
                 blocks.append(block)
@@ -204,6 +219,7 @@
     rest = grid - width * planes
     depth = width + rest
     share = packed_share(planes, outputs + shocks, rest)
+    near = planes // 2
     masks = range(1, planes)
 
     def cut(name, arrays, sent, counts, tail_at=None):
@@ -241,15 +257,13 @@
             flops=2 * len(group) * outputs * horizon * horizon * depth,
         )
 
-    def scattered(values, own, axis, masks, scale, joined):
+    def over_chips(values, begin):
         def block(index):
-            return jnp.concatenate(
-                [lax.dynamic_index_in_dim(value, index, 0, False) for value in values], axis=joined
-            )
-
-        return functools.reduce(
-            jnp.add, [block(own)] + [swap(block(own ^ m), axis, scale * m) for m in masks]
-        )
+            parts = [lax.dynamic_slice_in_dim(value, begin, near, axis=1) for value in values]
+            return jnp.concatenate([lax.dynamic_index_in_dim(part, index, 0, False) for part in parts], axis=1)
+
+        swaps = [swap(block(chip ^ m), "hcol", 2 * m) for m in range(chips - 1, 0, -1)]
+        return functools.reduce(jnp.add, [block(chip)] + swaps)
 
     def over_cores(keep, give):
         return keep + swap(give, "hcol", 1)
@@ -284,8 +298,18 @@
         )
         sums.append(over_cores(*parts))
 
-    chip_sum = scattered(sums, chip, "hcol", range(chips - 1, 0, -1), 2, 1)
-    total = scattered([chip_sum], z, "hrow", [planes - 1, *range(1, planes - 1)], 1, 0)
+    here = z // near * near
+    far_sum = over_chips(sums, planes - near - here)
+    near_sum = over_chips(sums, here)
+
+    def of_plane(m):
+        return lax.dynamic_index_in_dim(far_sum if m >= near else near_sum, (z ^ m) % near, 0, False)
+
+    far_total = functools.reduce(jnp.add, [swap(of_plane(m), "hrow", m) for m in range(near, planes)])
+    far_total = lax.optimization_barrier(far_total)
+    total = functools.reduce(
+        jnp.add, [far_total, of_plane(0)] + [swap(of_plane(m), "hrow", m) for m in range(1, near)]
+    )
     shock_of = pair_index[:, 0, None, None]
     output_of = pair_index[:, 1, None, None]
     picked = jnp.zeros((pairs, cols, rows), jnp.float32)

time: 62.9 us -> 61.1 us (0.971)
  waiting for transfers between devices: 33.2 us -> 28 us
  starting transfers between devices: 22.5 us -> 26.1 us
    ppermute x14 -> x17, waiting for transfers between devices: 33.2 us -> 28 us  [swap(): lax.ppermute(block, axis, [(i, i ^ mask) for i in range(lax.axis_size(axi...]
    ppermute x14 -> x17, starting transfers between devices: 22.5 us -> 26.1 us  [swap(): lax.ppermute(block, axis, [(i, i ^ mask) for i in range(lax.axis_size(axi...]
  transfers between devices with their start and end apart: 14 -> 17, of which waited for: 9 -> 7; matrix products, arithmetic and copies ran while one was open for 0% -> 0% of each run, Pallas kernels for 6% -> 5%
where the time goes in v6:
time: 61.1 us; the launch traced here: 61 us
  waiting for transfers between devices  28 us (46%)
  starting transfers between devices  26.1 us (43%)
  Pallas kernels  4 us (7%)
  local copies, waits for them, and re-layouts  1.77 us (3%)
  other arithmetic  0.9 us (1%)
    ppermute x17, waiting for transfers between devices, swap(): lax.ppermute(block, axis, [(i, i ^ mask) for i in range(lax.axis_size(axi...  28 us
    ppermute x17, starting transfers between devices, swap(): lax.ppermute(block, axis, [(i, i ^ mask) for i in range(lax.axis_size(axi...  26.1 us
    pallas_call x4, Pallas kernels, call(): pl.pallas_call(kernel, name=name, out_shape=out_shape, in_specs=[pl.Block...  4 us
    squeeze x1, local copies, waits for them, and re-layouts, shards(): distrib[s]  1.49 us
  transfers between devices with their start and end apart: 17, of which 7 were waited for; matrix products, arithmetic and copies ran while one was open for 0% of the time, Pallas kernels for 5%

profile of v6, /device:TPU:0, one launch (start us, length us, event | category | flops | bytes accessed | tf_op | source)
XLA Modules:
  0.0 61.0 jit_solution(7143636706065170610)
XLA Ops:
  0.0 1.5 %slice_bitcast_fusion = (bf16[64,3200]{1,0:T(8,128)(2,1)S(1)}, bf16[64,3200]{1,0:T(8,128)(2,1)S(1)}, bf16[64,3200]{1,0:T(8,128)(2,1)S(1)}, bf16[64,3200]{1,0:T(8,128)(2,1)S(1)}) fusion(bf16[2,64,3200]{2,1,0:T(8,128)(2,1)} %param.5, bf16[2,64,3200]{2,1,0:T(8,128)(2,1)} %param.4), kind=kLoop, calls=%fused_computation | loop fusion | bytes 3276800 | tf_op jit(solution)/shard_map/squeeze | solution.py:273
  1.5 0.6 %cut_0.1 = (bf16[64,3200]{1,0:T(8,128)(2,1)S(1)}, bf16[64,2432]{1,0:T(8,128)(2,1)S(1)}, bf16[64,2432]{1,0:T(8,128)(2,1)S(1)}, bf16[64,2432]{1,0:T(8,128)(2,1)S(1)}) custom-call(bf16[64,3200]{1,0:T(8,128)(2,1)S(1)} %get-tuple-element.61.refs_0_, bf16[64,3200]{1,0:T(8,128)(2,1)S(1)} %get-tuple-element.62.refs_1_, ...), custom_call_target="tpu_custom_call" | custom-call | bytes 2981888 | tf_op jit(solution)/shard_map/cut_0/pallas_call | solution.py:196
  2.1 5.1 %collective-permute-start = (bf16[64,2432]{1,0:T(8,128)(2,1)S(1)}, bf16[64,2432]{1,0:T(8,128)(2,1)S(1)}, u32[]{:S(2)}, u32[]{:S(2)}) collective-permute-start(bf16[64,2432]{1,0:T(8,128)(2,1)S(1)} %get-tuple-element.18), channel_id=1, source_target_pairs={{0,24},{8,16},{16,8},{24,0},{1,25},{9,17},{17,9},{25,1},{2,26},{10... | collective-permute-start | bytes 933896 | tf_op jit(solution)/shard_map/ppermute | solution.py:16
  7.3 0.6 %collective-permute-start.2 = (bf16[64,2432]{1,0:T(8,128)(2,1)S(1)}, bf16[64,2432]{1,0:T(8,128)(2,1)S(1)}, u32[]{:S(2)}, u32[]{:S(2)}) collective-permute-start(bf16[64,2432]{1,0:T(8,128)(2,1)S(1)} %get-tuple-element.20), channel_id=1, source_target_pairs={{0,8},{8,0},{16,24},{24,16},{1,9},{9,1},{17,25},{25,17},{2,10},{10... | collective-permute-start | bytes 933896 | tf_op jit(solution)/shard_map/ppermute | solution.py:16
  7.9 0.1 cut_1.1
  8.0 0.0 copy-start
  8.0 1.5 %collective-permute-start.4 = (bf16[64,768]{1,0:T(8,128)(2,1)S(1)}, bf16[64,768]{1,0:T(8,128)(2,1)S(1)}, u32[]{:S(2)}, u32[]{:S(2)}) collective-permute-start(bf16[64,768]{1,0:T(8,128)(2,1)S(1)} %get-tuple-element.26), channel_id=1, source_target_pairs={{0,8},{8,0},{16,24},{24,16},{1,9},{9,1},{17,25},{25,17},{2,10},{10... | collective-permute-start | bytes 294920 | tf_op jit(solution)/shard_map/ppermute | solution.py:16
  9.5 2.9 %collective-permute-start.5 = (bf16[64,768]{1,0:T(8,128)(2,1)S(1)}, bf16[64,768]{1,0:T(8,128)(2,1)S(1)}, u32[]{:S(2)}, u32[]{:S(2)}) collective-permute-start(bf16[64,768]{1,0:T(8,128)(2,1)S(1)} %get-tuple-element.27), channel_id=1, source_target_pairs={{0,16},{8,24},{16,0},{24,8},{1,17},{9,25},{17,1},{25,9},{2,18},{10... | collective-permute-start | bytes 294920 | tf_op jit(solution)/shard_map/ppermute | solution.py:16
  12.4 0.1 copy.5.direct_ref
  12.5 3.1 %collective-permute-done.refs_0_ = bf16[64,2432]{1,0:T(8,128)(2,1)S(1)} collective-permute-done((bf16[64,2432]{1,0:T(8,128)(2,1)S(1)}, bf16[64,2432]{1,0:T(8,128)(2,1)S(1)}, u32[]{:S(2)}, u32[]{:S(2)}) %collective-permute-start) | collective-permute-done | bytes 311328 | tf_op jit(solution)/shard_map/ppermute | solution.py:16
  15.6 3.8 %collective-permute-start.6 = (bf16[64,768]{1,0:T(8,128)(2,1)S(1)}, bf16[64,768]{1,0:T(8,128)(2,1)S(1)}, u32[]{:S(2)}, u32[]{:S(2)}) collective-permute-start(bf16[64,768]{1,0:T(8,128)(2,1)S(1)} %get-tuple-element.28), channel_id=1, source_target_pairs={{0,24},{8,16},{16,8},{24,0},{1,25},{9,17},{17,9},{25,1},{2,26},{10... | collective-permute-start | bytes 294920 | tf_op jit(solution)/shard_map/ppermute | solution.py:16
  19.4 19.6 %collective-permute-done.1.refs_1_ = bf16[64,2432]{1,0:T(8,128)(2,1)S(1)} collective-permute-done((bf16[64,2432]{1,0:T(8,128)(2,1)S(1)}, bf16[64,2432]{1,0:T(8,128)(2,1)S(1)}, u32[]{:S(2)}, u32[]{:S(2)}) %collective-permute-start.1) | collective-permute-done | bytes 311328 | tf_op jit(solution)/shard_map/ppermute | solution.py:16
  39.0 1.7 %partial_0.1 = (bf16[2,256,896]{2,1,0:T(8,128)(2,1)S(1)}, bf16[2,256,128]{2,1,0:T(8,128)(2,1)S(1)}, f32[4,4,1,32,128]{4,3,2,1,0:T(8,128)S(1)}, f32[4,4,1,32,128]{4,3,2,1,0:T(8,128)S(1)}) custom-call(f32[4,32,1]{2,1,0:T(8,128)S(1)} %copy.5.direct_ref, bf16[64,2432]{1,0:T(8,128)(2,1)S(1)} %collective-permute-done.refs_0_, ...), custom_call_target="tpu_custom_call" | custom-call | flops 234881024 | bytes 2981888 | tf_op jit(solution)/shard_map/partial_0/pallas_call | solution.py:196
  40.7 0.1 collective-permute-start.3
  40.8 0.3 collective-permute-done.5.refs_2_
  41.1 1.6 %partial_1.1 = (f32[4,4,1,32,128]{4,3,2,1,0:T(8,128)S(1)}, f32[4,4,1,32,128]{4,3,2,1,0:T(8,128)S(1)}) custom-call(f32[4,32,1]{2,1,0:T(8,128)S(1)} %copy.5.direct_ref, bf16[2,256,896]{2,1,0:T(8,128)(2,1)S(1)} %get-tuple-element.24.expect_ref, bf16[2,256,128]{2,1,0:T(8,128)(2,1)S(1)} %get-tuple-element.25.tails_ref, ...), custom_call_target="tpu_custom_call" | custom-call | flops 234881024 | bytes 2342912 | tf_op jit(solution)/shard_map/partial_1/pallas_call | solution.py:196
  42.6 0.3 collective-permute-start.7
  43.0 1.3 %collective-permute-done.7 = f32[4,4,1,32,128]{4,3,2,1,0:T(8,128)S(1)} collective-permute-done((f32[4,4,1,32,128]{4,3,2,1,0:T(8,128)S(1)}, f32[4,4,1,32,128]{4,3,2,1,0:T(8,128)S(1)}, u32[]{:S(2)}, u32[]{:S(2)}) %collective-permute-start.7) | collective-permute-done | bytes 262176 | tf_op jit(solution)/shard_map/ppermute | solution.py:16
  44.3 2.5 %collective-permute-start.8 = (f32[2,2,32,128]{3,2,0,1:T(8,128)S(1)}, f32[2,2,32,128]{3,2,0,1:T(8,128)S(1)}, u32[]{:S(2)}, u32[]{:S(2)}) collective-permute-start(f32[2,2,32,128]{3,2,0,1:T(8,128)S(1)} %pad_maximum_fusion), channel_id=1, source_target_pairs={{0,6},{1,7},{2,4},{3,5},{4,2},{5,3},{6,0},{7,1},{8,14},{9,15},{10,... | collective-permute-start | bytes 196616 | tf_op jit(solution)/shard_map/ppermute | solution.py:16
  46.8 0.5 collective-permute-start.9
  47.4 0.5 collective-permute-start.10
  47.9 2.4 %collective-permute-start.13 = (f32[2,2,32,128]{3,2,0,1:T(8,128)S(1)}, f32[2,2,32,128]{3,2,0,1:T(8,128)S(1)}, u32[]{:S(2)}, u32[]{:S(2)}) collective-permute-start(f32[2,2,32,128]{3,2,0,1:T(8,128)S(1)} %pad_maximum_fusion.3), channel_id=1, source_target_pairs={{0,6},{1,7},{2,4},{3,5},{4,2},{5,3},{6,0},{7,1},{8,14},{9,15},{10,... | collective-permute-start | bytes 196616 | tf_op jit(solution)/shard_map/ppermute | solution.py:16
  50.4 0.5 collective-permute-start.14
  50.9 0.6 collective-permute-start.15
  51.5 0.7 %collective-permute-done.10 = f32[2,2,32,128]{3,2,0,1:T(8,128)S(1)} collective-permute-done((f32[2,2,32,128]{3,2,0,1:T(8,128)S(1)}, f32[2,2,32,128]{3,2,0,1:T(8,128)S(1)}, u32[]{:S(2)}, u32[]{:S(2)}) %collective-permute-start.10) | collective-permute-done | bytes 65568 | tf_op jit(solution)/shard_map/ppermute | solution.py:16
  52.3 2.7 %collective-permute-start.12 = (f32[2,32,128]{2,1,0:T(8,128)S(1)}, f32[2,32,128]{2,1,0:T(8,128)S(1)}, u32[]{:S(2)}, u32[]{:S(2)}) collective-permute-start(f32[2,32,128]{2,1,0:T(8,128)S(1)} %get-tuple-element.51), channel_id=1, source_target_pairs={{0,24},{8,16},{16,8},{24,0},{1,25},{9,17},{17,9},{25,1},{2,26},{10... | collective-permute-start | bytes 98312 | tf_op jit(solution)/shard_map/ppermute | solution.py:16
  55.0 0.5 collective-permute-start.11
  55.5 1.5 %collective-permute-start.16 = (f32[2,32,128]{2,1,0:T(8,128)S(1)}, f32[2,32,128]{2,1,0:T(8,128)S(1)}, u32[]{:S(2)}, u32[]{:S(2)}) collective-permute-start(f32[2,32,128]{2,1,0:T(8,128)S(1)} %dynamic-slice_bitcast_fusion), channel_id=1, source_target_pairs={{0,8},{8,0},{16,24},{24,16},{1,9},{9,1},{17,25},{25,17},{2,10},{10... | collective-permute-start | bytes 98312 | tf_op jit(solution)/shard_map/ppermute | solution.py:16
  57.1 1.0 %collective-permute-done.12 = f32[2,32,128]{2,1,0:T(8,128)S(1)} collective-permute-done((f32[2,32,128]{2,1,0:T(8,128)S(1)}, f32[2,32,128]{2,1,0:T(8,128)S(1)}, u32[]{:S(2)}, u32[]{:S(2)}) %collective-permute-start.12) | collective-permute-done | bytes 32800 | tf_op jit(solution)/shard_map/ppermute | solution.py:16
  58.0 2.1 %collective-permute-done.11 = f32[2,32,128]{2,1,0:T(8,128)S(1)} collective-permute-done((f32[2,32,128]{2,1,0:T(8,128)S(1)}, f32[2,32,128]{2,1,0:T(8,128)S(1)}, u32[]{:S(2)}, u32[]{:S(2)}) %collective-permute-start.11) | collective-permute-done | bytes 32800 | tf_op jit(solution)/shard_map/ppermute | solution.py:16
  60.2 0.1 slice_bitcast_fusion.7
  60.2 0.7 %select_select_fusion = f32[4,64,32]{1,2,0:T(8,128)} fusion(f32[64,32]{0,1:T(8,128)S(1)} %get-tuple-element.54, f32[64,32]{0,1:T(8,128)S(1)} %get-tuple-element.55, f32[64,32]{0,1:T(8,128)S(1)} %get-tuple-element.56, f32[64,32]{0,1:T(8,128)S(1)} %get-tuple-element.53, pred[4]{0:T(512)(128)(4,1)S(1)} %get-tuple-element.58, ...), kind=kLoop, calls=%fused_computation.16 | loop fusion | flops 32768 | bytes 65552 | tf_op jit(solution)/shard_map/jit(_where)/select_n | solution.py:319
  (31 shorter events, 0.3 us)
Async XLA Ops:
  2.1 13.4 %collective-permute-start = (bf16[64,2432]{1,0:T(8,128)(2,1)S(1)}, bf16[64,2432]{1,0:T(8,128)(2,1)S(1)}, u32[]{:S(2)}, u32[]{:S(2)}) collective-permute-start(bf16[64,2432]{1,0:T(8,128)(2,1)S(1)} %get-tuple-element.18), channel_id=1, source_target_pairs={{0,24},{8,16},{16,8},{24,0},{1,25},{9,17},{17,9},{25,1},{2,26},{10... | collective-permute-start | bytes 933896 | tf_op jit(solution)/shard_map/ppermute | solution.py:16
  7.3 31.7 %collective-permute-start.1 = (bf16[64,2432]{1,0:T(8,128)(2,1)S(1)}, bf16[64,2432]{1,0:T(8,128)(2,1)S(1)}, u32[]{:S(2)}, u32[]{:S(2)}) collective-permute-start(bf16[64,2432]{1,0:T(8,128)(2,1)S(1)} %get-tuple-element.19), channel_id=1, source_target_pairs={{0,16},{8,24},{16,0},{24,8},{1,17},{9,25},{17,1},{25,9},{2,18},{10... | collective-permute-start | bytes 933896 | tf_op jit(solution)/shard_map/ppermute | solution.py:16
  7.3 31.7 %collective-permute-start.2 = (bf16[64,2432]{1,0:T(8,128)(2,1)S(1)}, bf16[64,2432]{1,0:T(8,128)(2,1)S(1)}, u32[]{:S(2)}, u32[]{:S(2)}) collective-permute-start(bf16[64,2432]{1,0:T(8,128)(2,1)S(1)} %get-tuple-element.20), channel_id=1, source_target_pairs={{0,8},{8,0},{16,24},{24,16},{1,9},{9,1},{17,25},{25,17},{2,10},{10... | collective-permute-start | bytes 933896 | tf_op jit(solution)/shard_map/ppermute | solution.py:16
  8.0 4.4 %copy-start = (f32[2,2,32]{2,1,0:T(2,128)S(1)}, f32[2,2,32]{2,1,0:T(2,128)}, u32[]{:S(2)}) copy-start(f32[2,2,32]{2,1,0:T(2,128)} %param.6) | copy-start | bytes 1540
  8.0 32.7 %collective-permute-start.4 = (bf16[64,768]{1,0:T(8,128)(2,1)S(1)}, bf16[64,768]{1,0:T(8,128)(2,1)S(1)}, u32[]{:S(2)}, u32[]{:S(2)}) collective-permute-start(bf16[64,768]{1,0:T(8,128)(2,1)S(1)} %get-tuple-element.26), channel_id=1, source_target_pairs={{0,8},{8,0},{16,24},{24,16},{1,9},{9,1},{17,25},{25,17},{2,10},{10... | collective-permute-start | bytes 294920 | tf_op jit(solution)/shard_map/ppermute | solution.py:16
  9.5 31.6 %collective-permute-start.5 = (bf16[64,768]{1,0:T(8,128)(2,1)S(1)}, bf16[64,768]{1,0:T(8,128)(2,1)S(1)}, u32[]{:S(2)}, u32[]{:S(2)}) collective-permute-start(bf16[64,768]{1,0:T(8,128)(2,1)S(1)} %get-tuple-element.27), channel_id=1, source_target_pairs={{0,16},{8,24},{16,0},{24,8},{1,17},{9,25},{17,1},{25,9},{2,18},{10... | collective-permute-start | bytes 294920 | tf_op jit(solution)/shard_map/ppermute | solution.py:16
  15.6 25.5 %collective-permute-start.6 = (bf16[64,768]{1,0:T(8,128)(2,1)S(1)}, bf16[64,768]{1,0:T(8,128)(2,1)S(1)}, u32[]{:S(2)}, u32[]{:S(2)}) collective-permute-start(bf16[64,768]{1,0:T(8,128)(2,1)S(1)} %get-tuple-element.28), channel_id=1, source_target_pairs={{0,24},{8,16},{16,8},{24,0},{1,25},{9,17},{17,9},{25,1},{2,26},{10... | collective-permute-start | bytes 294920 | tf_op jit(solution)/shard_map/ppermute | solution.py:16
  40.7 2.2 %collective-permute-start.3 = (f32[4,4,1,32,128]{4,3,2,1,0:T(8,128)S(1)}, f32[4,4,1,32,128]{4,3,2,1,0:T(8,128)S(1)}, u32[]{:S(2)}, u32[]{:S(2)}) collective-permute-start(f32[4,4,1,32,128]{4,3,2,1,0:T(8,128)S(1)} %get-tuple-element.23), channel_id=1, source_target_pairs={{0,1},{1,0},{2,3},{3,2},{4,5},{5,4},{6,7},{7,6},{8,9},{9,8},{10,11... | collective-permute-start | bytes 786440 | tf_op jit(solution)/shard_map/ppermute | solution.py:16
  42.6 1.6 %collective-permute-start.7 = (f32[4,4,1,32,128]{4,3,2,1,0:T(8,128)S(1)}, f32[4,4,1,32,128]{4,3,2,1,0:T(8,128)S(1)}, u32[]{:S(2)}, u32[]{:S(2)}) collective-permute-start(f32[4,4,1,32,128]{4,3,2,1,0:T(8,128)S(1)} %get-tuple-element.30), channel_id=1, source_target_pairs={{0,1},{1,0},{2,3},{3,2},{4,5},{5,4},{6,7},{7,6},{8,9},{9,8},{10,11... | collective-permute-start | bytes 786440 | tf_op jit(solution)/shard_map/ppermute | solution.py:16
  44.3 6.5 %collective-permute-start.8 = (f32[2,2,32,128]{3,2,0,1:T(8,128)S(1)}, f32[2,2,32,128]{3,2,0,1:T(8,128)S(1)}, u32[]{:S(2)}, u32[]{:S(2)}) collective-permute-start(f32[2,2,32,128]{3,2,0,1:T(8,128)S(1)} %pad_maximum_fusion), channel_id=1, source_target_pairs={{0,6},{1,7},{2,4},{3,5},{4,2},{5,3},{6,0},{7,1},{8,14},{9,15},{10,... | collective-permute-start | bytes 196616 | tf_op jit(solution)/shard_map/ppermute | solution.py:16
  46.8 4.6 %collective-permute-start.9 = (f32[2,2,32,128]{3,2,0,1:T(8,128)S(1)}, f32[2,2,32,128]{3,2,0,1:T(8,128)S(1)}, u32[]{:S(2)}, u32[]{:S(2)}) collective-permute-start(f32[2,2,32,128]{3,2,0,1:T(8,128)S(1)} %pad_maximum_fusion.1), channel_id=1, source_target_pairs={{0,4},{1,5},{2,6},{3,7},{4,0},{5,1},{6,2},{7,3},{8,12},{9,13},{10,... | collective-permute-start | bytes 196616 | tf_op jit(solution)/shard_map/ppermute | solution.py:16
  47.4 4.9 %collective-permute-start.10 = (f32[2,2,32,128]{3,2,0,1:T(8,128)S(1)}, f32[2,2,32,128]{3,2,0,1:T(8,128)S(1)}, u32[]{:S(2)}, u32[]{:S(2)}) collective-permute-start(f32[2,2,32,128]{3,2,0,1:T(8,128)S(1)} %pad_maximum_fusion.2), channel_id=1, source_target_pairs={{0,2},{1,3},{2,0},{3,1},{4,6},{5,7},{6,4},{7,5},{8,10},{9,11},{10,... | collective-permute-start | bytes 196616 | tf_op jit(solution)/shard_map/ppermute | solution.py:16
  47.9 7.5 %collective-permute-start.13 = (f32[2,2,32,128]{3,2,0,1:T(8,128)S(1)}, f32[2,2,32,128]{3,2,0,1:T(8,128)S(1)}, u32[]{:S(2)}, u32[]{:S(2)}) collective-permute-start(f32[2,2,32,128]{3,2,0,1:T(8,128)S(1)} %pad_maximum_fusion.3), channel_id=1, source_target_pairs={{0,6},{1,7},{2,4},{3,5},{4,2},{5,3},{6,0},{7,1},{8,14},{9,15},{10,... | collective-permute-start | bytes 196616 | tf_op jit(solution)/shard_map/ppermute | solution.py:16
  50.4 5.1 %collective-permute-start.14 = (f32[2,2,32,128]{3,2,0,1:T(8,128)S(1)}, f32[2,2,32,128]{3,2,0,1:T(8,128)S(1)}, u32[]{:S(2)}, u32[]{:S(2)}) collective-permute-start(f32[2,2,32,128]{3,2,0,1:T(8,128)S(1)} %pad_maximum_fusion.4), channel_id=1, source_target_pairs={{0,4},{1,5},{2,6},{3,7},{4,0},{5,1},{6,2},{7,3},{8,12},{9,13},{10,... | collective-permute-start | bytes 196616 | tf_op jit(solution)/shard_map/ppermute | solution.py:16
  50.9 4.6 %collective-permute-start.15 = (f32[2,2,32,128]{3,2,0,1:T(8,128)S(1)}, f32[2,2,32,128]{3,2,0,1:T(8,128)S(1)}, u32[]{:S(2)}, u32[]{:S(2)}) collective-permute-start(f32[2,2,32,128]{3,2,0,1:T(8,128)S(1)} %pad_maximum_fusion.5), channel_id=1, source_target_pairs={{0,2},{1,3},{2,0},{3,1},{4,6},{5,7},{6,4},{7,5},{8,10},{9,11},{10,... | collective-permute-start | bytes 196616 | tf_op jit(solution)/shard_map/ppermute | solution.py:16
  52.3 5.8 %collective-permute-start.12 = (f32[2,32,128]{2,1,0:T(8,128)S(1)}, f32[2,32,128]{2,1,0:T(8,128)S(1)}, u32[]{:S(2)}, u32[]{:S(2)}) collective-permute-start(f32[2,32,128]{2,1,0:T(8,128)S(1)} %get-tuple-element.51), channel_id=1, source_target_pairs={{0,24},{8,16},{16,8},{24,0},{1,25},{9,17},{17,9},{25,1},{2,26},{10... | collective-permute-start | bytes 98312 | tf_op jit(solution)/shard_map/ppermute | solution.py:16
  55.0 5.2 %collective-permute-start.11 = (f32[2,32,128]{2,1,0:T(8,128)S(1)}, f32[2,32,128]{2,1,0:T(8,128)S(1)}, u32[]{:S(2)}, u32[]{:S(2)}) collective-permute-start(f32[2,32,128]{2,1,0:T(8,128)S(1)} %get-tuple-element.52), channel_id=1, source_target_pairs={{0,16},{8,24},{16,0},{24,8},{1,17},{9,25},{17,1},{25,9},{2,18},{10... | collective-permute-start | bytes 98312 | tf_op jit(solution)/shard_map/ppermute | solution.py:16
  55.5 1.6 %copy-start.1 = (s32[4,2]{0,1:T(2,128)S(1)}, s32[4,2]{0,1:T(2,128)}, u32[]{:S(2)}) copy-start(s32[4,2]{0,1:T(2,128)} %param.7) | copy-start | bytes 100
  55.5 4.6 %collective-permute-start.16 = (f32[2,32,128]{2,1,0:T(8,128)S(1)}, f32[2,32,128]{2,1,0:T(8,128)S(1)}, u32[]{:S(2)}, u32[]{:S(2)}) collective-permute-start(f32[2,32,128]{2,1,0:T(8,128)S(1)} %dynamic-slice_bitcast_fusion), channel_id=1, source_target_pairs={{0,8},{8,0},{16,24},{24,16},{1,9},{9,1},{17,25},{25,17},{2,10},{10... | collective-permute-start | bytes 98312 | tf_op jit(solution)/shard_map/ppermute | solution.py:16

commit v7 on v6

--- a/solution.py
+++ b/solution.py
@@ -47,10 +47,30 @@
     return share if rest == LANES and share * arrays <= LANES and share * planes == rest else 0
 
 
+def far_kernel(far, planes, count, *refs):
+    pieces, ends, message = refs[:count], refs[count:-1], refs[-1]
+    width = pieces[0].shape[1]
+    for index, ref in enumerate(pieces):
+        message[:, index * width : (index + 1) * width] = ref[...]
+    tile = shared_tile([end[...] for end in ends], lax.axis_index("hrow") ^ far, ends[0].shape[1] // planes)
+    message[:, count * width :] = tile.astype(message.dtype)
+
+
+def shared_tile(ends, plane, share):
+    spot = lax.broadcasted_iota(jnp.int32, ends[0].shape, 1)
+    tile = jnp.zeros(ends[0].shape, jnp.float32)
+    for index, end in enumerate(ends):
+        shift = lax.rem(index * share + LANES - plane * share, LANES)
+        inside = (spot >= index * share) & (spot < (index + 1) * share)
+        tile = jnp.where(inside, pltpu.roll(end.astype(jnp.float32), shift, 1), tile)
+    return tile
+
+
 def cut_kernel(width, planes, masks, counts, tail_at, *refs):
-    arrays = list(refs[: len(refs) - len(masks) - 1])
-    *messages, sems = refs[len(arrays) :]
-    rows, grid = arrays[0].shape
+    wholes = refs[: len(refs) - len(masks) - 1]
+    *messages, sems = refs[len(wholes) :]
+    rows, grid = messages[0].shape[0], wholes[0].shape[1]
+    arrays = [ref.at[pl.ds(at, rows)] for ref in wholes for at in range(0, ref.shape[0], rows)]
     rest = grid - width * planes
     share = packed_share(planes, len(arrays), rest)
     z = lax.axis_index("hrow")
@@ -70,14 +90,9 @@
             for index, source in enumerate(last):
                 copy(source, grid - rest, rest, message, count * width + index * rest)
     if tail_at is not None and share:
-        spot = lax.broadcasted_iota(jnp.int32, (rows, LANES), 1)
-        tails = [source[:, grid - rest :].astype(jnp.float32) for source in arrays]
+        ends = [source[:, grid - rest :] for source in arrays]
         for message, mask, count in zip(messages, masks, counts):
-            tile = jnp.zeros((rows, LANES), jnp.float32)
-            for index, tail in enumerate(tails):
-                shift = lax.rem(index * share + LANES - (z ^ mask) * share, LANES)
-                inside = (spot >= index * share) & (spot < (index + 1) * share)
-                tile = jnp.where(inside, pltpu.roll(tail, shift, 1), tile)
+            tile = shared_tile(ends, z ^ mask, share)
             message[:, count * width : count * width + LANES] = tile.astype(message.dtype)
     for one in copies:
         one.wait()
@@ -226,14 +241,14 @@
         def columns(m, count):
             if tail_at is None or share:
                 return count * width + (0 if tail_at is None else LANES)
-            return count * width + (len(arrays) if m == 0 else len(arrays) - tail_at) * rest
+            return count * width + (outputs + shocks if m == 0 else outputs + shocks - tail_at) * rest
 
         return call(
             functools.partial(cut_kernel, width, planes, sent, counts, tail_at),
             name,
             [jax.ShapeDtypeStruct((rows, columns(m, count)), expect.dtype) for m, count in zip(sent, counts)],
             arrays,
-            [pltpu.SemaphoreType.DMA((sum(counts) + len(sent) * len(arrays),))],
+            [pltpu.SemaphoreType.DMA((sum(counts) + len(sent) * (outputs + shocks),))],
         )
 
     def to_planes(messages, sent):
@@ -270,10 +285,26 @@
 
     group = range(FIRST)
     rest_group = range(FIRST, shocks)
+    some = outputs + len(group)
+    counts = [outputs + shocks] + [some] * (planes - 1)
+    sent = list(range(planes))
+    alone = []
     arrays = [expect[o] for o in range(outputs)] + [distrib[s] for s in range(shocks)]
-    some = outputs + len(group)
-    counts = [len(arrays)] + [some] * (planes - 1)
-    first = to_planes(cut("cut_0", arrays, range(planes), counts, outputs), range(planes))
+    if share:
+        far = sent.pop()
+        begin = (z ^ far) * width
+        message = call(
+            functools.partial(far_kernel, far, planes, some),
+            "cut_far",
+            jax.ShapeDtypeStruct((rows, some * width + rest), expect.dtype),
+            [lax.dynamic_slice_in_dim(one, begin, width, 1) for one in arrays[:some]]
+            + [one[:, grid - rest :] for one in arrays],
+        )
+        expect, distrib, message = lax.optimization_barrier((expect, distrib, message))
+        alone = [message]
+    arrays = [expect[o] for o in range(outputs)] + [distrib[s] for s in range(shocks)]
+    whole = [expect.reshape(outputs * rows, grid)] + arrays[outputs:]
+    first = to_planes([*cut("cut_0", whole, sent, counts[: len(sent)], outputs), *alone], range(planes))
     if rest_group:
         later = cut("cut_1", arrays[some:], masks, [len(rest_group)] * len(masks))
         later = first[:1] + to_planes(later, masks)

time: 61.1 us -> 60.7 us (level)
  waiting for transfers between devices: 28 us -> 27.3 us
    ppermute x17, waiting for transfers between devices: 28 us -> 27.3 us  [swap(): lax.ppermute(block, axis, [(i, i ^ mask) for i in range(lax.axis_size(axi...]
    squeeze x1 -> x2, local copies, waits for them, and re-layouts: 1.49 us -> 1.34 us  [shards(): distrib[s]]
    pallas_call x4 -> x5, Pallas kernels: 4 us -> 4.05 us  [call(): pl.pallas_call(kernel, name=name, out_shape=out_shape, in_specs=[pl.Block...]
  transfers between devices with their start and end apart: 17 -> 17, of which waited for: 7 -> 7; matrix products, arithmetic and copies ran while one was open for 0% -> 1% of each run, Pallas kernels for 5% -> 7%
where the time goes in v7:
time: 60.7 us; the launch traced here: 60.5 us
  waiting for transfers between devices  27.3 us (45%)
  starting transfers between devices  26.1 us (43%)
  Pallas kernels  4.05 us (7%)
  local copies, waits for them, and re-layouts  1.88 us (3%)
  other arithmetic  0.9 us (1%)
    ppermute x17, waiting for transfers between devices, swap(): lax.ppermute(block, axis, [(i, i ^ mask) for i in range(lax.axis_size(axi...  27.3 us
    ppermute x17, starting transfers between devices, swap(): lax.ppermute(block, axis, [(i, i ^ mask) for i in range(lax.axis_size(axi...  26.1 us
    pallas_call x5, Pallas kernels, call(): pl.pallas_call(kernel, name=name, out_shape=out_shape, in_specs=[pl.Block...  4.05 us
    squeeze x2, local copies, waits for them, and re-layouts, shards(): distrib[s]  1.34 us
  transfers between devices with their start and end apart: 17, of which 7 were waited for; matrix products, arithmetic and copies ran while one was open for 1% of the time, Pallas kernels for 7%

profile of v7, /device:TPU:0, one launch (start us, length us, event | category | flops | bytes accessed | tf_op | source)
XLA Modules:
  0.0 60.5 jit_solution(10620012295695456858)
XLA Ops:
  0.0 1.3 %slice_bitcast_fusion.2 = (bf16[64,3200]{1,0:T(8,128)(2,1)S(1)}, bf16[64,3200]{1,0:T(8,128)(2,1)S(1)}, bf16[1,64,3200]{2,1,0:T(8,128)(2,1)S(1)}) fusion(bf16[2,64,3200]{2,1,0:T(8,128)(2,1)} %param.5), kind=kLoop, calls=%fused_computation.2 | loop fusion | bytes 2048000 | tf_op jit(solution)/shard_map/squeeze | solution.py:292
  1.4 0.1 slice_bitcast_fusion.8
  1.6 0.1 cut_far.1
  1.7 5.1 %collective-permute-start = (bf16[64,2432]{1,0:T(8,128)(2,1)S(1)}, bf16[64,2432]{1,0:T(8,128)(2,1)S(1)}, u32[]{:S(2)}, u32[]{:S(2)}) collective-permute-start(bf16[64,2432]{1,0:T(8,128)(2,1)S(1)} %cut_far.1), channel_id=1, source_target_pairs={{0,24},{8,16},{16,8},{24,0},{1,25},{9,17},{17,9},{25,1},{2,26},{10... | collective-permute-start | bytes 933896 | tf_op jit(solution)/shard_map/ppermute | solution.py:16
  6.9 0.5 cut_0.1
  7.5 1.4 %collective-permute-start.2 = (bf16[64,2432]{1,0:T(8,128)(2,1)S(1)}, bf16[64,2432]{1,0:T(8,128)(2,1)S(1)}, u32[]{:S(2)}, u32[]{:S(2)}) collective-permute-start(bf16[64,2432]{1,0:T(8,128)(2,1)S(1)} %get-tuple-element.24), channel_id=1, source_target_pairs={{0,8},{8,0},{16,24},{24,16},{1,9},{9,1},{17,25},{25,17},{2,10},{10... | collective-permute-start | bytes 933896 | tf_op jit(solution)/shard_map/ppermute | solution.py:16
  8.9 0.2 cut_1.1
  9.1 0.7 %collective-permute-start.4 = (bf16[64,768]{1,0:T(8,128)(2,1)S(1)}, bf16[64,768]{1,0:T(8,128)(2,1)S(1)}, u32[]{:S(2)}, u32[]{:S(2)}) collective-permute-start(bf16[64,768]{1,0:T(8,128)(2,1)S(1)} %get-tuple-element.30), channel_id=1, source_target_pairs={{0,8},{8,0},{16,24},{24,16},{1,9},{9,1},{17,25},{25,17},{2,10},{10... | collective-permute-start | bytes 294920 | tf_op jit(solution)/shard_map/ppermute | solution.py:16
  9.8 2.8 %collective-permute-start.5 = (bf16[64,768]{1,0:T(8,128)(2,1)S(1)}, bf16[64,768]{1,0:T(8,128)(2,1)S(1)}, u32[]{:S(2)}, u32[]{:S(2)}) collective-permute-start(bf16[64,768]{1,0:T(8,128)(2,1)S(1)} %get-tuple-element.31), channel_id=1, source_target_pairs={{0,16},{8,24},{16,0},{24,8},{1,17},{9,25},{17,1},{25,9},{2,18},{10... | collective-permute-start | bytes 294920 | tf_op jit(solution)/shard_map/ppermute | solution.py:16
  12.7 0.1 copy.5.direct_ref
  12.8 2.4 %collective-permute-done.refs_0_ = bf16[64,2432]{1,0:T(8,128)(2,1)S(1)} collective-permute-done((bf16[64,2432]{1,0:T(8,128)(2,1)S(1)}, bf16[64,2432]{1,0:T(8,128)(2,1)S(1)}, u32[]{:S(2)}, u32[]{:S(2)}) %collective-permute-start) | collective-permute-done | bytes 311328 | tf_op jit(solution)/shard_map/ppermute | solution.py:16
  15.2 3.8 %collective-permute-start.6 = (bf16[64,768]{1,0:T(8,128)(2,1)S(1)}, bf16[64,768]{1,0:T(8,128)(2,1)S(1)}, u32[]{:S(2)}, u32[]{:S(2)}) collective-permute-start(bf16[64,768]{1,0:T(8,128)(2,1)S(1)} %get-tuple-element.32), channel_id=1, source_target_pairs={{0,24},{8,16},{16,8},{24,0},{1,25},{9,17},{17,9},{25,1},{2,26},{10... | collective-permute-start | bytes 294920 | tf_op jit(solution)/shard_map/ppermute | solution.py:16
  19.0 19.6 %collective-permute-done.1.refs_1_ = bf16[64,2432]{1,0:T(8,128)(2,1)S(1)} collective-permute-done((bf16[64,2432]{1,0:T(8,128)(2,1)S(1)}, bf16[64,2432]{1,0:T(8,128)(2,1)S(1)}, u32[]{:S(2)}, u32[]{:S(2)}) %collective-permute-start.1) | collective-permute-done | bytes 311328 | tf_op jit(solution)/shard_map/ppermute | solution.py:16
  38.5 1.7 %partial_0.1 = (bf16[2,256,896]{2,1,0:T(8,128)(2,1)S(1)}, bf16[2,256,128]{2,1,0:T(8,128)(2,1)S(1)}, f32[4,4,1,32,128]{4,3,2,1,0:T(8,128)S(1)}, f32[4,4,1,32,128]{4,3,2,1,0:T(8,128)S(1)}) custom-call(f32[4,32,1]{2,1,0:T(8,128)S(1)} %copy.5.direct_ref, bf16[64,2432]{1,0:T(8,128)(2,1)S(1)} %collective-permute-done.refs_0_, ...), custom_call_target="tpu_custom_call" | custom-call | flops 234881024 | bytes 2981888 | tf_op jit(solution)/shard_map/partial_0/pallas_call | solution.py:211
  40.3 0.3 collective-permute-done.5.refs_2_
  40.6 1.5 %partial_1.1 = (f32[4,4,1,32,128]{4,3,2,1,0:T(8,128)S(1)}, f32[4,4,1,32,128]{4,3,2,1,0:T(8,128)S(1)}) custom-call(f32[4,32,1]{2,1,0:T(8,128)S(1)} %copy.5.direct_ref, bf16[2,256,896]{2,1,0:T(8,128)(2,1)S(1)} %get-tuple-element.28.expect_ref, bf16[2,256,128]{2,1,0:T(8,128)(2,1)S(1)} %get-tuple-element.29.tails_ref, ...), custom_call_target="tpu_custom_call" | custom-call | flops 234881024 | bytes 2342912 | tf_op jit(solution)/shard_map/partial_1/pallas_call | solution.py:211
  42.2 0.3 collective-permute-start.7
  42.5 1.2 %collective-permute-done.7 = f32[4,4,1,32,128]{4,3,2,1,0:T(8,128)S(1)} collective-permute-done((f32[4,4,1,32,128]{4,3,2,1,0:T(8,128)S(1)}, f32[4,4,1,32,128]{4,3,2,1,0:T(8,128)S(1)}, u32[]{:S(2)}, u32[]{:S(2)}) %collective-permute-start.7) | collective-permute-done | bytes 262176 | tf_op jit(solution)/shard_map/ppermute | solution.py:16
  43.9 2.5 %collective-permute-start.8 = (f32[2,2,32,128]{3,2,0,1:T(8,128)S(1)}, f32[2,2,32,128]{3,2,0,1:T(8,128)S(1)}, u32[]{:S(2)}, u32[]{:S(2)}) collective-permute-start(f32[2,2,32,128]{3,2,0,1:T(8,128)S(1)} %pad_maximum_fusion), channel_id=1, source_target_pairs={{0,6},{1,7},{2,4},{3,5},{4,2},{5,3},{6,0},{7,1},{8,14},{9,15},{10,... | collective-permute-start | bytes 196616 | tf_op jit(solution)/shard_map/ppermute | solution.py:16
  46.4 0.5 collective-permute-start.9
  46.9 0.5 collective-permute-start.10
  47.5 2.5 %collective-permute-start.13 = (f32[2,2,32,128]{3,2,0,1:T(8,128)S(1)}, f32[2,2,32,128]{3,2,0,1:T(8,128)S(1)}, u32[]{:S(2)}, u32[]{:S(2)}) collective-permute-start(f32[2,2,32,128]{3,2,0,1:T(8,128)S(1)} %pad_maximum_fusion.3), channel_id=1, source_target_pairs={{0,6},{1,7},{2,4},{3,5},{4,2},{5,3},{6,0},{7,1},{8,14},{9,15},{10,... | collective-permute-start | bytes 196616 | tf_op jit(solution)/shard_map/ppermute | solution.py:16
  49.9 0.5 collective-permute-start.14
  50.4 0.6 collective-permute-start.15
  51.0 0.7 %collective-permute-done.10 = f32[2,2,32,128]{3,2,0,1:T(8,128)S(1)} collective-permute-done((f32[2,2,32,128]{3,2,0,1:T(8,128)S(1)}, f32[2,2,32,128]{3,2,0,1:T(8,128)S(1)}, u32[]{:S(2)}, u32[]{:S(2)}) %collective-permute-start.10) | collective-permute-done | bytes 65568 | tf_op jit(solution)/shard_map/ppermute | solution.py:16
  51.8 2.7 %collective-permute-start.12 = (f32[2,32,128]{2,1,0:T(8,128)S(1)}, f32[2,32,128]{2,1,0:T(8,128)S(1)}, u32[]{:S(2)}, u32[]{:S(2)}) collective-permute-start(f32[2,32,128]{2,1,0:T(8,128)S(1)} %get-tuple-element.60), channel_id=1, source_target_pairs={{0,24},{8,16},{16,8},{24,0},{1,25},{9,17},{17,9},{25,1},{2,26},{10... | collective-permute-start | bytes 98312 | tf_op jit(solution)/shard_map/ppermute | solution.py:16
  54.5 0.4 collective-permute-start.11
  55.1 1.5 %collective-permute-start.16 = (f32[2,32,128]{2,1,0:T(8,128)S(1)}, f32[2,32,128]{2,1,0:T(8,128)S(1)}, u32[]{:S(2)}, u32[]{:S(2)}) collective-permute-start(f32[2,32,128]{2,1,0:T(8,128)S(1)} %dynamic-slice_bitcast_fusion.3), channel_id=1, source_target_pairs={{0,8},{8,0},{16,24},{24,16},{1,9},{9,1},{17,25},{25,17},{2,10},{10... | collective-permute-start | bytes 98312 | tf_op jit(solution)/shard_map/ppermute | solution.py:16
  56.6 1.0 %collective-permute-done.12 = f32[2,32,128]{2,1,0:T(8,128)S(1)} collective-permute-done((f32[2,32,128]{2,1,0:T(8,128)S(1)}, f32[2,32,128]{2,1,0:T(8,128)S(1)}, u32[]{:S(2)}, u32[]{:S(2)}) %collective-permute-start.12) | collective-permute-done | bytes 32800 | tf_op jit(solution)/shard_map/ppermute | solution.py:16
  57.6 2.1 %collective-permute-done.11 = f32[2,32,128]{2,1,0:T(8,128)S(1)} collective-permute-done((f32[2,32,128]{2,1,0:T(8,128)S(1)}, f32[2,32,128]{2,1,0:T(8,128)S(1)}, u32[]{:S(2)}, u32[]{:S(2)}) %collective-permute-start.11) | collective-permute-done | bytes 32800 | tf_op jit(solution)/shard_map/ppermute | solution.py:16
  59.7 0.1 slice_bitcast_fusion.6
  59.8 0.7 %select_select_fusion = f32[4,64,32]{1,2,0:T(8,128)} fusion(f32[64,32]{0,1:T(8,128)S(1)} %get-tuple-element.63, f32[64,32]{0,1:T(8,128)S(1)} %get-tuple-element.64, f32[64,32]{0,1:T(8,128)S(1)} %get-tuple-element.65, f32[64,32]{0,1:T(8,128)S(1)} %get-tuple-element.62, pred[4]{0:T(512)(128)(4,1)S(1)} %get-tuple-element.67, ...), kind=kLoop, calls=%fused_computation.18 | loop fusion | flops 32768 | bytes 65552 | tf_op jit(solution)/shard_map/jit(_where)/select_n | solution.py:350
  (44 shorter events, 0.6 us)
Async XLA Ops:
  0.0 1.4 %copy-start = (bf16[2,64,3200]{2,1,0:T(8,128)(2,1)S(1)}, bf16[2,64,3200]{2,1,0:T(8,128)(2,1)}, u32[]{:S(2)}) copy-start(bf16[2,64,3200]{2,1,0:T(8,128)(2,1)} %param.4) | copy-start | bytes 2457604
  1.5 5.3 %copy-start.1 = (bf16[2,64,3200]{2,1,0:T(8,128)(2,1)S(1)}, bf16[2,64,3200]{2,1,0:T(8,128)(2,1)}, u32[]{:S(2)}) copy-start(bf16[2,64,3200]{2,1,0:T(8,128)(2,1)} %param.5) | copy-start | bytes 2457604
  1.7 13.4 %collective-permute-start = (bf16[64,2432]{1,0:T(8,128)(2,1)S(1)}, bf16[64,2432]{1,0:T(8,128)(2,1)S(1)}, u32[]{:S(2)}, u32[]{:S(2)}) collective-permute-start(bf16[64,2432]{1,0:T(8,128)(2,1)S(1)} %cut_far.1), channel_id=1, source_target_pairs={{0,24},{8,16},{16,8},{24,0},{1,25},{9,17},{17,9},{25,1},{2,26},{10... | collective-permute-start | bytes 933896 | tf_op jit(solution)/shard_map/ppermute | solution.py:16
  7.4 31.1 %collective-permute-start.1 = (bf16[64,2432]{1,0:T(8,128)(2,1)S(1)}, bf16[64,2432]{1,0:T(8,128)(2,1)S(1)}, u32[]{:S(2)}, u32[]{:S(2)}) collective-permute-start(bf16[64,2432]{1,0:T(8,128)(2,1)S(1)} %get-tuple-element.23), channel_id=1, source_target_pairs={{0,16},{8,24},{16,0},{24,8},{1,17},{9,25},{17,1},{25,9},{2,18},{10... | collective-permute-start | bytes 933896 | tf_op jit(solution)/shard_map/ppermute | solution.py:16
  7.5 31.0 %collective-permute-start.2 = (bf16[64,2432]{1,0:T(8,128)(2,1)S(1)}, bf16[64,2432]{1,0:T(8,128)(2,1)S(1)}, u32[]{:S(2)}, u32[]{:S(2)}) collective-permute-start(bf16[64,2432]{1,0:T(8,128)(2,1)S(1)} %get-tuple-element.24), channel_id=1, source_target_pairs={{0,8},{8,0},{16,24},{24,16},{1,9},{9,1},{17,25},{25,17},{2,10},{10... | collective-permute-start | bytes 933896 | tf_op jit(solution)/shard_map/ppermute | solution.py:16
  9.1 3.6 %copy-start.2 = (f32[2,2,32]{2,1,0:T(2,128)S(1)}, f32[2,2,32]{2,1,0:T(2,128)}, u32[]{:S(2)}) copy-start(f32[2,2,32]{2,1,0:T(2,128)} %param.6) | copy-start | bytes 1540
  9.1 31.2 %collective-permute-start.4 = (bf16[64,768]{1,0:T(8,128)(2,1)S(1)}, bf16[64,768]{1,0:T(8,128)(2,1)S(1)}, u32[]{:S(2)}, u32[]{:S(2)}) collective-permute-start(bf16[64,768]{1,0:T(8,128)(2,1)S(1)} %get-tuple-element.30), channel_id=1, source_target_pairs={{0,8},{8,0},{16,24},{24,16},{1,9},{9,1},{17,25},{25,17},{2,10},{10... | collective-permute-start | bytes 294920 | tf_op jit(solution)/shard_map/ppermute | solution.py:16
  9.8 30.8 %collective-permute-start.5 = (bf16[64,768]{1,0:T(8,128)(2,1)S(1)}, bf16[64,768]{1,0:T(8,128)(2,1)S(1)}, u32[]{:S(2)}, u32[]{:S(2)}) collective-permute-start(bf16[64,768]{1,0:T(8,128)(2,1)S(1)} %get-tuple-element.31), channel_id=1, source_target_pairs={{0,16},{8,24},{16,0},{24,8},{1,17},{9,25},{17,1},{25,9},{2,18},{10... | collective-permute-start | bytes 294920 | tf_op jit(solution)/shard_map/ppermute | solution.py:16
  15.2 25.5 %collective-permute-start.6 = (bf16[64,768]{1,0:T(8,128)(2,1)S(1)}, bf16[64,768]{1,0:T(8,128)(2,1)S(1)}, u32[]{:S(2)}, u32[]{:S(2)}) collective-permute-start(bf16[64,768]{1,0:T(8,128)(2,1)S(1)} %get-tuple-element.32), channel_id=1, source_target_pairs={{0,24},{8,16},{16,8},{24,0},{1,25},{9,17},{17,9},{25,1},{2,26},{10... | collective-permute-start | bytes 294920 | tf_op jit(solution)/shard_map/ppermute | solution.py:16
  40.2 2.2 %collective-permute-start.3 = (f32[4,4,1,32,128]{4,3,2,1,0:T(8,128)S(1)}, f32[4,4,1,32,128]{4,3,2,1,0:T(8,128)S(1)}, u32[]{:S(2)}, u32[]{:S(2)}) collective-permute-start(f32[4,4,1,32,128]{4,3,2,1,0:T(8,128)S(1)} %get-tuple-element.27), channel_id=1, source_target_pairs={{0,1},{1,0},{2,3},{3,2},{4,5},{5,4},{6,7},{7,6},{8,9},{9,8},{10,11... | collective-permute-start | bytes 786440 | tf_op jit(solution)/shard_map/ppermute | solution.py:16
  42.2 1.6 %collective-permute-start.7 = (f32[4,4,1,32,128]{4,3,2,1,0:T(8,128)S(1)}, f32[4,4,1,32,128]{4,3,2,1,0:T(8,128)S(1)}, u32[]{:S(2)}, u32[]{:S(2)}) collective-permute-start(f32[4,4,1,32,128]{4,3,2,1,0:T(8,128)S(1)} %get-tuple-element.34), channel_id=1, source_target_pairs={{0,1},{1,0},{2,3},{3,2},{4,5},{5,4},{6,7},{7,6},{8,9},{9,8},{10,11... | collective-permute-start | bytes 786440 | tf_op jit(solution)/shard_map/ppermute | solution.py:16
  43.9 6.5 %collective-permute-start.8 = (f32[2,2,32,128]{3,2,0,1:T(8,128)S(1)}, f32[2,2,32,128]{3,2,0,1:T(8,128)S(1)}, u32[]{:S(2)}, u32[]{:S(2)}) collective-permute-start(f32[2,2,32,128]{3,2,0,1:T(8,128)S(1)} %pad_maximum_fusion), channel_id=1, source_target_pairs={{0,6},{1,7},{2,4},{3,5},{4,2},{5,3},{6,0},{7,1},{8,14},{9,15},{10,... | collective-permute-start | bytes 196616 | tf_op jit(solution)/shard_map/ppermute | solution.py:16
  46.4 4.6 %collective-permute-start.9 = (f32[2,2,32,128]{3,2,0,1:T(8,128)S(1)}, f32[2,2,32,128]{3,2,0,1:T(8,128)S(1)}, u32[]{:S(2)}, u32[]{:S(2)}) collective-permute-start(f32[2,2,32,128]{3,2,0,1:T(8,128)S(1)} %pad_maximum_fusion.1), channel_id=1, source_target_pairs={{0,4},{1,5},{2,6},{3,7},{4,0},{5,1},{6,2},{7,3},{8,12},{9,13},{10,... | collective-permute-start | bytes 196616 | tf_op jit(solution)/shard_map/ppermute | solution.py:16
  46.9 4.9 %collective-permute-start.10 = (f32[2,2,32,128]{3,2,0,1:T(8,128)S(1)}, f32[2,2,32,128]{3,2,0,1:T(8,128)S(1)}, u32[]{:S(2)}, u32[]{:S(2)}) collective-permute-start(f32[2,2,32,128]{3,2,0,1:T(8,128)S(1)} %pad_maximum_fusion.2), channel_id=1, source_target_pairs={{0,2},{1,3},{2,0},{3,1},{4,6},{5,7},{6,4},{7,5},{8,10},{9,11},{10,... | collective-permute-start | bytes 196616 | tf_op jit(solution)/shard_map/ppermute | solution.py:16
  47.5 7.5 %collective-permute-start.13 = (f32[2,2,32,128]{3,2,0,1:T(8,128)S(1)}, f32[2,2,32,128]{3,2,0,1:T(8,128)S(1)}, u32[]{:S(2)}, u32[]{:S(2)}) collective-permute-start(f32[2,2,32,128]{3,2,0,1:T(8,128)S(1)} %pad_maximum_fusion.3), channel_id=1, source_target_pairs={{0,6},{1,7},{2,4},{3,5},{4,2},{5,3},{6,0},{7,1},{8,14},{9,15},{10,... | collective-permute-start | bytes 196616 | tf_op jit(solution)/shard_map/ppermute | solution.py:16
  49.9 5.1 %collective-permute-start.14 = (f32[2,2,32,128]{3,2,0,1:T(8,128)S(1)}, f32[2,2,32,128]{3,2,0,1:T(8,128)S(1)}, u32[]{:S(2)}, u32[]{:S(2)}) collective-permute-start(f32[2,2,32,128]{3,2,0,1:T(8,128)S(1)} %pad_maximum_fusion.4), channel_id=1, source_target_pairs={{0,4},{1,5},{2,6},{3,7},{4,0},{5,1},{6,2},{7,3},{8,12},{9,13},{10,... | collective-permute-start | bytes 196616 | tf_op jit(solution)/shard_map/ppermute | solution.py:16
  50.4 4.6 %collective-permute-start.15 = (f32[2,2,32,128]{3,2,0,1:T(8,128)S(1)}, f32[2,2,32,128]{3,2,0,1:T(8,128)S(1)}, u32[]{:S(2)}, u32[]{:S(2)}) collective-permute-start(f32[2,2,32,128]{3,2,0,1:T(8,128)S(1)} %pad_maximum_fusion.5), channel_id=1, source_target_pairs={{0,2},{1,3},{2,0},{3,1},{4,6},{5,7},{6,4},{7,5},{8,10},{9,11},{10,... | collective-permute-start | bytes 196616 | tf_op jit(solution)/shard_map/ppermute | solution.py:16
  51.8 5.8 %collective-permute-start.12 = (f32[2,32,128]{2,1,0:T(8,128)S(1)}, f32[2,32,128]{2,1,0:T(8,128)S(1)}, u32[]{:S(2)}, u32[]{:S(2)}) collective-permute-start(f32[2,32,128]{2,1,0:T(8,128)S(1)} %get-tuple-element.60), channel_id=1, source_target_pairs={{0,24},{8,16},{16,8},{24,0},{1,25},{9,17},{17,9},{25,1},{2,26},{10... | collective-permute-start | bytes 98312 | tf_op jit(solution)/shard_map/ppermute | solution.py:16
  54.5 5.2 %collective-permute-start.11 = (f32[2,32,128]{2,1,0:T(8,128)S(1)}, f32[2,32,128]{2,1,0:T(8,128)S(1)}, u32[]{:S(2)}, u32[]{:S(2)}) collective-permute-start(f32[2,32,128]{2,1,0:T(8,128)S(1)} %get-tuple-element.61), channel_id=1, source_target_pairs={{0,16},{8,24},{16,0},{24,8},{1,17},{9,25},{17,1},{25,9},{2,18},{10... | collective-permute-start | bytes 98312 | tf_op jit(solution)/shard_map/ppermute | solution.py:16
  55.0 1.6 %copy-start.3 = (s32[4,2]{0,1:T(2,128)S(1)}, s32[4,2]{0,1:T(2,128)}, u32[]{:S(2)}) copy-start(s32[4,2]{0,1:T(2,128)} %param.7) | copy-start | bytes 100
  55.1 4.7 %collective-permute-start.16 = (f32[2,32,128]{2,1,0:T(8,128)S(1)}, f32[2,32,128]{2,1,0:T(8,128)S(1)}, u32[]{:S(2)}, u32[]{:S(2)}) collective-permute-start(f32[2,32,128]{2,1,0:T(8,128)S(1)} %dynamic-slice_bitcast_fusion.3), channel_id=1, source_target_pairs={{0,8},{8,0},{16,24},{24,16},{1,9},{9,1},{17,25},{25,17},{2,10},{10... | collective-permute-start | bytes 98312 | tf_op jit(solution)/shard_map/ppermute | solution.py:16

commit v8 on v7

--- a/solution.py
+++ b/solution.py
@@ -98,9 +98,10 @@
         one.wait()
 
 
-def partial_sums(shocks, expect_ref, direct_ref, keep_ref, give_ref, responses, products):
+def partial_sums(shocks, expect_ref, direct_ref, parts, responses, products):
     outputs, horizon = products.shape[:2]
-    chips, planes, _, half, lanes = keep_ref.shape
+    chips, near, _, half, lanes = parts[0].shape
+    planes = 2 * near
     width = lanes // outputs
     step = min(horizon, 256)
     z = lax.axis_index("hrow")
@@ -132,15 +133,20 @@
                     block = block + jnp.where(date_id > row_id, moved, 0.0)
                 last[output] = block[step - 1 :]
                 blocks.append(block)
+            both = []
             for plane in range(planes):
                 dates = slice(plane * width, (plane + 1) * width)
-                both = jnp.concatenate([block[:, dates] for block in blocks], axis=1)
-                for part in range(step // (2 * half)):
-                    low = both[2 * part * half : (2 * part + 1) * half]
-                    high = both[(2 * part + 1) * half : (2 * part + 2) * half]
-                    chip = start // (2 * half) + part
-                    keep_ref[chip, plane, index] = jnp.where(core == 0, low, high)
-                    give_ref[chip, plane, index] = jnp.where(core == 0, high, low)
+                both.append(jnp.concatenate([block[:, dates] for block in blocks], axis=1))
+            for plane in range(near):
+                far = jnp.where(z < near, both[near + plane], both[plane])
+                here = jnp.where(z < near, both[plane], both[near + plane])
+                for side, block in enumerate((far, here)):
+                    for part in range(step // (2 * half)):
+                        low = block[2 * part * half : (2 * part + 1) * half]
+                        high = block[(2 * part + 1) * half : (2 * part + 2) * half]
+                        chip = start // (2 * half) + part
+                        parts[2 * side][chip, plane, index] = jnp.where(core == 0, low, high)
+                        parts[2 * side + 1][chip, plane, index] = jnp.where(core == 0, high, low)
 
 
 def place(z, mask, rows):
@@ -149,7 +155,7 @@
 
 def first_kernel(width, planes, counts, shocks, direct_ref, *refs):
     messages = refs[:planes][::-1]
-    expect_ref, tails_ref, keep_ref, give_ref, responses, products = refs[planes:]
+    expect_ref, tails_ref, *parts, responses, products = refs[planes:]
     outputs = expect_ref.shape[0]
     rows = messages[0].shape[0]
     rest = tails_ref.shape[2]
@@ -184,12 +190,12 @@
                     expect_ref[index - arrays + outputs, spot, width:] = moved
     for index, shock in enumerate(shocks):
         responses[index, :, width:] = tails_ref[shock]
-    partial_sums(shocks, expect_ref, direct_ref, keep_ref, give_ref, responses, products)
+    partial_sums(shocks, expect_ref, direct_ref, parts, responses, products)
 
 
 def next_kernel(width, begins, shocks, direct_ref, expect_ref, tails_ref, *refs):
     messages = refs[: len(begins)]
-    keep_ref, give_ref, responses, products = refs[len(begins) :]
+    *parts, responses, products = refs[len(begins) :]
     rows = messages[0].shape[0]
     z = lax.axis_index("hrow")
     for index, shock in enumerate(shocks):
@@ -197,7 +203,7 @@
             column = begin + index * width
             responses[index, place(z, mask, rows), :width] = ref[:, column : column + width]
         responses[index, :, width:] = tails_ref[shock]
-    partial_sums(shocks, expect_ref, direct_ref, keep_ref, give_ref, responses, products)
+    partial_sums(shocks, expect_ref, direct_ref, parts, responses, products)
 
 
 def size_of(leaf):
@@ -259,11 +265,11 @@
     flat = direct.reshape(shocks * outputs, cols, 1)
 
     def kernel_call(kernel, name, group, arrays, extra=()):
-        part = jax.ShapeDtypeStruct((chips, planes, len(group), cols, outputs * rows), jnp.float32)
+        part = jax.ShapeDtypeStruct((chips, near, len(group), cols, outputs * rows), jnp.float32)
         return call(
             kernel,
             name,
-            (*extra, part, part),
+            (*extra, part, part, part, part),
             arrays,
             [
                 pltpu.VMEM((len(group), horizon, depth), distrib.dtype),
@@ -272,16 +278,15 @@
             flops=2 * len(group) * outputs * horizon * horizon * depth,
         )
 
-    def over_chips(values, begin):
+    def over_cores(far_keep, far_give, near_keep, near_give):
+        return far_keep + swap(far_give, "hcol", 1), near_keep + swap(near_give, "hcol", 1)
+
+    def over_chips(values):
         def block(index):
-            parts = [lax.dynamic_slice_in_dim(value, begin, near, axis=1) for value in values]
-            return jnp.concatenate([lax.dynamic_index_in_dim(part, index, 0, False) for part in parts], axis=1)
+            return jnp.concatenate([lax.dynamic_index_in_dim(one, index, 0, False) for one in values], axis=1)
 
         swaps = [swap(block(chip ^ m), "hcol", 2 * m) for m in range(chips - 1, 0, -1)]
         return functools.reduce(jnp.add, [block(chip)] + swaps)
-
-    def over_cores(keep, give):
-        return keep + swap(give, "hcol", 1)
 
     group = range(FIRST)
     rest_group = range(FIRST, shocks)
@@ -329,9 +334,7 @@
         )
         sums.append(over_cores(*parts))
 
-    here = z // near * near
-    far_sum = over_chips(sums, planes - near - here)
-    near_sum = over_chips(sums, here)
+    far_sum, near_sum = (over_chips(values) for values in zip(*sums))
 
     def of_plane(m):
         return lax.dynamic_index_in_dim(far_sum if m >= near else near_sum, (z ^ m) % near, 0, False)

time: 60.7 us -> 60.3 us (level)
  waiting for transfers between devices: 27.3 us -> 26.1 us
  starting transfers between devices: 26.1 us -> 26.9 us
    ppermute x17 -> x19, waiting for transfers between devices: 27.3 us -> 26.1 us  [swap(): lax.ppermute(block, axis, [(i, i ^ mask) for i in range(lax.axis_size(axi...]
    ppermute x17 -> x19, starting transfers between devices: 26.1 us -> 26.9 us  [swap(): lax.ppermute(block, axis, [(i, i ^ mask) for i in range(lax.axis_size(axi...]
  transfers between devices with their start and end apart: 17 -> 19, of which waited for: 7 -> 8; matrix products, arithmetic and copies ran while one was open for 1% -> 1% of each run, Pallas kernels for 7% -> 7%
where the time goes in v8:
time: 60.3 us; the launch traced here: 60.1 us
  starting transfers between devices  26.9 us (45%)
  waiting for transfers between devices  26.1 us (43%)
  Pallas kernels  4.05 us (7%)
  local copies, waits for them, and re-layouts  1.89 us (3%)
  other arithmetic  0.9 us (1%)
    ppermute x19, starting transfers between devices, swap(): lax.ppermute(block, axis, [(i, i ^ mask) for i in range(lax.axis_size(axi...  26.9 us
    ppermute x19, waiting for transfers between devices, swap(): lax.ppermute(block, axis, [(i, i ^ mask) for i in range(lax.axis_size(axi...  26.1 us
    pallas_call x5, Pallas kernels, call(): pl.pallas_call(kernel, name=name, out_shape=out_shape, in_specs=[pl.Block...  4.05 us
    squeeze x2, local copies, waits for them, and re-layouts, shards(): distrib[s]  1.34 us
  transfers between devices with their start and end apart: 19, of which 8 were waited for; matrix products, arithmetic and copies ran while one was open for 1% of the time, Pallas kernels for 7%

profile of v8, /device:TPU:0, one launch (start us, length us, event | category | flops | bytes accessed | tf_op | source)
XLA Modules:
  0.0 60.1 jit_solution(12457454782358209619)
XLA Ops:
  0.0 1.3 %slice_bitcast_fusion.2 = (bf16[64,3200]{1,0:T(8,128)(2,1)S(1)}, bf16[64,3200]{1,0:T(8,128)(2,1)S(1)}, bf16[1,64,3200]{2,1,0:T(8,128)(2,1)S(1)}) fusion(bf16[2,64,3200]{2,1,0:T(8,128)(2,1)} %param.5), kind=kLoop, calls=%fused_computation.2 | loop fusion | bytes 2048000 | tf_op jit(solution)/shard_map/squeeze | solution.py:297
  1.4 0.1 slice_bitcast_fusion.8
  1.7 5.1 %collective-permute-start = (bf16[64,2432]{1,0:T(8,128)(2,1)S(1)}, bf16[64,2432]{1,0:T(8,128)(2,1)S(1)}, u32[]{:S(2)}, u32[]{:S(2)}) collective-permute-start(bf16[64,2432]{1,0:T(8,128)(2,1)S(1)} %cut_far.1), channel_id=1, source_target_pairs={{0,24},{8,16},{16,8},{24,0},{1,25},{9,17},{17,9},{25,1},{2,26},{10... | collective-permute-start | bytes 933896 | tf_op jit(solution)/shard_map/ppermute | solution.py:16
  6.9 0.5 cut_0.1
  7.5 1.4 %collective-permute-start.2 = (bf16[64,2432]{1,0:T(8,128)(2,1)S(1)}, bf16[64,2432]{1,0:T(8,128)(2,1)S(1)}, u32[]{:S(2)}, u32[]{:S(2)}) collective-permute-start(bf16[64,2432]{1,0:T(8,128)(2,1)S(1)} %get-tuple-element.28), channel_id=1, source_target_pairs={{0,8},{8,0},{16,24},{24,16},{1,9},{9,1},{17,25},{25,17},{2,10},{10... | collective-permute-start | bytes 933896 | tf_op jit(solution)/shard_map/ppermute | solution.py:16
  8.9 0.2 cut_1.1
  9.1 0.7 %collective-permute-start.4 = (bf16[64,768]{1,0:T(8,128)(2,1)S(1)}, bf16[64,768]{1,0:T(8,128)(2,1)S(1)}, u32[]{:S(2)}, u32[]{:S(2)}) collective-permute-start(bf16[64,768]{1,0:T(8,128)(2,1)S(1)} %get-tuple-element.34), channel_id=1, source_target_pairs={{0,8},{8,0},{16,24},{24,16},{1,9},{9,1},{17,25},{25,17},{2,10},{10... | collective-permute-start | bytes 294920 | tf_op jit(solution)/shard_map/ppermute | solution.py:16
  9.8 2.8 %collective-permute-start.5 = (bf16[64,768]{1,0:T(8,128)(2,1)S(1)}, bf16[64,768]{1,0:T(8,128)(2,1)S(1)}, u32[]{:S(2)}, u32[]{:S(2)}) collective-permute-start(bf16[64,768]{1,0:T(8,128)(2,1)S(1)} %get-tuple-element.35), channel_id=1, source_target_pairs={{0,16},{8,24},{16,0},{24,8},{1,17},{9,25},{17,1},{25,9},{2,18},{10... | collective-permute-start | bytes 294920 | tf_op jit(solution)/shard_map/ppermute | solution.py:16
  12.8 2.4 %collective-permute-done.refs_0_ = bf16[64,2432]{1,0:T(8,128)(2,1)S(1)} collective-permute-done((bf16[64,2432]{1,0:T(8,128)(2,1)S(1)}, bf16[64,2432]{1,0:T(8,128)(2,1)S(1)}, u32[]{:S(2)}, u32[]{:S(2)}) %collective-permute-start) | collective-permute-done | bytes 311328 | tf_op jit(solution)/shard_map/ppermute | solution.py:16
  15.2 3.8 %collective-permute-start.6 = (bf16[64,768]{1,0:T(8,128)(2,1)S(1)}, bf16[64,768]{1,0:T(8,128)(2,1)S(1)}, u32[]{:S(2)}, u32[]{:S(2)}) collective-permute-start(bf16[64,768]{1,0:T(8,128)(2,1)S(1)} %get-tuple-element.36), channel_id=1, source_target_pairs={{0,24},{8,16},{16,8},{24,0},{1,25},{9,17},{17,9},{25,1},{2,26},{10... | collective-permute-start | bytes 294920 | tf_op jit(solution)/shard_map/ppermute | solution.py:16
  19.0 19.6 %collective-permute-done.1.refs_1_ = bf16[64,2432]{1,0:T(8,128)(2,1)S(1)} collective-permute-done((bf16[64,2432]{1,0:T(8,128)(2,1)S(1)}, bf16[64,2432]{1,0:T(8,128)(2,1)S(1)}, u32[]{:S(2)}, u32[]{:S(2)}) %collective-permute-start.1) | collective-permute-done | bytes 311328 | tf_op jit(solution)/shard_map/ppermute | solution.py:16
  38.5 1.7 %partial_0.1 = (bf16[2,256,896]{2,1,0:T(8,128)(2,1)S(1)}, bf16[2,256,128]{2,1,0:T(8,128)(2,1)S(1)}, f32[4,2,1,32,128]{4,3,2,1,0:T(8,128)S(1)}, f32[4,2,1,32,128]...) custom-call(f32[4,32,1]{2,1,0:T(8,128)S(1)} %copy.5.direct_ref, ...), custom_call_target="tpu_custom_call" | custom-call | flops 234881024 | bytes 2981888 | tf_op jit(solution)/shard_map/partial_0/pallas_call | solution.py:217
  40.3 0.3 collective-permute-done.5.refs_2_
  40.6 1.6 %partial_1.1 = (f32[4,2,1,32,128]{4,3,2,1,0:T(8,128)S(1)}, f32[4,2,1,32,128]{4,3,2,1,0:T(8,128)S(1)}, f32[4,2,1,32,128]{4,3,2,1,0:T(8,128)S(1)}, f32[4,2,1,32,128]{4,3,2,1,0:T(8,128)S(1)}) custom-call(f32[4,32,1]{2,1,0:T(8,128)S(1)} %copy.5.direct_ref, bf16[2,256,896]{2,1,0:T(8,128)(2,1)S(1)} %get-tuple-element.32.expect_ref, ...), custom_call_target="tpu_custom_call" | custom-call | flops 234881024 | bytes 2342912 | tf_op jit(solution)/shard_map/partial_1/pallas_call | solution.py:217
  42.2 0.3 collective-permute-start.7
  42.5 0.3 collective-permute-start.14
  42.8 0.2 collective-permute-start.13
  43.0 0.6 collective-permute-done.7
  43.7 2.5 %collective-permute-start.8 = (f32[2,2,32,128]{3,2,0,1:T(8,128)S(1)}, f32[2,2,32,128]{3,2,0,1:T(8,128)S(1)}, u32[]{:S(2)}, u32[]{:S(2)}) collective-permute-start(f32[2,2,32,128]{3,2,0,1:T(8,128)S(1)} %pad_maximum_fusion), channel_id=1, source_target_pairs={{0,6},{1,7},{2,4},{3,5},{4,2},{5,3},{6,0},{7,1},{8,14},{9,15},{10,... | collective-permute-start | bytes 196616 | tf_op jit(solution)/shard_map/ppermute | solution.py:16
  46.2 0.5 collective-permute-start.9
  46.7 0.5 collective-permute-start.10
  47.4 2.5 %collective-permute-start.15 = (f32[2,2,32,128]{3,2,0,1:T(8,128)S(1)}, f32[2,2,32,128]{3,2,0,1:T(8,128)S(1)}, u32[]{:S(2)}, u32[]{:S(2)}) collective-permute-start(f32[2,2,32,128]{3,2,0,1:T(8,128)S(1)} %pad_maximum_fusion.3), channel_id=1, source_target_pairs={{0,6},{1,7},{2,4},{3,5},{4,2},{5,3},{6,0},{7,1},{8,14},{9,15},{10,... | collective-permute-start | bytes 196616 | tf_op jit(solution)/shard_map/ppermute | solution.py:16
  49.9 0.5 collective-permute-start.16
  50.4 0.6 collective-permute-start.17
  51.0 0.6 collective-permute-done.10
  51.6 2.5 %collective-permute-start.12 = (f32[2,32,128]{2,1,0:T(8,128)S(1)}, f32[2,32,128]{2,1,0:T(8,128)S(1)}, u32[]{:S(2)}, u32[]{:S(2)}) collective-permute-start(f32[2,32,128]{2,1,0:T(8,128)S(1)} %get-tuple-element.68), channel_id=1, source_target_pairs={{0,24},{8,16},{16,8},{24,0},{1,25},{9,17},{17,9},{25,1},{2,26},{10... | collective-permute-start | bytes 98312 | tf_op jit(solution)/shard_map/ppermute | solution.py:16
  54.2 0.7 %collective-permute-start.11 = (f32[2,32,128]{2,1,0:T(8,128)S(1)}, f32[2,32,128]{2,1,0:T(8,128)S(1)}, u32[]{:S(2)}, u32[]{:S(2)}) collective-permute-start(f32[2,32,128]{2,1,0:T(8,128)S(1)} %get-tuple-element.69), channel_id=1, source_target_pairs={{0,16},{8,24},{16,0},{24,8},{1,17},{9,25},{17,1},{25,9},{2,18},{10... | collective-permute-start | bytes 98312 | tf_op jit(solution)/shard_map/ppermute | solution.py:16
  55.0 1.6 %collective-permute-start.18 = (f32[2,32,128]{2,1,0:T(8,128)S(1)}, f32[2,32,128]{2,1,0:T(8,128)S(1)}, u32[]{:S(2)}, u32[]{:S(2)}) collective-permute-start(f32[2,32,128]{2,1,0:T(8,128)S(1)} %dynamic-slice_bitcast_fusion.3), channel_id=1, source_target_pairs={{0,8},{8,0},{16,24},{24,16},{1,9},{9,1},{17,25},{25,17},{2,10},{10... | collective-permute-start | bytes 98312 | tf_op jit(solution)/shard_map/ppermute | solution.py:16
  56.6 0.8 %collective-permute-done.12 = f32[2,32,128]{2,1,0:T(8,128)S(1)} collective-permute-done((f32[2,32,128]{2,1,0:T(8,128)S(1)}, f32[2,32,128]{2,1,0:T(8,128)S(1)}, u32[]{:S(2)}, u32[]{:S(2)}) %collective-permute-start.12) | collective-permute-done | bytes 32800 | tf_op jit(solution)/shard_map/ppermute | solution.py:16
  57.4 1.7 %collective-permute-done.11 = f32[2,32,128]{2,1,0:T(8,128)S(1)} collective-permute-done((f32[2,32,128]{2,1,0:T(8,128)S(1)}, f32[2,32,128]{2,1,0:T(8,128)S(1)}, u32[]{:S(2)}, u32[]{:S(2)}) %collective-permute-start.11) | collective-permute-done | bytes 32800 | tf_op jit(solution)/shard_map/ppermute | solution.py:16
  59.1 0.2 collective-permute-done.18
  59.4 0.7 %select_select_fusion = f32[4,64,32]{1,2,0:T(8,128)} fusion(f32[64,32]{0,1:T(8,128)S(1)} %get-tuple-element.71, f32[64,32]{0,1:T(8,128)S(1)} %get-tuple-element.72, f32[64,32]{0,1:T(8,128)S(1)} %get-tuple-element.73, f32[64,32]{0,1:T(8,128)S(1)} %get-tuple-element.70, pred[4]{0:T(512)(128)(4,1)S(1)} %get-tuple-element.75, ...), kind=kLoop, calls=%fused_computation.18 | loop fusion | flops 32768 | bytes 65552 | tf_op jit(solution)/shard_map/jit(_where)/select_n | solution.py:353
  (52 shorter events, 0.9 us)
Async XLA Ops:
  0.0 1.4 %copy-start = (bf16[2,64,3200]{2,1,0:T(8,128)(2,1)S(1)}, bf16[2,64,3200]{2,1,0:T(8,128)(2,1)}, u32[]{:S(2)}) copy-start(bf16[2,64,3200]{2,1,0:T(8,128)(2,1)} %param.4) | copy-start | bytes 2457604
  1.5 5.3 %copy-start.1 = (bf16[2,64,3200]{2,1,0:T(8,128)(2,1)S(1)}, bf16[2,64,3200]{2,1,0:T(8,128)(2,1)}, u32[]{:S(2)}) copy-start(bf16[2,64,3200]{2,1,0:T(8,128)(2,1)} %param.5) | copy-start | bytes 2457604
  1.7 13.4 %collective-permute-start = (bf16[64,2432]{1,0:T(8,128)(2,1)S(1)}, bf16[64,2432]{1,0:T(8,128)(2,1)S(1)}, u32[]{:S(2)}, u32[]{:S(2)}) collective-permute-start(bf16[64,2432]{1,0:T(8,128)(2,1)S(1)} %cut_far.1), channel_id=1, source_target_pairs={{0,24},{8,16},{16,8},{24,0},{1,25},{9,17},{17,9},{25,1},{2,26},{10... | collective-permute-start | bytes 933896 | tf_op jit(solution)/shard_map/ppermute | solution.py:16
  7.4 31.1 %collective-permute-start.1 = (bf16[64,2432]{1,0:T(8,128)(2,1)S(1)}, bf16[64,2432]{1,0:T(8,128)(2,1)S(1)}, u32[]{:S(2)}, u32[]{:S(2)}) collective-permute-start(bf16[64,2432]{1,0:T(8,128)(2,1)S(1)} %get-tuple-element.27), channel_id=1, source_target_pairs={{0,16},{8,24},{16,0},{24,8},{1,17},{9,25},{17,1},{25,9},{2,18},{10... | collective-permute-start | bytes 933896 | tf_op jit(solution)/shard_map/ppermute | solution.py:16
  7.5 31.0 %collective-permute-start.2 = (bf16[64,2432]{1,0:T(8,128)(2,1)S(1)}, bf16[64,2432]{1,0:T(8,128)(2,1)S(1)}, u32[]{:S(2)}, u32[]{:S(2)}) collective-permute-start(bf16[64,2432]{1,0:T(8,128)(2,1)S(1)} %get-tuple-element.28), channel_id=1, source_target_pairs={{0,8},{8,0},{16,24},{24,16},{1,9},{9,1},{17,25},{25,17},{2,10},{10... | collective-permute-start | bytes 933896 | tf_op jit(solution)/shard_map/ppermute | solution.py:16
  9.1 3.6 %copy-start.2 = (f32[2,2,32]{2,1,0:T(2,128)S(1)}, f32[2,2,32]{2,1,0:T(2,128)}, u32[]{:S(2)}) copy-start(f32[2,2,32]{2,1,0:T(2,128)} %param.6) | copy-start | bytes 1540
  9.1 31.2 %collective-permute-start.4 = (bf16[64,768]{1,0:T(8,128)(2,1)S(1)}, bf16[64,768]{1,0:T(8,128)(2,1)S(1)}, u32[]{:S(2)}, u32[]{:S(2)}) collective-permute-start(bf16[64,768]{1,0:T(8,128)(2,1)S(1)} %get-tuple-element.34), channel_id=1, source_target_pairs={{0,8},{8,0},{16,24},{24,16},{1,9},{9,1},{17,25},{25,17},{2,10},{10... | collective-permute-start | bytes 294920 | tf_op jit(solution)/shard_map/ppermute | solution.py:16
  9.8 30.8 %collective-permute-start.5 = (bf16[64,768]{1,0:T(8,128)(2,1)S(1)}, bf16[64,768]{1,0:T(8,128)(2,1)S(1)}, u32[]{:S(2)}, u32[]{:S(2)}) collective-permute-start(bf16[64,768]{1,0:T(8,128)(2,1)S(1)} %get-tuple-element.35), channel_id=1, source_target_pairs={{0,16},{8,24},{16,0},{24,8},{1,17},{9,25},{17,1},{25,9},{2,18},{10... | collective-permute-start | bytes 294920 | tf_op jit(solution)/shard_map/ppermute | solution.py:16
  15.2 25.5 %collective-permute-start.6 = (bf16[64,768]{1,0:T(8,128)(2,1)S(1)}, bf16[64,768]{1,0:T(8,128)(2,1)S(1)}, u32[]{:S(2)}, u32[]{:S(2)}) collective-permute-start(bf16[64,768]{1,0:T(8,128)(2,1)S(1)} %get-tuple-element.36), channel_id=1, source_target_pairs={{0,24},{8,16},{16,8},{24,0},{1,25},{9,17},{17,9},{25,1},{2,26},{10... | collective-permute-start | bytes 294920 | tf_op jit(solution)/shard_map/ppermute | solution.py:16
  40.2 2.7 %collective-permute-start.3 = (f32[4,2,1,32,128]{4,3,2,1,0:T(8,128)S(1)}, f32[4,2,1,32,128]{4,3,2,1,0:T(8,128)S(1)}, u32[]{:S(2)}, u32[]{:S(2)}) collective-permute-start(f32[4,2,1,32,128]{4,3,2,1,0:T(8,128)S(1)} %get-tuple-element.31), channel_id=1, source_target_pairs={{0,1},{1,0},{2,3},{3,2},{4,5},{5,4},{6,7},{7,6},{8,9},{9,8},{10,11... | collective-permute-start | bytes 393224 | tf_op jit(solution)/shard_map/ppermute | solution.py:16
  42.2 1.4 %collective-permute-start.7 = (f32[4,2,1,32,128]{4,3,2,1,0:T(8,128)S(1)}, f32[4,2,1,32,128]{4,3,2,1,0:T(8,128)S(1)}, u32[]{:S(2)}, u32[]{:S(2)}) collective-permute-start(f32[4,2,1,32,128]{4,3,2,1,0:T(8,128)S(1)} %get-tuple-element.38), channel_id=1, source_target_pairs={{0,1},{1,0},{2,3},{3,2},{4,5},{5,4},{6,7},{7,6},{8,9},{9,8},{10,11... | collective-permute-start | bytes 393224 | tf_op jit(solution)/shard_map/ppermute | solution.py:16
  42.5 4.8 %collective-permute-start.14 = (f32[4,2,1,32,128]{4,3,2,1,0:T(8,128)S(1)}, f32[4,2,1,32,128]{4,3,2,1,0:T(8,128)S(1)}, u32[]{:S(2)}, u32[]{:S(2)}) collective-permute-start(f32[4,2,1,32,128]{4,3,2,1,0:T(8,128)S(1)} %get-tuple-element.42), channel_id=1, source_target_pairs={{0,1},{1,0},{2,3},{3,2},{4,5},{5,4},{6,7},{7,6},{8,9},{9,8},{10,11... | collective-permute-start | bytes 393224 | tf_op jit(solution)/shard_map/ppermute | solution.py:16
  42.8 4.5 %collective-permute-start.13 = (f32[4,2,1,32,128]{4,3,2,1,0:T(8,128)S(1)}, f32[4,2,1,32,128]{4,3,2,1,0:T(8,128)S(1)}, u32[]{:S(2)}, u32[]{:S(2)}) collective-permute-start(f32[4,2,1,32,128]{4,3,2,1,0:T(8,128)S(1)} %get-tuple-element.40), channel_id=1, source_target_pairs={{0,1},{1,0},{2,3},{3,2},{4,5},{5,4},{6,7},{7,6},{8,9},{9,8},{10,11... | collective-permute-start | bytes 393224 | tf_op jit(solution)/shard_map/ppermute | solution.py:16
  43.7 6.7 %collective-permute-start.8 = (f32[2,2,32,128]{3,2,0,1:T(8,128)S(1)}, f32[2,2,32,128]{3,2,0,1:T(8,128)S(1)}, u32[]{:S(2)}, u32[]{:S(2)}) collective-permute-start(f32[2,2,32,128]{3,2,0,1:T(8,128)S(1)} %pad_maximum_fusion), channel_id=1, source_target_pairs={{0,6},{1,7},{2,4},{3,5},{4,2},{5,3},{6,0},{7,1},{8,14},{9,15},{10,... | collective-permute-start | bytes 196616 | tf_op jit(solution)/shard_map/ppermute | solution.py:16
  46.2 4.8 %collective-permute-start.9 = (f32[2,2,32,128]{3,2,0,1:T(8,128)S(1)}, f32[2,2,32,128]{3,2,0,1:T(8,128)S(1)}, u32[]{:S(2)}, u32[]{:S(2)}) collective-permute-start(f32[2,2,32,128]{3,2,0,1:T(8,128)S(1)} %pad_maximum_fusion.1), channel_id=1, source_target_pairs={{0,4},{1,5},{2,6},{3,7},{4,0},{5,1},{6,2},{7,3},{8,12},{9,13},{10,... | collective-permute-start | bytes 196616 | tf_op jit(solution)/shard_map/ppermute | solution.py:16
  46.7 4.9 %collective-permute-start.10 = (f32[2,2,32,128]{3,2,0,1:T(8,128)S(1)}, f32[2,2,32,128]{3,2,0,1:T(8,128)S(1)}, u32[]{:S(2)}, u32[]{:S(2)}) collective-permute-start(f32[2,2,32,128]{3,2,0,1:T(8,128)S(1)} %pad_maximum_fusion.2), channel_id=1, source_target_pairs={{0,2},{1,3},{2,0},{3,1},{4,6},{5,7},{6,4},{7,5},{8,10},{9,11},{10,... | collective-permute-start | bytes 196616 | tf_op jit(solution)/shard_map/ppermute | solution.py:16
  47.4 7.5 %collective-permute-start.15 = (f32[2,2,32,128]{3,2,0,1:T(8,128)S(1)}, f32[2,2,32,128]{3,2,0,1:T(8,128)S(1)}, u32[]{:S(2)}, u32[]{:S(2)}) collective-permute-start(f32[2,2,32,128]{3,2,0,1:T(8,128)S(1)} %pad_maximum_fusion.3), channel_id=1, source_target_pairs={{0,6},{1,7},{2,4},{3,5},{4,2},{5,3},{6,0},{7,1},{8,14},{9,15},{10,... | collective-permute-start | bytes 196616 | tf_op jit(solution)/shard_map/ppermute | solution.py:16
  49.9 5.0 %collective-permute-start.16 = (f32[2,2,32,128]{3,2,0,1:T(8,128)S(1)}, f32[2,2,32,128]{3,2,0,1:T(8,128)S(1)}, u32[]{:S(2)}, u32[]{:S(2)}) collective-permute-start(f32[2,2,32,128]{3,2,0,1:T(8,128)S(1)} %pad_maximum_fusion.4), channel_id=1, source_target_pairs={{0,4},{1,5},{2,6},{3,7},{4,0},{5,1},{6,2},{7,3},{8,12},{9,13},{10,... | collective-permute-start | bytes 196616 | tf_op jit(solution)/shard_map/ppermute | solution.py:16
  50.4 4.5 %collective-permute-start.17 = (f32[2,2,32,128]{3,2,0,1:T(8,128)S(1)}, f32[2,2,32,128]{3,2,0,1:T(8,128)S(1)}, u32[]{:S(2)}, u32[]{:S(2)}) collective-permute-start(f32[2,2,32,128]{3,2,0,1:T(8,128)S(1)} %pad_maximum_fusion.5), channel_id=1, source_target_pairs={{0,2},{1,3},{2,0},{3,1},{4,6},{5,7},{6,4},{7,5},{8,10},{9,11},{10,... | collective-permute-start | bytes 196616 | tf_op jit(solution)/shard_map/ppermute | solution.py:16
  51.6 5.8 %collective-permute-start.12 = (f32[2,32,128]{2,1,0:T(8,128)S(1)}, f32[2,32,128]{2,1,0:T(8,128)S(1)}, u32[]{:S(2)}, u32[]{:S(2)}) collective-permute-start(f32[2,32,128]{2,1,0:T(8,128)S(1)} %get-tuple-element.68), channel_id=1, source_target_pairs={{0,24},{8,16},{16,8},{24,0},{1,25},{9,17},{17,9},{25,1},{2,26},{10... | collective-permute-start | bytes 98312 | tf_op jit(solution)/shard_map/ppermute | solution.py:16
  54.2 4.9 %collective-permute-start.11 = (f32[2,32,128]{2,1,0:T(8,128)S(1)}, f32[2,32,128]{2,1,0:T(8,128)S(1)}, u32[]{:S(2)}, u32[]{:S(2)}) collective-permute-start(f32[2,32,128]{2,1,0:T(8,128)S(1)} %get-tuple-element.69), channel_id=1, source_target_pairs={{0,16},{8,24},{16,0},{24,8},{1,17},{9,25},{17,1},{25,9},{2,18},{10... | collective-permute-start | bytes 98312 | tf_op jit(solution)/shard_map/ppermute | solution.py:16
  55.0 1.6 %copy-start.3 = (s32[4,2]{0,1:T(2,128)S(1)}, s32[4,2]{0,1:T(2,128)}, u32[]{:S(2)}) copy-start(s32[4,2]{0,1:T(2,128)} %param.7) | copy-start | bytes 100
  55.0 4.3 %collective-permute-start.18 = (f32[2,32,128]{2,1,0:T(8,128)S(1)}, f32[2,32,128]{2,1,0:T(8,128)S(1)}, u32[]{:S(2)}, u32[]{:S(2)}) collective-permute-start(f32[2,32,128]{2,1,0:T(8,128)S(1)} %dynamic-slice_bitcast_fusion.3), channel_id=1, source_target_pairs={{0,8},{8,0},{16,24},{24,16},{1,9},{9,1},{17,25},{25,17},{2,10},{10... | collective-permute-start | bytes 98312 | tf_op jit(solution)/shard_map/ppermute | solution.py:16

commit v9 on v8

--- a/solution.py
+++ b/solution.py
@@ -45,15 +45,6 @@
 def packed_share(planes, arrays, rest):
     share = rest // planes
     return share if rest == LANES and share * arrays <= LANES and share * planes == rest else 0
-
-
-def far_kernel(far, planes, count, *refs):
-    pieces, ends, message = refs[:count], refs[count:-1], refs[-1]
-    width = pieces[0].shape[1]
-    for index, ref in enumerate(pieces):
-        message[:, index * width : (index + 1) * width] = ref[...]
-    tile = shared_tile([end[...] for end in ends], lax.axis_index("hrow") ^ far, ends[0].shape[1] // planes)
-    message[:, count * width :] = tile.astype(message.dtype)
 
 
 def shared_tile(ends, plane, share):
@@ -295,21 +286,10 @@
     sent = list(range(planes))
     alone = []
     arrays = [expect[o] for o in range(outputs)] + [distrib[s] for s in range(shocks)]
-    if share:
-        far = sent.pop()
-        begin = (z ^ far) * width
-        message = call(
-            functools.partial(far_kernel, far, planes, some),
-            "cut_far",
-            jax.ShapeDtypeStruct((rows, some * width + rest), expect.dtype),
-            [lax.dynamic_slice_in_dim(one, begin, width, 1) for one in arrays[:some]]
-            + [one[:, grid - rest :] for one in arrays],
-        )
-        expect, distrib, message = lax.optimization_barrier((expect, distrib, message))
-        alone = [message]
-    arrays = [expect[o] for o in range(outputs)] + [distrib[s] for s in range(shocks)]
     whole = [expect.reshape(outputs * rows, grid)] + arrays[outputs:]
-    first = to_planes([*cut("cut_0", whole, sent, counts[: len(sent)], outputs), *alone], range(planes))
+    (message,) = cut("cut_far", whole, sent[-1:], counts[-1:], outputs)
+    whole, message = lax.optimization_barrier((whole, message))
+    first = to_planes([*cut("cut_0", whole, sent[:-1], counts[:-1], outputs), message], range(planes))
     if rest_group:
         later = cut("cut_1", arrays[some:], masks, [len(rest_group)] * len(masks))
         later = first[:1] + to_planes(later, masks)

time: 60.3 us -> 60.2 us (level)
    squeeze x2 -> x1, local copies, waits for them, and re-layouts: 1.34 us -> 1.26 us  [shards(): distrib[s]]
where the time goes in v9:
time: 60.2 us; the launch traced here: 60 us
  starting transfers between devices  26.9 us (45%)
  waiting for transfers between devices  26.2 us (44%)
  Pallas kernels  4.13 us (7%)
  local copies, waits for them, and re-layouts  1.69 us (3%)
  other arithmetic  0.9 us (1%)
    ppermute x19, starting transfers between devices, swap(): lax.ppermute(block, axis, [(i, i ^ mask) for i in range(lax.axis_size(axi...  26.9 us
    ppermute x19, waiting for transfers between devices, swap(): lax.ppermute(block, axis, [(i, i ^ mask) for i in range(lax.axis_size(axi...  26.2 us
    pallas_call x5, Pallas kernels, call(): pl.pallas_call(kernel, name=name, out_shape=out_shape, in_specs=[pl.Block...  4.13 us
    squeeze x1, local copies, waits for them, and re-layouts, shards(): distrib[s]  1.26 us
  transfers between devices with their start and end apart: 19, of which 8 were waited for; matrix products, arithmetic and copies ran while one was open for 1% of the time, Pallas kernels for 7%

profile of v9, /device:TPU:0, one launch (start us, length us, event | category | flops | bytes accessed | tf_op | source)
XLA Modules:
  0.0 60.0 jit_solution(2827439477083842822)
XLA Ops:
  0.0 1.3 %slice_bitcast_fusion = (bf16[64,3200]{1,0:T(8,128)(2,1)S(1)}, bf16[64,3200]{1,0:T(8,128)(2,1)S(1)}) fusion(bf16[2,64,3200]{2,1,0:T(8,128)(2,1)} %param.5), kind=kLoop, calls=%fused_computation | loop fusion | bytes 1638400 | tf_op jit(solution)/shard_map/squeeze | solution.py:288
  1.4 0.2 cut_far.1
  1.6 5.1 %collective-permute-start = (bf16[64,2432]{1,0:T(8,128)(2,1)S(1)}, bf16[64,2432]{1,0:T(8,128)(2,1)S(1)}, u32[]{:S(2)}, u32[]{:S(2)}) collective-permute-start(bf16[64,2432]{1,0:T(8,128)(2,1)S(1)} %cut_far.1), channel_id=1, source_target_pairs={{0,24},{8,16},{16,8},{24,0},{1,25},{9,17},{17,9},{25,1},{2,26},{10... | collective-permute-start | bytes 933896 | tf_op jit(solution)/shard_map/ppermute | solution.py:16
  6.7 0.5 cut_0.1
  7.3 0.6 collective-permute-start.2
  7.9 0.2 cut_1.1
  8.1 1.6 %collective-permute-start.4 = (bf16[64,768]{1,0:T(8,128)(2,1)S(1)}, bf16[64,768]{1,0:T(8,128)(2,1)S(1)}, u32[]{:S(2)}, u32[]{:S(2)}) collective-permute-start(bf16[64,768]{1,0:T(8,128)(2,1)S(1)} %get-tuple-element.36), channel_id=1, source_target_pairs={{0,8},{8,0},{16,24},{24,16},{1,9},{9,1},{17,25},{25,17},{2,10},{10... | collective-permute-start | bytes 294920 | tf_op jit(solution)/shard_map/ppermute | solution.py:16
  9.6 2.8 %collective-permute-start.5 = (bf16[64,768]{1,0:T(8,128)(2,1)S(1)}, bf16[64,768]{1,0:T(8,128)(2,1)S(1)}, u32[]{:S(2)}, u32[]{:S(2)}) collective-permute-start(bf16[64,768]{1,0:T(8,128)(2,1)S(1)} %get-tuple-element.37), channel_id=1, source_target_pairs={{0,16},{8,24},{16,0},{24,8},{1,17},{9,25},{17,1},{25,9},{2,18},{10... | collective-permute-start | bytes 294920 | tf_op jit(solution)/shard_map/ppermute | solution.py:16
  12.6 2.4 %collective-permute-done.refs_0_ = bf16[64,2432]{1,0:T(8,128)(2,1)S(1)} collective-permute-done((bf16[64,2432]{1,0:T(8,128)(2,1)S(1)}, bf16[64,2432]{1,0:T(8,128)(2,1)S(1)}, u32[]{:S(2)}, u32[]{:S(2)}) %collective-permute-start) | collective-permute-done | bytes 311328 | tf_op jit(solution)/shard_map/ppermute | solution.py:16
  15.0 3.8 %collective-permute-start.6 = (bf16[64,768]{1,0:T(8,128)(2,1)S(1)}, bf16[64,768]{1,0:T(8,128)(2,1)S(1)}, u32[]{:S(2)}, u32[]{:S(2)}) collective-permute-start(bf16[64,768]{1,0:T(8,128)(2,1)S(1)} %get-tuple-element.38), channel_id=1, source_target_pairs={{0,24},{8,16},{16,8},{24,0},{1,25},{9,17},{17,9},{25,1},{2,26},{10... | collective-permute-start | bytes 294920 | tf_op jit(solution)/shard_map/ppermute | solution.py:16
  18.9 19.6 %collective-permute-done.1.refs_1_ = bf16[64,2432]{1,0:T(8,128)(2,1)S(1)} collective-permute-done((bf16[64,2432]{1,0:T(8,128)(2,1)S(1)}, bf16[64,2432]{1,0:T(8,128)(2,1)S(1)}, u32[]{:S(2)}, u32[]{:S(2)}) %collective-permute-start.1) | collective-permute-done | bytes 311328 | tf_op jit(solution)/shard_map/ppermute | solution.py:16
  38.4 1.7 %partial_0.1 = (bf16[2,256,896]{2,1,0:T(8,128)(2,1)S(1)}, bf16[2,256,128]{2,1,0:T(8,128)(2,1)S(1)}, f32[4,2,1,32,128]{4,3,2,1,0:T(8,128)S(1)}, f32[4,2,1,32,128]...) custom-call(f32[4,32,1]{2,1,0:T(8,128)S(1)} %copy.5.direct_ref, ...), custom_call_target="tpu_custom_call" | custom-call | flops 234881024 | bytes 2981888 | tf_op jit(solution)/shard_map/partial_0/pallas_call | solution.py:208
  40.2 0.3 collective-permute-done.5.refs_2_
  40.5 1.6 %partial_1.1 = (f32[4,2,1,32,128]{4,3,2,1,0:T(8,128)S(1)}, f32[4,2,1,32,128]{4,3,2,1,0:T(8,128)S(1)}, f32[4,2,1,32,128]{4,3,2,1,0:T(8,128)S(1)}, f32[4,2,1,32,128]{4,3,2,1,0:T(8,128)S(1)}) custom-call(f32[4,32,1]{2,1,0:T(8,128)S(1)} %copy.5.direct_ref, bf16[2,256,896]{2,1,0:T(8,128)(2,1)S(1)} %get-tuple-element.34.expect_ref, ...), custom_call_target="tpu_custom_call" | custom-call | flops 234881024 | bytes 2342912 | tf_op jit(solution)/shard_map/partial_1/pallas_call | solution.py:208
  42.1 0.3 collective-permute-start.7
  42.3 0.3 collective-permute-start.14
  42.7 0.2 collective-permute-start.13
  42.9 0.6 collective-permute-done.7
  43.6 2.5 %collective-permute-start.8 = (f32[2,2,32,128]{3,2,0,1:T(8,128)S(1)}, f32[2,2,32,128]{3,2,0,1:T(8,128)S(1)}, u32[]{:S(2)}, u32[]{:S(2)}) collective-permute-start(f32[2,2,32,128]{3,2,0,1:T(8,128)S(1)} %pad_maximum_fusion), channel_id=1, source_target_pairs={{0,6},{1,7},{2,4},{3,5},{4,2},{5,3},{6,0},{7,1},{8,14},{9,15},{10,... | collective-permute-start | bytes 196616 | tf_op jit(solution)/shard_map/ppermute | solution.py:16
  46.1 0.5 collective-permute-start.9
  46.6 0.5 collective-permute-start.10
  47.3 2.5 %collective-permute-start.15 = (f32[2,2,32,128]{3,2,0,1:T(8,128)S(1)}, f32[2,2,32,128]{3,2,0,1:T(8,128)S(1)}, u32[]{:S(2)}, u32[]{:S(2)}) collective-permute-start(f32[2,2,32,128]{3,2,0,1:T(8,128)S(1)} %pad_maximum_fusion.3), channel_id=1, source_target_pairs={{0,6},{1,7},{2,4},{3,5},{4,2},{5,3},{6,0},{7,1},{8,14},{9,15},{10,... | collective-permute-start | bytes 196616 | tf_op jit(solution)/shard_map/ppermute | solution.py:16
  49.8 0.5 collective-permute-start.16
  50.3 0.6 %collective-permute-start.17 = (f32[2,2,32,128]{3,2,0,1:T(8,128)S(1)}, f32[2,2,32,128]{3,2,0,1:T(8,128)S(1)}, u32[]{:S(2)}, u32[]{:S(2)}) collective-permute-start(f32[2,2,32,128]{3,2,0,1:T(8,128)S(1)} %pad_maximum_fusion.5), channel_id=1, source_target_pairs={{0,2},{1,3},{2,0},{3,1},{4,6},{5,7},{6,4},{7,5},{8,10},{9,11},{10,... | collective-permute-start | bytes 196616 | tf_op jit(solution)/shard_map/ppermute | solution.py:16
  50.9 0.6 collective-permute-done.10
  51.5 2.5 %collective-permute-start.12 = (f32[2,32,128]{2,1,0:T(8,128)S(1)}, f32[2,32,128]{2,1,0:T(8,128)S(1)}, u32[]{:S(2)}, u32[]{:S(2)}) collective-permute-start(f32[2,32,128]{2,1,0:T(8,128)S(1)} %get-tuple-element.63), channel_id=1, source_target_pairs={{0,24},{8,16},{16,8},{24,0},{1,25},{9,17},{17,9},{25,1},{2,26},{10... | collective-permute-start | bytes 98312 | tf_op jit(solution)/shard_map/ppermute | solution.py:16
  54.1 0.8 %collective-permute-start.11 = (f32[2,32,128]{2,1,0:T(8,128)S(1)}, f32[2,32,128]{2,1,0:T(8,128)S(1)}, u32[]{:S(2)}, u32[]{:S(2)}) collective-permute-start(f32[2,32,128]{2,1,0:T(8,128)S(1)} %get-tuple-element.64), channel_id=1, source_target_pairs={{0,16},{8,24},{16,0},{24,8},{1,17},{9,25},{17,1},{25,9},{2,18},{10... | collective-permute-start | bytes 98312 | tf_op jit(solution)/shard_map/ppermute | solution.py:16
  54.9 1.6 %collective-permute-start.18 = (f32[2,32,128]{2,1,0:T(8,128)S(1)}, f32[2,32,128]{2,1,0:T(8,128)S(1)}, u32[]{:S(2)}, u32[]{:S(2)}) collective-permute-start(f32[2,32,128]{2,1,0:T(8,128)S(1)} %dynamic-slice_bitcast_fusion), channel_id=1, source_target_pairs={{0,8},{8,0},{16,24},{24,16},{1,9},{9,1},{17,25},{25,17},{2,10},{10... | collective-permute-start | bytes 98312 | tf_op jit(solution)/shard_map/ppermute | solution.py:16
  56.5 0.8 %collective-permute-done.12 = f32[2,32,128]{2,1,0:T(8,128)S(1)} collective-permute-done((f32[2,32,128]{2,1,0:T(8,128)S(1)}, f32[2,32,128]{2,1,0:T(8,128)S(1)}, u32[]{:S(2)}, u32[]{:S(2)}) %collective-permute-start.12) | collective-permute-done | bytes 32800 | tf_op jit(solution)/shard_map/ppermute | solution.py:16
  57.3 1.7 %collective-permute-done.11 = f32[2,32,128]{2,1,0:T(8,128)S(1)} collective-permute-done((f32[2,32,128]{2,1,0:T(8,128)S(1)}, f32[2,32,128]{2,1,0:T(8,128)S(1)}, u32[]{:S(2)}, u32[]{:S(2)}) %collective-permute-start.11) | collective-permute-done | bytes 32800 | tf_op jit(solution)/shard_map/ppermute | solution.py:16
  59.0 0.2 collective-permute-done.18
  59.3 0.7 %select_select_fusion = f32[4,64,32]{1,2,0:T(8,128)} fusion(f32[64,32]{0,1:T(8,128)S(1)} %get-tuple-element.66, f32[64,32]{0,1:T(8,128)S(1)} %get-tuple-element.67, f32[64,32]{0,1:T(8,128)S(1)} %get-tuple-element.68, f32[64,32]{0,1:T(8,128)S(1)} %get-tuple-element.65, pred[4]{0:T(512)(128)(4,1)S(1)} %get-tuple-element.70, ...), kind=kLoop, calls=%fused_computation.14 | loop fusion | flops 32768 | bytes 65552 | tf_op jit(solution)/shard_map/jit(_where)/select_n | solution.py:333
  (42 shorter events, 0.8 us)
Async XLA Ops:
  0.0 1.4 %copy-start = (bf16[2,64,3200]{2,1,0:T(8,128)(2,1)S(1)}, bf16[2,64,3200]{2,1,0:T(8,128)(2,1)}, u32[]{:S(2)}) copy-start(bf16[2,64,3200]{2,1,0:T(8,128)(2,1)} %param.4) | copy-start | bytes 2457604
  1.6 13.4 %collective-permute-start = (bf16[64,2432]{1,0:T(8,128)(2,1)S(1)}, bf16[64,2432]{1,0:T(8,128)(2,1)S(1)}, u32[]{:S(2)}, u32[]{:S(2)}) collective-permute-start(bf16[64,2432]{1,0:T(8,128)(2,1)S(1)} %cut_far.1), channel_id=1, source_target_pairs={{0,24},{8,16},{16,8},{24,0},{1,25},{9,17},{17,9},{25,1},{2,26},{10... | collective-permute-start | bytes 933896 | tf_op jit(solution)/shard_map/ppermute | solution.py:16
  7.2 31.2 %collective-permute-start.1 = (bf16[64,2432]{1,0:T(8,128)(2,1)S(1)}, bf16[64,2432]{1,0:T(8,128)(2,1)S(1)}, u32[]{:S(2)}, u32[]{:S(2)}) collective-permute-start(bf16[64,2432]{1,0:T(8,128)(2,1)S(1)} %get-tuple-element.29), channel_id=1, source_target_pairs={{0,16},{8,24},{16,0},{24,8},{1,17},{9,25},{17,1},{25,9},{2,18},{10... | collective-permute-start | bytes 933896 | tf_op jit(solution)/shard_map/ppermute | solution.py:16
  7.3 31.1 %collective-permute-start.2 = (bf16[64,2432]{1,0:T(8,128)(2,1)S(1)}, bf16[64,2432]{1,0:T(8,128)(2,1)S(1)}, u32[]{:S(2)}, u32[]{:S(2)}) collective-permute-start(bf16[64,2432]{1,0:T(8,128)(2,1)S(1)} %get-tuple-element.30), channel_id=1, source_target_pairs={{0,8},{8,0},{16,24},{24,16},{1,9},{9,1},{17,25},{25,17},{2,10},{10... | collective-permute-start | bytes 933896 | tf_op jit(solution)/shard_map/ppermute | solution.py:16
  8.1 4.4 %copy-start.1 = (f32[2,2,32]{2,1,0:T(2,128)S(1)}, f32[2,2,32]{2,1,0:T(2,128)}, u32[]{:S(2)}) copy-start(f32[2,2,32]{2,1,0:T(2,128)} %param.6) | copy-start | bytes 1540
  8.1 32.1 %collective-permute-start.4 = (bf16[64,768]{1,0:T(8,128)(2,1)S(1)}, bf16[64,768]{1,0:T(8,128)(2,1)S(1)}, u32[]{:S(2)}, u32[]{:S(2)}) collective-permute-start(bf16[64,768]{1,0:T(8,128)(2,1)S(1)} %get-tuple-element.36), channel_id=1, source_target_pairs={{0,8},{8,0},{16,24},{24,16},{1,9},{9,1},{17,25},{25,17},{2,10},{10... | collective-permute-start | bytes 294920 | tf_op jit(solution)/shard_map/ppermute | solution.py:16
  9.6 30.9 %collective-permute-start.5 = (bf16[64,768]{1,0:T(8,128)(2,1)S(1)}, bf16[64,768]{1,0:T(8,128)(2,1)S(1)}, u32[]{:S(2)}, u32[]{:S(2)}) collective-permute-start(bf16[64,768]{1,0:T(8,128)(2,1)S(1)} %get-tuple-element.37), channel_id=1, source_target_pairs={{0,16},{8,24},{16,0},{24,8},{1,17},{9,25},{17,1},{25,9},{2,18},{10... | collective-permute-start | bytes 294920 | tf_op jit(solution)/shard_map/ppermute | solution.py:16
  15.0 25.5 %collective-permute-start.6 = (bf16[64,768]{1,0:T(8,128)(2,1)S(1)}, bf16[64,768]{1,0:T(8,128)(2,1)S(1)}, u32[]{:S(2)}, u32[]{:S(2)}) collective-permute-start(bf16[64,768]{1,0:T(8,128)(2,1)S(1)} %get-tuple-element.38), channel_id=1, source_target_pairs={{0,24},{8,16},{16,8},{24,0},{1,25},{9,17},{17,9},{25,1},{2,26},{10... | collective-permute-start | bytes 294920 | tf_op jit(solution)/shard_map/ppermute | solution.py:16
  40.1 2.7 %collective-permute-start.3 = (f32[4,2,1,32,128]{4,3,2,1,0:T(8,128)S(1)}, f32[4,2,1,32,128]{4,3,2,1,0:T(8,128)S(1)}, u32[]{:S(2)}, u32[]{:S(2)}) collective-permute-start(f32[4,2,1,32,128]{4,3,2,1,0:T(8,128)S(1)} %get-tuple-element.33), channel_id=1, source_target_pairs={{0,1},{1,0},{2,3},{3,2},{4,5},{5,4},{6,7},{7,6},{8,9},{9,8},{10,11... | collective-permute-start | bytes 393224 | tf_op jit(solution)/shard_map/ppermute | solution.py:16
  42.1 1.4 %collective-permute-start.7 = (f32[4,2,1,32,128]{4,3,2,1,0:T(8,128)S(1)}, f32[4,2,1,32,128]{4,3,2,1,0:T(8,128)S(1)}, u32[]{:S(2)}, u32[]{:S(2)}) collective-permute-start(f32[4,2,1,32,128]{4,3,2,1,0:T(8,128)S(1)} %get-tuple-element.40), channel_id=1, source_target_pairs={{0,1},{1,0},{2,3},{3,2},{4,5},{5,4},{6,7},{7,6},{8,9},{9,8},{10,11... | collective-permute-start | bytes 393224 | tf_op jit(solution)/shard_map/ppermute | solution.py:16
  42.3 4.8 %collective-permute-start.14 = (f32[4,2,1,32,128]{4,3,2,1,0:T(8,128)S(1)}, f32[4,2,1,32,128]{4,3,2,1,0:T(8,128)S(1)}, u32[]{:S(2)}, u32[]{:S(2)}) collective-permute-start(f32[4,2,1,32,128]{4,3,2,1,0:T(8,128)S(1)} %get-tuple-element.44), channel_id=1, source_target_pairs={{0,1},{1,0},{2,3},{3,2},{4,5},{5,4},{6,7},{7,6},{8,9},{9,8},{10,11... | collective-permute-start | bytes 393224 | tf_op jit(solution)/shard_map/ppermute | solution.py:16
  42.7 4.5 %collective-permute-start.13 = (f32[4,2,1,32,128]{4,3,2,1,0:T(8,128)S(1)}, f32[4,2,1,32,128]{4,3,2,1,0:T(8,128)S(1)}, u32[]{:S(2)}, u32[]{:S(2)}) collective-permute-start(f32[4,2,1,32,128]{4,3,2,1,0:T(8,128)S(1)} %get-tuple-element.42), channel_id=1, source_target_pairs={{0,1},{1,0},{2,3},{3,2},{4,5},{5,4},{6,7},{7,6},{8,9},{9,8},{10,11... | collective-permute-start | bytes 393224 | tf_op jit(solution)/shard_map/ppermute | solution.py:16
  43.6 6.7 %collective-permute-start.8 = (f32[2,2,32,128]{3,2,0,1:T(8,128)S(1)}, f32[2,2,32,128]{3,2,0,1:T(8,128)S(1)}, u32[]{:S(2)}, u32[]{:S(2)}) collective-permute-start(f32[2,2,32,128]{3,2,0,1:T(8,128)S(1)} %pad_maximum_fusion), channel_id=1, source_target_pairs={{0,6},{1,7},{2,4},{3,5},{4,2},{5,3},{6,0},{7,1},{8,14},{9,15},{10,... | collective-permute-start | bytes 196616 | tf_op jit(solution)/shard_map/ppermute | solution.py:16
  46.1 4.8 %collective-permute-start.9 = (f32[2,2,32,128]{3,2,0,1:T(8,128)S(1)}, f32[2,2,32,128]{3,2,0,1:T(8,128)S(1)}, u32[]{:S(2)}, u32[]{:S(2)}) collective-permute-start(f32[2,2,32,128]{3,2,0,1:T(8,128)S(1)} %pad_maximum_fusion.1), channel_id=1, source_target_pairs={{0,4},{1,5},{2,6},{3,7},{4,0},{5,1},{6,2},{7,3},{8,12},{9,13},{10,... | collective-permute-start | bytes 196616 | tf_op jit(solution)/shard_map/ppermute | solution.py:16
  46.6 4.9 %collective-permute-start.10 = (f32[2,2,32,128]{3,2,0,1:T(8,128)S(1)}, f32[2,2,32,128]{3,2,0,1:T(8,128)S(1)}, u32[]{:S(2)}, u32[]{:S(2)}) collective-permute-start(f32[2,2,32,128]{3,2,0,1:T(8,128)S(1)} %pad_maximum_fusion.2), channel_id=1, source_target_pairs={{0,2},{1,3},{2,0},{3,1},{4,6},{5,7},{6,4},{7,5},{8,10},{9,11},{10,... | collective-permute-start | bytes 196616 | tf_op jit(solution)/shard_map/ppermute | solution.py:16
  47.3 7.5 %collective-permute-start.15 = (f32[2,2,32,128]{3,2,0,1:T(8,128)S(1)}, f32[2,2,32,128]{3,2,0,1:T(8,128)S(1)}, u32[]{:S(2)}, u32[]{:S(2)}) collective-permute-start(f32[2,2,32,128]{3,2,0,1:T(8,128)S(1)} %pad_maximum_fusion.3), channel_id=1, source_target_pairs={{0,6},{1,7},{2,4},{3,5},{4,2},{5,3},{6,0},{7,1},{8,14},{9,15},{10,... | collective-permute-start | bytes 196616 | tf_op jit(solution)/shard_map/ppermute | solution.py:16
  49.8 5.0 %collective-permute-start.16 = (f32[2,2,32,128]{3,2,0,1:T(8,128)S(1)}, f32[2,2,32,128]{3,2,0,1:T(8,128)S(1)}, u32[]{:S(2)}, u32[]{:S(2)}) collective-permute-start(f32[2,2,32,128]{3,2,0,1:T(8,128)S(1)} %pad_maximum_fusion.4), channel_id=1, source_target_pairs={{0,4},{1,5},{2,6},{3,7},{4,0},{5,1},{6,2},{7,3},{8,12},{9,13},{10,... | collective-permute-start | bytes 196616 | tf_op jit(solution)/shard_map/ppermute | solution.py:16
  50.3 4.5 %collective-permute-start.17 = (f32[2,2,32,128]{3,2,0,1:T(8,128)S(1)}, f32[2,2,32,128]{3,2,0,1:T(8,128)S(1)}, u32[]{:S(2)}, u32[]{:S(2)}) collective-permute-start(f32[2,2,32,128]{3,2,0,1:T(8,128)S(1)} %pad_maximum_fusion.5), channel_id=1, source_target_pairs={{0,2},{1,3},{2,0},{3,1},{4,6},{5,7},{6,4},{7,5},{8,10},{9,11},{10,... | collective-permute-start | bytes 196616 | tf_op jit(solution)/shard_map/ppermute | solution.py:16
  51.5 5.8 %collective-permute-start.12 = (f32[2,32,128]{2,1,0:T(8,128)S(1)}, f32[2,32,128]{2,1,0:T(8,128)S(1)}, u32[]{:S(2)}, u32[]{:S(2)}) collective-permute-start(f32[2,32,128]{2,1,0:T(8,128)S(1)} %get-tuple-element.63), channel_id=1, source_target_pairs={{0,24},{8,16},{16,8},{24,0},{1,25},{9,17},{17,9},{25,1},{2,26},{10... | collective-permute-start | bytes 98312 | tf_op jit(solution)/shard_map/ppermute | solution.py:16
  54.1 4.9 %collective-permute-start.11 = (f32[2,32,128]{2,1,0:T(8,128)S(1)}, f32[2,32,128]{2,1,0:T(8,128)S(1)}, u32[]{:S(2)}, u32[]{:S(2)}) collective-permute-start(f32[2,32,128]{2,1,0:T(8,128)S(1)} %get-tuple-element.64), channel_id=1, source_target_pairs={{0,16},{8,24},{16,0},{24,8},{1,17},{9,25},{17,1},{25,9},{2,18},{10... | collective-permute-start | bytes 98312 | tf_op jit(solution)/shard_map/ppermute | solution.py:16
  54.8 1.6 %copy-start.2 = (s32[4,2]{0,1:T(2,128)S(1)}, s32[4,2]{0,1:T(2,128)}, u32[]{:S(2)}) copy-start(s32[4,2]{0,1:T(2,128)} %param.7) | copy-start | bytes 100
  54.9 4.3 %collective-permute-start.18 = (f32[2,32,128]{2,1,0:T(8,128)S(1)}, f32[2,32,128]{2,1,0:T(8,128)S(1)}, u32[]{:S(2)}, u32[]{:S(2)}) collective-permute-start(f32[2,32,128]{2,1,0:T(8,128)S(1)} %dynamic-slice_bitcast_fusion), channel_id=1, source_target_pairs={{0,8},{8,0},{16,24},{24,16},{1,9},{9,1},{17,25},{25,17},{2,10},{10... | collective-permute-start | bytes 98312 | tf_op jit(solution)/shard_map/ppermute | solution.py:16
